TPU v7x, 32 devices: a whole 2x2x4 slice. The times are simulated.
32 devices in a mesh: groups: 2 (over x), dom: 8 (over z, y), sub: 2 (over core).
Axes of the slice: x: 2, y: 2, z: 4, core: 2. Of those that a mesh axis runs over, the one named last changes fastest.
Arguments:
- node_latent: bfloat16 [98304, 128], P(('groups', 'dom', 'sub')), parts along dimension 0, may hold values from -6 to 6
- edge_latent: bfloat16 [589824, 128], P(('groups', 'dom', 'sub')), parts along dimension 0, may hold values from -6 to 6
- receivers: int32 [589824], P(('groups', 'dom', 'sub')), parts along dimension 0, may hold values from 0 to 49151, as said below
- senders: int32 [589824], P(('groups', 'dom', 'sub')), parts along dimension 0, may hold values from 0 to 49151, as said below
- coarse_map: int32 [98304], P(('groups', 'dom', 'sub')), parts along dimension 0, may hold values from 0 to 6143, as said below
- coarse_recv: int32 [73728], P(('groups', 'dom', 'sub')), parts along dimension 0, may hold values from 0 to 6143, as said below
- coarse_send: int32 [73728], P(('groups', 'dom', 'sub')), parts along dimension 0, may hold values from 0 to 6143, as said below
- edge_w1: bfloat16 [384, 128], replicated, may hold values from -0.3125 to 0.3125
- mod_u: bfloat16 [384, 32], replicated, may hold values from -0.3125 to 0.3125
- mod_v: bfloat16 [32, 128], replicated, may hold values from -1 to 1
- edge_w2: bfloat16 [128, 128], replicated, may hold values from -0.5 to 0.5
- edge_gain: float32 [128], replicated, may hold values from 0.5 to 1.5
- node_w1: bfloat16 [256, 128], replicated, may hold values from -0.375 to 0.375
- node_w2: bfloat16 [128, 128], replicated, may hold values from -0.5 to 0.5
- node_gain: float32 [128], replicated, may hold values from 0.5 to 1.5
- coarse_w1: bfloat16 [256, 128], replicated, may hold values from -0.375 to 0.375
- coarse_w2: bfloat16 [128, 128], replicated, may hold values from -0.5 to 0.5
- coarse_gain: float32 [128], replicated, may hold values from 0.5 to 1.5
Outputs:
- node_out: bfloat16 [98304, 128], P(('groups', 'dom', 'sub')), parts along dimension 0
- edge_out: bfloat16 [589824, 128], P(('groups', 'dom', 'sub')), parts along dimension 0
There are 2 independent parts, one for each index of `groups`. A program takes and returns all parts, laid end to end along the dimension named above; an argument that names none is the same for every part. Nothing has to cross between parts.
Inputs may be any that keep to these rules, and one draw needn't show every extreme that they name: `receivers`: the edges form aligned blocks of 768; every edge of the k-th block has its receiver among nodes k * 128 to (k + 1) * 128 - 1. `senders`: each edge's sender differs from its receiver by at most 256. coarse_map[n] // 384 equals n // 3072. coarse_recv[k] // 384 equals k // 2304. With b = k // 2304, coarse_send[k] // 384 equals b or differs from b in exactly one bit.
All inputs are finite; a program needn't handle non-finite values.
Results may differ from a plain program's by a relative error of at most 0.0061.
Values may be sent and summed in bfloat16 or wider, within the bound.
No kernel may reach another device: no remote copies, remote signals or barrier semaphores. Data moves between devices by JAX's collectives and lax.ppermute only.
A program may use at most 128 MiB of HBM per device.

v0:
```python
import jax
import jax.numpy as jnp
from jax import lax
from jax.sharding import PartitionSpec as P

TILE = 128
HALO = 256
COARSEN = 8


def padded(shard, sides, width):
    for axis, dim in sides:
        size, length = (lax.axis_size(axis), shard.shape[dim])
        up = [(i, (i + 1) % size) for i in range(size - 1)]
        down = [(j, i) for i, j in up]
        last = lax.slice_in_dim(shard, length - width, length, axis=dim)
        first = lax.slice_in_dim(shard, 0, width, axis=dim)
        before = lax.ppermute(last, axis, up)
        after = lax.ppermute(first, axis, down)
        shard = jnp.concatenate([before, shard, after], axis=dim)
    return shard


def layer_norm(values, gain_vec):
    average = jnp.mean(values, axis=-1, keepdims=True)
    centred = values - average
    spread = jnp.mean(centred * centred, axis=-1, keepdims=True)
    return centred * lax.rsqrt(spread + 1e-05) * gain_vec


def on_device(
    node_latent,
    edge_latent,
    receivers,
    senders,
    coarse_map,
    coarse_recv,
    coarse_send,
    edge_w1,
    mod_u,
    mod_v,
    edge_w2,
    edge_gain,
    node_w1,
    node_w2,
    node_gain,
    coarse_w1,
    coarse_w2,
    coarse_gain,
):
    dev_index = lax.axis_index(("dom", "sub"))
    node_rows = node_latent.shape[0]
    width = node_latent.shape[1]
    coarse_rows = node_rows // COARSEN
    tiles = node_rows // TILE
    window = TILE + 2 * HALO
    extended = padded(node_latent, ((("dom", "sub"), 0),), HALO)
    local_recv = receivers - dev_index * node_rows
    tile_starts = jnp.arange(tiles, dtype=jnp.int32) * TILE
    tile_recv = local_recv.reshape(tiles, -1) - tile_starts[:, None]
    tile_send = (senders - dev_index * node_rows + HALO).reshape(tiles, -1) - tile_starts[:, None]

    def pick_rows(operands):
        start, send_off, recv_off = operands
        beside_all = lax.dynamic_slice_in_dim(extended, start, window, 0)
        own = lax.dynamic_slice_in_dim(node_latent, start, TILE, 0)
        send_hot = (send_off[:, None] == jnp.arange(window, dtype=jnp.int32)[None, :]).astype(
            jnp.bfloat16
        )
        recv_hot = (recv_off[:, None] == jnp.arange(TILE, dtype=jnp.int32)[None, :]).astype(
            jnp.bfloat16
        )
        sent_part = jnp.dot(send_hot, beside_all, preferred_element_type=jnp.float32).astype(
            jnp.bfloat16
        )
        recv_part = jnp.dot(recv_hot, own, preferred_element_type=jnp.float32).astype(jnp.bfloat16)
        return (sent_part, recv_part)

    sent_rows, recv_rows = lax.map(pick_rows, (tile_starts, tile_send, tile_recv))
    sent_rows = sent_rows.reshape(-1, width)
    recv_rows = recv_rows.reshape(-1, width)
    edge_in = jnp.concatenate([edge_latent, sent_rows, recv_rows], axis=1)
    low_rank = jnp.dot(edge_in, mod_u, preferred_element_type=jnp.float32).astype(jnp.bfloat16)
    preact = jnp.dot(edge_in, edge_w1, preferred_element_type=jnp.float32) + jnp.dot(
        low_rank, mod_v, preferred_element_type=jnp.float32
    )
    edge_hidden = jax.nn.silu(preact).astype(jnp.bfloat16)
    update = jnp.dot(edge_hidden, edge_w2, preferred_element_type=jnp.float32)
    edge_out = (edge_latent.astype(jnp.float32) + layer_norm(update, edge_gain)).astype(
        jnp.bfloat16
    )
    one_hot = (tile_recv[:, None, :] == jnp.arange(TILE, dtype=jnp.int32)[None, :, None]).astype(
        jnp.bfloat16
    )
    incoming = jnp.einsum(
        "tne,tel->tnl",
        one_hot,
        edge_out.reshape(tiles, -1, width),
        preferred_element_type=jnp.float32,
    )
    incoming = incoming.reshape(node_rows, width).astype(jnp.bfloat16)
    node_in = jnp.concatenate([node_latent, incoming], axis=1)
    node_hidden = jax.nn.silu(jnp.dot(node_in, node_w1, preferred_element_type=jnp.float32)).astype(
        jnp.bfloat16
    )
    node_update = jnp.dot(node_hidden, node_w2, preferred_element_type=jnp.float32)
    fine_new = (node_latent.astype(jnp.float32) + layer_norm(node_update, node_gain)).astype(
        jnp.bfloat16
    )
    local_coarse = coarse_map - dev_index * coarse_rows
    member = (jnp.arange(coarse_rows, dtype=jnp.int32)[:, None] == local_coarse[None, :]).astype(
        jnp.bfloat16
    )
    coarse_sum = jnp.dot(member, fine_new, preferred_element_type=jnp.float32)
    counts = jnp.sum(member.astype(jnp.float32), axis=1)
    coarse_latent = (coarse_sum / jnp.maximum(counts, 1.0)[:, None]).astype(jnp.bfloat16)
    everything = lax.all_gather(coarse_latent, ("dom", "sub"), axis=0, tiled=True)
    send_rows = jnp.take(everything, coarse_send, axis=0)
    local_crecv = coarse_recv - dev_index * coarse_rows
    coarse_hot = (jnp.arange(coarse_rows, dtype=jnp.int32)[:, None] == local_crecv[None, :]).astype(
        jnp.bfloat16
    )
    crecv_rows = jnp.dot(coarse_hot.T, coarse_latent, preferred_element_type=jnp.float32).astype(
        jnp.bfloat16
    )
    coarse_in_rows = jnp.concatenate([send_rows, crecv_rows], axis=1)
    coarse_hidden = jax.nn.silu(
        jnp.dot(coarse_in_rows, coarse_w1, preferred_element_type=jnp.float32)
    ).astype(jnp.bfloat16)
    coarse_msg = jnp.dot(coarse_hidden, coarse_w2, preferred_element_type=jnp.float32).astype(
        jnp.bfloat16
    )
    coarse_in = jnp.dot(coarse_hot, coarse_msg, preferred_element_type=jnp.float32)
    coarse_delta = layer_norm(coarse_latent.astype(jnp.float32) + coarse_in, coarse_gain).astype(
        jnp.bfloat16
    )
    spread_back = jnp.dot(member.T, coarse_delta, preferred_element_type=jnp.float32)
    node_out = (fine_new.astype(jnp.float32) + spread_back).astype(jnp.bfloat16)
    return (node_out, edge_out)


def solution(mesh):
    placed = (
        P(("groups", "dom", "sub"), None),
        P(("groups", "dom", "sub"), None),
        P(("groups", "dom", "sub")),
        P(("groups", "dom", "sub")),
        P(("groups", "dom", "sub")),
        P(("groups", "dom", "sub")),
        P(("groups", "dom", "sub")),
        P(),
        P(),
        P(),
        P(),
        P(),
        P(),
        P(),
        P(),
        P(),
        P(),
        P(),
    )
    return jax.shard_map(
        on_device,
        mesh=mesh,
        in_specs=placed,
        out_specs=(P(("groups", "dom", "sub"), None), P(("groups", "dom", "sub"), None)),
        check_vma=False,
    )
```

profile of v0, /device:TPU:0, one launch (start us, length us, event | category | flops | bytes accessed | tf_op | source)
XLA Modules:
  0.0 295.6 jit_solution(14921041900104339032)
XLA Ops:
  8.1 2.4 collective-permute-start
  17.0 163.1 %while.12 = (s32[]{:T(128)}, bf16[24,768,128]{2,1,0:T(8,128)(2,1)}, bf16[24,768,128]{2,1,0:T(8,128)(2,1)}, s32[24,768]{1,0:T(8,128)S(1)}, s32[24]{0:T(128)S(1)},...) while((s32[]{:T(128)}, bf16[24,768,128]{2,1,0:T(8,128)(2,1)}, ...), condition=%wide.region_1.2_spmd, body=%wide.region_0.1_spmd.sunk | while | flops 151781376 | bytes 610504 | solution.py:79
  19.6 1.7 fusion.83
  26.4 1.7 fusion.83
  39.9 1.8 fusion.83
  46.7 1.7 fusion.83
  53.5 1.7 fusion.83
  60.3 1.7 fusion.83
  67.1 1.8 fusion.83
  74.0 1.7 fusion.83
  80.8 1.8 fusion.83
  94.4 1.7 fusion.83
  101.1 1.8 fusion.83
  108.0 1.7 fusion.83
  114.8 1.7 fusion.83
  121.5 1.7 fusion.83
  135.1 1.7 fusion.83
  141.9 1.7 fusion.83
  148.7 1.7 fusion.83
  155.5 1.8 fusion.83
  162.3 1.7 fusion.83
  180.1 9.3 %fusion.13 = f32[18432,128]{1,0:T(8,128)} fusion(bf16[384,128]{1,0:T(8,128)(2,1)S(1)} %copy-done, bf16[18432,128]{1,0:T(8,128)(2,1)} %bitcast.35, bf16[18432,128]{1,0:T(8,128)(2,1)} %bitcast.33, bf16[18432,128]{1,0:T(8,128)(2,1)} %param.21), kind=kOutput, calls=%fused_computation.26 | convolution fusion | flops 1854406656 | bytes 23691264 | tf_op jit(solution)/shard_map/dot_general | solution.py:84
  189.4 14.0 %multiply_convert_fusion = bf16[18432,128]{1,0:T(8,128)(2,1)} fusion(f32[18432,128]{1,0:T(8,128)} %fusion.13, bf16[32,128]{1,0:T(8,128)(2,1)S(1)} %copy-done.14, bf16[384,32]{0,1:T(8,128)(2,1)S(1)} %copy-done.13, bf16[18432,128]{1,0:T(8,128)(2,1)} %bitcast.36, bf16[18432,128]{1,0:T(8,128)(2,1)} %bitcast.34, bf16[18432,128]{1,0:T(8,128)(2,1)} %param.21), kind=kOutput, calls=%fused_computation.23 | convolution fusion | flops 661192704 | bytes 28344320 | tf_op jit(solution)/shard_map/dot_general | solution.py:84
  203.4 4.6 %fusion.58 = (f32[18432]{0:T(1024)S(1)}, f32[18432,128]{1,0:T(8,128)S(1)}) fusion(bf16[18432,128]{1,0:T(8,128)(2,1)} %multiply_convert_fusion, bf16[128,128]{1,0:T(8,128)(2,1)S(1)} %copy-done.5), kind=kOutput, calls=%fused_computation.92 | convolution fusion | flops 606320640 | bytes 14262272 | tf_op jit(solution)/shard_map/dot_general | solution.py:88
  208.1 5.5 %multiply_reduce_fusion = f32[18432]{0:T(1024)S(1)} fusion(f32[18432,128]{1,0:T(8,128)S(1)} %get-tuple-element.74, f32[18432]{0:T(1024)S(1)} %broadcast_multiply_fusion), kind=kLoop, calls=%fused_computation.22 | loop fusion | flops 7059456 | bytes 9584640 | tf_op jit(solution)/shard_map/reduce_sum | solution.py:27
  213.6 11.3 %add_convert_fusion = bf16[18432,128]{1,0:T(8,128)(2,1)S(1)} fusion(bf16[18432,128]{1,0:T(8,128)(2,1)} %param.21, f32[18432,128]{1,0:T(8,128)S(1)} %get-tuple-element.74, f32[128]{0:T(128)S(1)} %copy-done.7, f32[18432]{0:T(1024)S(1)} %add_rsqrt_fusion, f32[18432]{0:T(1024)S(1)} %broadcast_multiply_fusion), kind=kLoop, calls=%fused_computation.21 | loop fusion | flops 14155776 | bytes 19022336 | tf_op jit(solution)/shard_map/convert_element_type | solution.py:89
  224.9 2.8 fusion.36
  227.7 2.2 fusion.59
  232.3 2.4 convolution_convert_fusion.3
  234.7 41.1 %all-gather.2.cloned.1.call-done = bf16[6144,128]{0,1:T(8,128)(2,1)} async-done(((bf16[384,128]{0,1:T(8,128)(2,1)}), bf16[6144,128]{0,1:T(8,128)(2,1)}) %all-gather.2.cloned.1.call-update) | async-done | bytes 1572880 | tf_op jit(solution)/shard_map/all_gather | solution.py:117
  275.8 1.9 copy.25
  277.8 4.7 %gather_fusion = bf16[2304,128]{1,0:T(8,128)(2,1)S(1)} fusion(bf16[6144,128]{1,0:T(8,128)(2,1)S(1)} %copy.25, s32[3072]{0:T(1024)S(1)} %pad_clamp_fusion), kind=kCustom, calls=%fused_computation | custom fusion | bytes 1188864 | tf_op jit(solution)/shard_map/jit(_take)/gather | solution.py:118
  (146 shorter events, 69.5 us)
Async XLA Ops:
  7.2 172.9 %copy-start = (bf16[384,128]{1,0:T(8,128)(2,1)S(1)}, bf16[384,128]{1,0:T(8,128)(2,1)}, u32[]{:S(2)}) copy-start(bf16[384,128]{1,0:T(8,128)(2,1)} %param.27) | copy-start | bytes 294916
  7.2 268.7 %all-gather.2.cloned.1.call-start = ((), (), s32[]{:S(2)}) async-start(), calls=%async_computation | async-start | bytes 1671168 | tf_op jit(solution)/shard_map/all_gather | solution.py:117
  8.1 7.5 %collective-permute-start = (bf16[256,128]{1,0:T(8,128)(2,1)S(1)}, bf16[256,128]{1,0:T(8,128)(2,1)S(1)}, u32[]{:S(2)}, u32[]{:S(2)}) collective-permute-start(bf16[256,128]{1,0:T(8,128)(2,1)S(1)} %get-tuple-element.69), channel_id=1, source_target_pairs={{0,1},{1,2},{2,3},{3,4},{4,5},{5,6},{6,7},{7,8},{8,9},{9,10},{10,1... | collective-permute-start | bytes 196616 | tf_op jit(solution)/shard_map/ppermute | solution.py:18
  10.5 5.3 %collective-permute-start.1 = (bf16[256,128]{1,0:T(8,128)(2,1)S(1)}, bf16[256,128]{1,0:T(8,128)(2,1)S(1)}, u32[]{:S(2)}, u32[]{:S(2)}) collective-permute-start(bf16[256,128]{1,0:T(8,128)(2,1)S(1)} %get-tuple-element.70), channel_id=1, source_target_pairs={{1,0},{2,1},{3,2},{4,3},{5,4},{6,5},{7,6},{8,7},{9,8},{10,9},{11,1... | collective-permute-start | bytes 196616 | tf_op jit(solution)/shard_map/ppermute | solution.py:19
  180.1 9.3 %copy-start.13 = (bf16[384,32]{0,1:T(8,128)(2,1)S(1)}, bf16[384,32]{0,1:T(8,128)(2,1)}, u32[]{:S(2)}) copy-start(bf16[384,32]{0,1:T(8,128)(2,1)} %param.28) | copy-start | bytes 73732
  180.1 9.3 %copy-start.14 = (bf16[32,128]{1,0:T(8,128)(2,1)S(1)}, bf16[32,128]{1,0:T(8,128)(2,1)}, u32[]{:S(2)}) copy-start(bf16[32,128]{1,0:T(8,128)(2,1)} %param.29) | copy-start | bytes 24580
  189.4 14.0 %copy-start.5 = (bf16[128,128]{1,0:T(8,128)(2,1)S(1)}, bf16[128,128]{1,0:T(8,128)(2,1)}, u32[]{:S(2)}) copy-start(bf16[128,128]{1,0:T(8,128)(2,1)} %param.30) | copy-start | bytes 98308
  208.0 5.5 %copy-start.7 = (f32[128]{0:T(128)S(1)}, f32[128]{0:T(128)}, u32[]{:S(2)}) copy-start(f32[128]{0:T(128)} %param.31) | copy-start | bytes 1540
  224.8 2.9 copy-start.1
  224.9 2.9 copy-start.2
  224.9 2.9 copy-start.9
  224.9 2.8 copy-start.11
  227.7 2.5 copy-start.8
  230.0 2.3 copy-start.4
  230.0 2.3 copy-start.6
  234.7 49.0 %copy-start.10 = (bf16[256,128]{1,0:T(8,128)(2,1)S(1)}, bf16[256,128]{1,0:T(8,128)(2,1)}, u32[]{:S(2)}) copy-start(bf16[256,128]{1,0:T(8,128)(2,1)} %param.35) | copy-start | bytes 196612
  282.4 2.8 copy-start.3
  282.4 2.8 copy-start.12
  283.7 2.7 copy-start.15
Sparse Core Ops, SparseCore 0:
  232.4 43.4 all-gather.1
where the time goes:
time: 299 us; the launch traced here: 296 us
  matrix products  111 us (37%)
  loops' own time  76.3 us (26%)
  waiting for transfers between devices  41.3 us (14%)
  local copies, waits for them, and re-layouts  26.4 us (9%)
  other arithmetic  22.1 us (7%)
  between operations  14.5 us (5%)
  starting transfers between devices  3.69 us (1%)
    another operation x1, loops' own time, on_device(): lax.map(pick_rows, (tile_starts, tile_send, tile_recv))  76.3 us
    dot_general x24, matrix products, pick_rows(): jnp.dot(recv_hot, own, preferred_element_type=jnp.float32)  41.8 us
    all_gather x1, waiting for transfers between devices, on_device(): lax.all_gather(coarse_latent, ('dom', 'sub'), axis=0, tiled=True)  41.1 us
    dot_general x24, matrix products, pick_rows(): jnp.dot(send_hot, beside_all, preferred_element_type=jnp.float32)  28.8 us
    dynamic_slice x48, local copies, waits for them, and re-layouts, on_device(): lax.map(pick_rows, (tile_starts, tile_send, tile_recv))  16.3 us
    dot_general x1, matrix products, on_device(): jnp.dot(low_rank, mod_v, preferred_element_type=jnp.float32)  14 us
    convert_element_type x1, other arithmetic, on_device(): (edge_latent.astype(jnp.float32) + layer_norm(update, edge_gain)).astype(...  11.3 us
    dot_general x1, matrix products, on_device(): jnp.dot(edge_in, edge_w1, preferred_element_type=jnp.float32)  9.31 us
  transfers between devices with their start and end apart: 3, of which 2 were waited for; matrix products, arithmetic and copies ran while one was open for 2% of the time, Pallas kernels for 0%

commit v1 on v0

v1 whole, which is shorter than its diff:
```python
import functools

import jax
import jax.numpy as jnp
from jax import lax
from jax.experimental import pallas as pl
from jax.experimental.pallas import tpu as pltpu
from jax.sharding import PartitionSpec as P

TILE = 128
HALO = 256
COARSEN = 8
STEP = 4
BF = jnp.bfloat16
F32 = jnp.float32


def dot(a, b):
    return jnp.dot(a, b, preferred_element_type=F32)


def silu(x):
    y = 0.5 * x
    return y * jnp.tanh(y) + y


def one_hot(mask):
    return jnp.where(mask, 1.0, 0.0).astype(BF)


def centred_weight(w):
    w = w.astype(F32)
    return (w - jnp.mean(w, axis=1, keepdims=True)).astype(BF)


def twice(w):
    z = jnp.zeros_like(w)
    return jnp.concatenate(
        [jnp.concatenate([w, z], axis=1), jnp.concatenate([z, w], axis=1)], axis=0
    )


def pair_dot(x, w2):
    half = x.shape[0] // 2
    out = dot(jnp.concatenate([x[:half], x[half:]], axis=1), w2)
    n = out.shape[1] // 2
    return jnp.concatenate([out[:, :n], out[:, n:]], axis=0)


def fine_kernel(
    edge_ref, send_ref, recv_ref, before_ref, own_ref, after_ref, cmap_ref, base_ref,
    w1_ref, u_ref, v_ref, w2_ref, gain_ref, nw1_ref, nw2_ref, ngain_ref,
    edge_out_ref, fine_ref, coarse_ref,
    sent_s, recv_s, we_s, w2_s, nw2_s, ones_s, pool_s,
):
    step = pl.program_id(0)
    lat = own_ref.shape[1]
    rows = own_ref.shape[0]
    window = TILE + 2 * HALO
    groups = send_ref.shape[0] // STEP
    crows = coarse_ref.shape[0]

    @pl.when(step == 0)
    def _():
        w_eff = (w1_ref[...].astype(F32) + dot(u_ref[...], v_ref[...])).astype(BF)
        we_s[...] = twice(w_eff[:lat])
        ws = w_eff[lat : 2 * lat]
        sent_s[0:HALO] = dot(before_ref[...], ws).astype(BF)
        sent_s[HALO : HALO + rows] = dot(own_ref[...], ws).astype(BF)
        sent_s[HALO + rows :] = dot(after_ref[...], ws).astype(BF)
        recv_s[...] = dot(own_ref[...], w_eff[2 * lat :]).astype(BF)
        w2_s[...] = twice(centred_weight(w2_ref[...]))
        nw2_s[...] = twice(centred_weight(nw2_ref[...]))
        ones_s[...] = twice(jnp.full((lat, lat), 1.0 / lat, BF))
        pool_s[...] = jnp.zeros_like(pool_s)

    lane = lax.broadcasted_iota(jnp.int32, (TILE, TILE), 1)
    sub = lax.broadcasted_iota(jnp.int32, (TILE, TILE), 0)
    recv = recv_ref[...]
    loc = recv & (TILE - 1)
    off = send_ref[...] - (recv - loc) + HALO
    loc_t = loc.T
    off_t = off.T
    gain = gain_ref[...]
    incoming = []
    for k in range(STEP):
        start = pl.multiple_of((step * STEP + k) * TILE, TILE)
        rhs = jnp.concatenate(
            [sent_s[pl.ds(start, window)], recv_s[pl.ds(start, TILE)]], axis=0
        )
        lhs = []
        for j in range(groups):
            col = k * groups + j
            o = jnp.broadcast_to(off_t[:, col : col + 1], (TILE, TILE))
            r = jnp.broadcast_to(loc_t[:, col : col + 1], (TILE, TILE))
            parts = [one_hot(o == lane + c * TILE) for c in range(window // TILE)]
            parts.append(one_hot(r == lane))
            lhs.append(jnp.concatenate(parts, axis=1))
        lhs = jnp.concatenate(lhs, axis=0)
        e0 = k * groups * TILE
        edges = edge_ref[e0 : e0 + groups * TILE]
        preact = dot(lhs, rhs) + pair_dot(edges, we_s[...])
        hidden = silu(preact).astype(BF)
        c = pair_dot(hidden, w2_s[...])
        var = pair_dot((c * c).astype(BF), ones_s[...])
        new = (edges.astype(F32) + c * lax.rsqrt(var + 1e-05) * gain).astype(BF)
        edge_out_ref[e0 : e0 + groups * TILE] = new
        back = jnp.concatenate(
            [
                one_hot(loc[k * groups + j : k * groups + j + 1] == sub)
                for j in range(groups)
            ],
            axis=1,
        )
        incoming.append(dot(back, new).astype(BF))
    incoming = jnp.concatenate(incoming, axis=0)
    start = pl.multiple_of(step * STEP * TILE, STEP * TILE)
    own = own_ref[pl.ds(start, STEP * TILE)]
    hidden = silu(dot(jnp.concatenate([own, incoming], axis=1), nw1_ref[...])).astype(BF)
    c = pair_dot(hidden, nw2_s[...])
    var = pair_dot((c * c).astype(BF), ones_s[...])
    fine = (own.astype(F32) + c * lax.rsqrt(var + 1e-05) * ngain_ref[...]).astype(BF)
    fine_ref[...] = fine
    csub = lax.broadcasted_iota(jnp.int32, (crows, TILE), 0) + base_ref[0] * crows
    member = jnp.concatenate(
        [
            one_hot(cmap_ref[pl.ds(step * STEP + k, 1), :] == csub)
            for k in range(STEP)
        ],
        axis=1,
    )
    pool_s[...] += dot(member, jnp.concatenate([fine, jnp.ones_like(fine)], axis=1))

    @pl.when(step == pl.num_programs(0) - 1)
    def _():
        total = pool_s[...]
        coarse_ref[...] = (total[:, :lat] / jnp.maximum(total[:, lat:], 1.0)).astype(BF)


def coarse_kernel(
    base_ref, send_ref, recv_ref, cmap_ref, fine_ref, w1_ref, w2_ref, gain_ref, *rest
):
    tables, out_ref = rest[:-1], rest[-1]
    dev = base_ref[0]
    crows, lat = tables[0].shape
    rows = send_ref.shape[0]
    send = send_ref[...]
    owner = lax.div(send, jnp.full_like(send, crows))
    other = owner ^ dev
    slot = jnp.zeros_like(send)
    for j in range(len(tables) - 1):
        slot = jnp.where(other == (1 << j), j + 1, slot)
    off = send - owner * crows + slot * crows
    loc = recv_ref[...] - dev * crows
    ws = w1_ref[:lat]
    proj = [dot(t[...], ws).astype(BF) for t in tables]
    own = tables[0][...]
    proj.append(dot(own, w1_ref[lat:]).astype(BF))
    rhs = jnp.concatenate(proj, axis=0)
    lane = lax.broadcasted_iota(jnp.int32, (TILE, TILE), 1)
    off_t = off.T
    loc_t = loc.T
    chunks = crows // TILE
    csub = lax.broadcasted_iota(jnp.int32, (crows, TILE), 0)
    group = 6 if rows % 6 == 0 else 1
    total = own.astype(F32)
    for g in range(rows // group):
        lhs = []
        for j in range(group):
            col = g * group + j
            o = jnp.broadcast_to(off_t[:, col : col + 1], (TILE, TILE))
            r = jnp.broadcast_to(loc_t[:, col : col + 1], (TILE, TILE))
            parts = [one_hot(o == lane + c * TILE) for c in range(chunks * len(tables))]
            parts += [one_hot(r == lane + c * TILE) for c in range(chunks)]
            lhs.append(jnp.concatenate(parts, axis=1))
        hidden = silu(dot(jnp.concatenate(lhs, axis=0), rhs)).astype(BF)
        msg = dot(hidden, w2_ref[...]).astype(BF)
        back = jnp.concatenate(
            [one_hot(loc[g * group + j : g * group + j + 1] == csub) for j in range(group)],
            axis=1,
        )
        total = total + dot(back, msg)
    centred = total - jnp.mean(total, axis=1, keepdims=True)
    var = jnp.mean(centred * centred, axis=1, keepdims=True)
    delta = (centred * lax.rsqrt(var + 1e-05) * gain_ref[...]).astype(BF)
    cm_t = (cmap_ref[...] - dev * crows).T
    for t in range(cmap_ref.shape[0]):
        m = jnp.broadcast_to(cm_t[:, t : t + 1], (TILE, TILE))
        hot = jnp.concatenate([one_hot(m == lane + c * TILE) for c in range(chunks)], axis=1)
        sl = slice(t * TILE, (t + 1) * TILE)
        out_ref[sl] = (fine_ref[sl].astype(F32) + dot(hot, delta)).astype(BF)


def on_device(
    node_latent, edge_latent, receivers, senders, coarse_map, coarse_recv, coarse_send,
    edge_w1, mod_u, mod_v, edge_w2, edge_gain, node_w1, node_w2, node_gain,
    coarse_w1, coarse_w2, coarse_gain,
):
    axes = ("dom", "sub")
    size = lax.axis_size(axes)
    dev = lax.axis_index(axes).astype(jnp.int32).reshape(1)
    nodes, lat = node_latent.shape
    edges = edge_latent.shape[0]
    tiles = nodes // TILE
    per = edges // tiles
    crows = nodes // COARSEN
    steps = tiles // STEP
    up = [(i, i + 1) for i in range(size - 1)]
    down = [(j, i) for i, j in up]
    before = lax.ppermute(node_latent[nodes - HALO :], axes, up)
    after = lax.ppermute(node_latent[:HALO], axes, down)
    send2 = senders.reshape(edges // TILE, TILE)
    recv2 = receivers.reshape(edges // TILE, TILE)
    cmap2 = coarse_map.reshape(tiles, TILE)
    vm = pl.BlockSpec(memory_space=pltpu.VMEM)
    sm = pl.BlockSpec(memory_space=pltpu.SMEM)
    idx = pl.BlockSpec((STEP * per // TILE, TILE), lambda i: (i, 0))
    edge_out, fine, coarse = pl.pallas_call(
        fine_kernel,
        grid=(steps,),
        in_specs=[pl.BlockSpec((STEP * per, lat), lambda i: (i, 0)), idx, idx]
        + [vm] * 4 + [sm] + [vm] * 8,
        out_specs=[
            pl.BlockSpec((STEP * per, lat), lambda i: (i, 0)),
            pl.BlockSpec((STEP * TILE, lat), lambda i: (i, 0)),
            pl.BlockSpec((crows, lat), lambda i: (0, 0)),
        ],
        out_shape=[
            jax.ShapeDtypeStruct((edges, lat), BF),
            jax.ShapeDtypeStruct((nodes, lat), BF),
            jax.ShapeDtypeStruct((crows, lat), BF),
        ],
        scratch_shapes=[
            pltpu.VMEM((nodes + 2 * HALO, lat), BF),
            pltpu.VMEM((nodes, lat), BF),
            pltpu.VMEM((2 * lat, 2 * lat), BF),
            pltpu.VMEM((2 * lat, 2 * lat), BF),
            pltpu.VMEM((2 * lat, 2 * lat), BF),
            pltpu.VMEM((2 * lat, 2 * lat), BF),
            pltpu.VMEM((crows, 2 * lat), F32),
        ],
        compiler_params=pltpu.CompilerParams(
            dimension_semantics=("arbitrary",), vmem_limit_bytes=48 * 2**20
        ),
        name="fine",
    )(
        edge_latent, send2, recv2, before, node_latent, after, cmap2, dev,
        edge_w1, mod_u, mod_v, edge_w2, edge_gain.reshape(1, lat),
        node_w1, node_w2, node_gain.reshape(1, lat),
    )
    tables = [coarse]
    bit = 1
    while bit < size:
        tables.append(lax.ppermute(coarse, axes, [(i, i ^ bit) for i in range(size)]))
        bit *= 2
    cedges = coarse_send.shape[0]
    node_out = pl.pallas_call(
        coarse_kernel,
        in_specs=[sm] + [vm] * (7 + len(tables)),
        out_specs=vm,
        out_shape=jax.ShapeDtypeStruct((nodes, lat), BF),
        compiler_params=pltpu.CompilerParams(vmem_limit_bytes=48 * 2**20),
        name="coarse",
    )(
        dev, coarse_send.reshape(cedges // TILE, TILE), coarse_recv.reshape(cedges // TILE, TILE),
        cmap2, fine, coarse_w1, coarse_w2, coarse_gain.reshape(1, lat), *tables,
    )
    return (node_out, edge_out)


def solution(mesh):
    split = P(("groups", "dom", "sub"))
    wide = P(("groups", "dom", "sub"), None)
    return jax.shard_map(
        on_device,
        mesh=mesh,
        in_specs=(wide, wide) + (split,) * 5 + (P(),) * 11,
        out_specs=(wide, wide),
        check_vma=False,
    )
```

time: 299 us -> 66 us (0.22)
  matrix products: 111 us -> 0 us
  loops' own time: 76.3 us -> 0 us
  waiting for transfers between devices: 41.3 us -> 4.62 us
  Pallas kernels: 0 us -> 35.2 us
  other arithmetic: 22.1 us -> 0 us
  local copies, waits for them, and re-layouts: 26.4 us -> 10.7 us
  between operations: 14.5 us -> 0.77 us
  starting transfers between devices: 3.69 us -> 14 us
    dot_general x58 -> x0, matrix products: 111 us -> none  [the longest x24 41.8 us: pick_rows(): jnp.dot(recv_hot, own, preferred_element_type=jnp.float32)]
    another operation x1 -> x0, loops' own time: 76.3 us -> none  [on_device(): lax.map(pick_rows, (tile_starts, tile_send, tile_recv))]
    all_gather x1 -> x0, waiting for transfers between devices: 41.1 us -> none  [on_device(): lax.all_gather(coarse_latent, ('dom', 'sub'), axis=0, tiled=True)]
    pallas_call x0 -> x2, Pallas kernels: none -> 35.2 us  [the longest x1 26.2 us: on_device(): pl.pallas_call(fine_kernel, grid=(steps,), in_specs=[pl.BlockSpec((STEP *...]
    dynamic_slice x48 -> x0, local copies, waits for them, and re-layouts: 16.3 us -> none  [on_device(): lax.map(pick_rows, (tile_starts, tile_send, tile_recv))]
    convert_element_type x2 -> x0, other arithmetic: 11.6 us -> none  [the longest x1 11.3 us: on_device(): (edge_latent.astype(jnp.float32) + layer_norm(update, edge_gain)).astype(...]
    ppermute x2 -> x6, starting transfers between devices: 3.65 us -> 14 us  [the longest x4 9.65 us: on_device(): lax.ppermute(coarse, axes, [(i, i ^ bit) for i in range(size)])]
    unnamed x34 -> x33, local copies, waits for them, and re-layouts: 2.65 us -> 9.73 us
  transfers between devices with their start and end apart: 3 -> 6, of which waited for: 2 -> 3; matrix products, arithmetic and copies ran while one was open for 2% -> 1% of each run, Pallas kernels for 0% -> 0%
where the time goes in v1:
time: 66 us; the launch traced here: 65.3 us
  Pallas kernels  35.2 us (53%)
  starting transfers between devices  14 us (21%)
  local copies, waits for them, and re-layouts  10.7 us (16%)
  waiting for transfers between devices  4.62 us (7%)
  between operations  0.77 us (1%)
    pallas_call x1, Pallas kernels, on_device(): pl.pallas_call(fine_kernel, grid=(steps,), in_specs=[pl.BlockSpec((STEP *...  26.2 us
    unnamed x33, local copies, waits for them, and re-layouts  9.73 us
    ppermute x4, starting transfers between devices, on_device(): lax.ppermute(coarse, axes, [(i, i ^ bit) for i in range(size)])  9.65 us
    pallas_call x1, Pallas kernels, on_device(): pl.pallas_call(coarse_kernel, in_specs=[sm] + [vm] * (7 + len(tables)), o...  9.05 us
    ppermute x4, waiting for transfers between devices, on_device(): lax.ppermute(coarse, axes, [(i, i ^ bit) for i in range(size)])  4.61 us
    ppermute x1, starting transfers between devices, on_device(): before = lax.ppermute(node_latent[nodes - HALO:], axes, up)  3.03 us
  transfers between devices with their start and end apart: 6, of which 3 were waited for; matrix products, arithmetic and copies ran while one was open for 1% of the time, Pallas kernels for 0%

profile of v1, /device:TPU:0, one launch (start us, length us, event | category | flops | bytes accessed | tf_op | source)
XLA Modules:
  0.0 65.3 jit_solution(12339448592168298469)
XLA Ops:
  0.6 0.0 copy-start.15
  0.6 0.0 copy-start.9
  0.7 0.0 copy-start.5
  0.7 0.0 copy-start.10
  0.7 0.9 %fusion = (bf16[256,128]{1,0:T(8,128)(2,1)S(1)}, bf16[256,128]{1,0:T(8,128)(2,1)S(1)}) fusion(bf16[3072,128]{1,0:T(8,128)(2,1)} %own_ref.1), kind=kLoop, calls=%fused_computation | loop fusion | bytes 262144 | tf_op jit(solution)/shard_map/slice | solution.py:211
  1.6 1.3 %collective-permute-start.1 = (bf16[256,128]{1,0:T(8,128)(2,1)S(1)}, bf16[256,128]{1,0:T(8,128)(2,1)S(1)}, u32[]{:S(2)}, u32[]{:S(2)}) collective-permute-start(bf16[256,128]{1,0:T(8,128)(2,1)S(1)} %get-tuple-element.8), channel_id=1, source_target_pairs={{1,0},{2,1},{3,2},{4,3},{5,4},{6,5},{7,6},{8,7},{9,8},{10,9},{11,1... | collective-permute-start | bytes 196616 | tf_op jit(solution)/shard_map/ppermute | solution.py:211
  2.9 3.0 %collective-permute-start = (bf16[256,128]{1,0:T(8,128)(2,1)S(1)}, bf16[256,128]{1,0:T(8,128)(2,1)S(1)}, u32[]{:S(2)}, u32[]{:S(2)}) collective-permute-start(bf16[256,128]{1,0:T(8,128)(2,1)S(1)} %get-tuple-element.9), channel_id=1, source_target_pairs={{0,1},{1,2},{2,3},{3,4},{4,5},{5,6},{6,7},{7,8},{8,9},{9,10},{10,1... | collective-permute-start | bytes 196616 | tf_op jit(solution)/shard_map/ppermute | solution.py:210
  6.0 0.9 %copy.20.u_ref = bf16[384,32]{1,0:T(8,128)(2,1)S(1)} copy(bf16[384,32]{0,1:T(8,128)(2,1)} %param.26) | data formatting | bytes 49152 | tf_op args[8]
  6.8 0.0 collective-permute-done.1.after_ref
  6.8 0.0 collective-permute-done.before_ref
  6.8 0.0 copy-start
  6.9 1.1 %copy-done = bf16[3072,128]{1,0:T(8,128)(2,1)S(1)} copy-done((bf16[3072,128]{1,0:T(8,128)(2,1)S(1)}, bf16[3072,128]{1,0:T(8,128)(2,1)}, u32[]{:S(2)}) %copy-start) | copy-done | bytes 786456
  8.0 0.9 %copy-done.1 = bf16[384,128]{1,0:T(8,128)(2,1)S(1)} copy-done((bf16[384,128]{1,0:T(8,128)(2,1)S(1)}, bf16[384,128]{1,0:T(8,128)(2,1)}, u32[]{:S(2)}) %copy-start.1) | copy-done | bytes 98328
  8.9 0.9 %copy-done.2 = s32[18432]{0:T(1024)S(1)} copy-done((s32[18432]{0:T(1024)S(1)}, s32[18432]{0:T(1024)}, u32[]{:S(2)}) %copy-start.2) | copy-done | bytes 73752
  9.8 0.9 %copy-done.3 = s32[18432]{0:T(1024)S(1)} copy-done((s32[18432]{0:T(1024)S(1)}, s32[18432]{0:T(1024)}, u32[]{:S(2)}) %copy-start.3) | copy-done | bytes 73752
  10.6 0.8 %copy-done.4 = bf16[256,128]{1,0:T(8,128)(2,1)S(1)} copy-done((bf16[256,128]{1,0:T(8,128)(2,1)S(1)}, bf16[256,128]{1,0:T(8,128)(2,1)}, u32[]{:S(2)}) %copy-start.4) | copy-done | bytes 65560
  11.5 0.7 %copy-done.6 = s32[3072]{0:T(1024)S(1)} copy-done((s32[3072]{0:T(1024)S(1)}, s32[3072]{0:T(1024)}, u32[]{:S(2)}) %copy-start.6) | copy-done | bytes 12312
  12.2 0.8 %copy-done.7 = bf16[128,128]{1,0:T(8,128)(2,1)S(1)} copy-done((bf16[128,128]{1,0:T(8,128)(2,1)S(1)}, bf16[128,128]{1,0:T(8,128)(2,1)}, u32[]{:S(2)}) %copy-start.7) | copy-done | bytes 32792
  13.0 0.8 %copy-done.8 = bf16[128,128]{1,0:T(8,128)(2,1)S(1)} copy-done((bf16[128,128]{1,0:T(8,128)(2,1)S(1)}, bf16[128,128]{1,0:T(8,128)(2,1)}, u32[]{:S(2)}) %copy-start.8) | copy-done | bytes 32792
  13.7 0.7 %copy-done.12 = bf16[32,128]{1,0:T(8,128)(2,1)S(1)} copy-done((bf16[32,128]{1,0:T(8,128)(2,1)S(1)}, bf16[32,128]{1,0:T(8,128)(2,1)}, u32[]{:S(2)}) %copy-start.12) | copy-done | bytes 8216
  14.4 0.7 %copy-done.13 = f32[128]{0:T(128)S(1)} copy-done((f32[128]{0:T(128)S(1)}, f32[128]{0:T(128)}, u32[]{:S(2)}) %copy-start.13) | copy-done | bytes 536
  15.1 0.7 %copy-done.14 = f32[128]{0:T(128)S(1)} copy-done((f32[128]{0:T(128)S(1)}, f32[128]{0:T(128)}, u32[]{:S(2)}) %copy-start.14) | copy-done | bytes 536
  15.7 26.2 %fine.1 = (bf16[18432,128]{1,0:T(8,128)(2,1)}, bf16[3072,128]{1,0:T(8,128)(2,1)S(1)}, bf16[384,128]{1,0:T(8,128)(2,1)S(1)}) custom-call(bf16[18432,128]{1,0:T(8,128)(2,1)} %edge_ref.1, s32[144,128]{1,0:T(8,128)S(1)} %bitcast.9, s32[144,128]{1,0:T(8,128)S(1)} %bitcast.10, bf16[256,128]{1,0:T(8,128)(2,1)S(1)} %collective-permute-done.before_ref, ...), custom_call_target="tpu_custom_call" | custom-call | tf_op jit(solution)/shard_map/fine/pallas_call | solution.py:218
  41.9 8.0 %collective-permute-start.5 = (bf16[384,128]{1,0:T(8,128)(2,1)S(1)}, bf16[384,128]{1,0:T(8,128)(2,1)S(1)}, u32[]{:S(2)}, u32[]{:S(2)}) collective-permute-start(bf16[384,128]{1,0:T(8,128)(2,1)S(1)} %get-tuple-element.6.rest_0_), channel_id=1, source_target_pairs={{0,8},{1,9},{2,10},{3,11},{4,12},{5,13},{6,14},{7,15},{8,0},{9,1},... | collective-permute-start | bytes 294920 | tf_op jit(solution)/shard_map/ppermute | solution.py:254
  49.9 1.6 %collective-permute-start.4 = (bf16[384,128]{1,0:T(8,128)(2,1)S(1)}, bf16[384,128]{1,0:T(8,128)(2,1)S(1)}, u32[]{:S(2)}, u32[]{:S(2)}) collective-permute-start(bf16[384,128]{1,0:T(8,128)(2,1)S(1)} %get-tuple-element.6.rest_0_), channel_id=1, source_target_pairs={{0,4},{1,5},{2,6},{3,7},{4,0},{5,1},{6,2},{7,3},{8,12},{9,13},{10,... | collective-permute-start | bytes 294920 | tf_op jit(solution)/shard_map/ppermute | solution.py:254
  51.6 0.0 collective-permute-start.3
  51.6 0.0 collective-permute-start.2
  51.6 1.0 %collective-permute-done.5.rest_4_ = bf16[384,128]{1,0:T(8,128)(2,1)S(1)} collective-permute-done((bf16[384,128]{1,0:T(8,128)(2,1)S(1)}, bf16[384,128]{1,0:T(8,128)(2,1)S(1)}, u32[]{:S(2)}, u32[]{:S(2)}) %collective-permute-start.5) | collective-permute-done | bytes 98336 | tf_op jit(solution)/shard_map/ppermute | solution.py:254
  52.5 2.0 %collective-permute-done.4.rest_3_ = bf16[384,128]{1,0:T(8,128)(2,1)S(1)} collective-permute-done((bf16[384,128]{1,0:T(8,128)(2,1)S(1)}, bf16[384,128]{1,0:T(8,128)(2,1)S(1)}, u32[]{:S(2)}, u32[]{:S(2)}) %collective-permute-start.4) | collective-permute-done | bytes 98336 | tf_op jit(solution)/shard_map/ppermute | solution.py:254
  54.6 1.6 %collective-permute-done.3.rest_2_ = bf16[384,128]{1,0:T(8,128)(2,1)S(1)} collective-permute-done((bf16[384,128]{1,0:T(8,128)(2,1)S(1)}, bf16[384,128]{1,0:T(8,128)(2,1)S(1)}, u32[]{:S(2)}, u32[]{:S(2)}) %collective-permute-start.3) | collective-permute-done | bytes 98336 | tf_op jit(solution)/shard_map/ppermute | solution.py:254
  56.2 0.0 collective-permute-done.2.rest_1_
  56.2 9.0 %coarse.1 = bf16[3072,128]{1,0:T(8,128)(2,1)} custom-call(s32[1]{0:T(128)} %bitcast.base_ref, s32[18,128]{1,0:T(8,128)S(1)} %bitcast.13, s32[18,128]{1,0:T(8,128)S(1)} %bitcast.14, s32[24,128]{1,0:T(8,128)S(1)} %bitcast.12, bf16[3072,128]{1,0:T(8,128)(2,1)S(1)} %get-tuple-element.5.fine_ref, bf16[256,128]{1,0:T(8,128)(2,1)S(1)} %copy-done.5, ...), custom_call_target="tpu_custom_call" | custom-call | tf_op jit(solution)/shard_map/coarse/pallas_call | solution.py:257
  (16 shorter events, 0.0 us)
Async XLA Ops:
  0.6 55.5 %copy-start.15 = (f32[128]{0:T(128)S(1)}, f32[128]{0:T(128)}, u32[]{:S(2)}) copy-start(f32[128]{0:T(128)} %param.35) | copy-start | bytes 1540
  0.6 55.5 %copy-start.9 = (bf16[128,128]{1,0:T(8,128)(2,1)S(1)}, bf16[128,128]{1,0:T(8,128)(2,1)}, u32[]{:S(2)}) copy-start(bf16[128,128]{1,0:T(8,128)(2,1)} %w2_ref.3) | copy-start | bytes 98308
  0.7 55.5 %copy-start.5 = (bf16[256,128]{1,0:T(8,128)(2,1)S(1)}, bf16[256,128]{1,0:T(8,128)(2,1)}, u32[]{:S(2)}) copy-start(bf16[256,128]{1,0:T(8,128)(2,1)} %w1_ref.3) | copy-start | bytes 196612
  0.7 55.5 %copy-start.10 = (s32[2304]{0:T(1024)S(1)}, s32[2304]{0:T(1024)}, u32[]{:S(2)}) copy-start(s32[2304]{0:T(1024)} %param.24) | copy-start | bytes 27652
  0.7 55.5 %copy-start.11 = (s32[2304]{0:T(1024)S(1)}, s32[2304]{0:T(1024)}, u32[]{:S(2)}) copy-start(s32[2304]{0:T(1024)} %param.23) | copy-start | bytes 27652
  1.6 5.2 %collective-permute-start.1 = (bf16[256,128]{1,0:T(8,128)(2,1)S(1)}, bf16[256,128]{1,0:T(8,128)(2,1)S(1)}, u32[]{:S(2)}, u32[]{:S(2)}) collective-permute-start(bf16[256,128]{1,0:T(8,128)(2,1)S(1)} %get-tuple-element.8), channel_id=1, source_target_pairs={{1,0},{2,1},{3,2},{4,3},{5,4},{6,5},{7,6},{8,7},{9,8},{10,9},{11,1... | collective-permute-start | bytes 196616 | tf_op jit(solution)/shard_map/ppermute | solution.py:211
  2.9 3.9 %collective-permute-start = (bf16[256,128]{1,0:T(8,128)(2,1)S(1)}, bf16[256,128]{1,0:T(8,128)(2,1)S(1)}, u32[]{:S(2)}, u32[]{:S(2)}) collective-permute-start(bf16[256,128]{1,0:T(8,128)(2,1)S(1)} %get-tuple-element.9), channel_id=1, source_target_pairs={{0,1},{1,2},{2,3},{3,4},{4,5},{5,6},{6,7},{7,8},{8,9},{9,10},{10,1... | collective-permute-start | bytes 196616 | tf_op jit(solution)/shard_map/ppermute | solution.py:210
  6.8 1.1 %copy-start = (bf16[3072,128]{1,0:T(8,128)(2,1)S(1)}, bf16[3072,128]{1,0:T(8,128)(2,1)}, u32[]{:S(2)}) copy-start(bf16[3072,128]{1,0:T(8,128)(2,1)} %own_ref.1) | copy-start | bytes 2359300
  8.0 0.9 %copy-start.1 = (bf16[384,128]{1,0:T(8,128)(2,1)S(1)}, bf16[384,128]{1,0:T(8,128)(2,1)}, u32[]{:S(2)}) copy-start(bf16[384,128]{1,0:T(8,128)(2,1)} %w1_ref.2) | copy-start | bytes 294916
  8.9 0.9 %copy-start.2 = (s32[18432]{0:T(1024)S(1)}, s32[18432]{0:T(1024)}, u32[]{:S(2)}) copy-start(s32[18432]{0:T(1024)} %param.21) | copy-start | bytes 221188
  9.8 0.9 %copy-start.3 = (s32[18432]{0:T(1024)S(1)}, s32[18432]{0:T(1024)}, u32[]{:S(2)}) copy-start(s32[18432]{0:T(1024)} %param.20) | copy-start | bytes 221188
  10.6 0.8 %copy-start.4 = (bf16[256,128]{1,0:T(8,128)(2,1)S(1)}, bf16[256,128]{1,0:T(8,128)(2,1)}, u32[]{:S(2)}) copy-start(bf16[256,128]{1,0:T(8,128)(2,1)} %nw1_ref.1) | copy-start | bytes 196612
  11.5 0.7 %copy-start.6 = (s32[3072]{0:T(1024)S(1)}, s32[3072]{0:T(1024)}, u32[]{:S(2)}) copy-start(s32[3072]{0:T(1024)} %param.22) | copy-start | bytes 36868
  12.2 0.8 %copy-start.7 = (bf16[128,128]{1,0:T(8,128)(2,1)S(1)}, bf16[128,128]{1,0:T(8,128)(2,1)}, u32[]{:S(2)}) copy-start(bf16[128,128]{1,0:T(8,128)(2,1)} %w2_ref.2) | copy-start | bytes 98308
  13.0 0.8 %copy-start.8 = (bf16[128,128]{1,0:T(8,128)(2,1)S(1)}, bf16[128,128]{1,0:T(8,128)(2,1)}, u32[]{:S(2)}) copy-start(bf16[128,128]{1,0:T(8,128)(2,1)} %nw2_ref.1) | copy-start | bytes 98308
  13.7 0.7 %copy-start.12 = (bf16[32,128]{1,0:T(8,128)(2,1)S(1)}, bf16[32,128]{1,0:T(8,128)(2,1)}, u32[]{:S(2)}) copy-start(bf16[32,128]{1,0:T(8,128)(2,1)} %v_ref.1) | copy-start | bytes 24580
  14.4 0.7 %copy-start.13 = (f32[128]{0:T(128)S(1)}, f32[128]{0:T(128)}, u32[]{:S(2)}) copy-start(f32[128]{0:T(128)} %param.29) | copy-start | bytes 1540
  15.1 0.7 %copy-start.14 = (f32[128]{0:T(128)S(1)}, f32[128]{0:T(128)}, u32[]{:S(2)}) copy-start(f32[128]{0:T(128)} %param.32) | copy-start | bytes 1540
  41.9 10.6 %collective-permute-start.5 = (bf16[384,128]{1,0:T(8,128)(2,1)S(1)}, bf16[384,128]{1,0:T(8,128)(2,1)S(1)}, u32[]{:S(2)}, u32[]{:S(2)}) collective-permute-start(bf16[384,128]{1,0:T(8,128)(2,1)S(1)} %get-tuple-element.6.rest_0_), channel_id=1, source_target_pairs={{0,8},{1,9},{2,10},{3,11},{4,12},{5,13},{6,14},{7,15},{8,0},{9,1},... | collective-permute-start | bytes 294920 | tf_op jit(solution)/shard_map/ppermute | solution.py:254
  49.9 4.6 %collective-permute-start.4 = (bf16[384,128]{1,0:T(8,128)(2,1)S(1)}, bf16[384,128]{1,0:T(8,128)(2,1)S(1)}, u32[]{:S(2)}, u32[]{:S(2)}) collective-permute-start(bf16[384,128]{1,0:T(8,128)(2,1)S(1)} %get-tuple-element.6.rest_0_), channel_id=1, source_target_pairs={{0,4},{1,5},{2,6},{3,7},{4,0},{5,1},{6,2},{7,3},{8,12},{9,13},{10,... | collective-permute-start | bytes 294920 | tf_op jit(solution)/shard_map/ppermute | solution.py:254
  51.6 4.6 %collective-permute-start.3 = (bf16[384,128]{1,0:T(8,128)(2,1)S(1)}, bf16[384,128]{1,0:T(8,128)(2,1)S(1)}, u32[]{:S(2)}, u32[]{:S(2)}) collective-permute-start(bf16[384,128]{1,0:T(8,128)(2,1)S(1)} %get-tuple-element.6.rest_0_), channel_id=1, source_target_pairs={{0,2},{1,3},{2,0},{3,1},{4,6},{5,7},{6,4},{7,5},{8,10},{9,11},{10,... | collective-permute-start | bytes 294920 | tf_op jit(solution)/shard_map/ppermute | solution.py:254
  51.6 4.6 %collective-permute-start.2 = (bf16[384,128]{1,0:T(8,128)(2,1)S(1)}, bf16[384,128]{1,0:T(8,128)(2,1)S(1)}, u32[]{:S(2)}, u32[]{:S(2)}) collective-permute-start(bf16[384,128]{1,0:T(8,128)(2,1)S(1)} %get-tuple-element.6.rest_0_), channel_id=1, source_target_pairs={{0,1},{1,0},{2,3},{3,2},{4,5},{5,4},{6,7},{7,6},{8,9},{9,8},{10,11... | collective-permute-start | bytes 294920 | tf_op jit(solution)/shard_map/ppermute | solution.py:254

commit v2 on v1

v2 whole, which is shorter than its diff:
```python
import functools

import jax
import jax.numpy as jnp
from jax import lax
from jax.experimental import pallas as pl
from jax.experimental.pallas import tpu as pltpu
from jax.sharding import PartitionSpec as P

TILE = 128
HALO = 256
COARSEN = 8
STEP = 2
PARTS = 2
PAD = 16
BF = jnp.bfloat16
F32 = jnp.float32
I16 = jnp.int16


def dot(a, b):
    return jnp.dot(a, b, preferred_element_type=F32)


def one_hot(mask):
    return jnp.where(mask, jnp.ones((), BF), jnp.zeros((), BF))


def pick(off, lane, blocks):
    return [one_hot(off == lane + I16(c * TILE)) for c in range(blocks)]


def column(rows_t, col):
    return jnp.broadcast_to(rows_t[:, col : col + 1], (TILE, TILE))


def along_lanes(row, count):
    return jnp.broadcast_to(row, (count, TILE)).astype(I16)


def twice(w):
    z = jnp.zeros_like(w)
    return jnp.concatenate(
        [jnp.concatenate([w, z], axis=1), jnp.concatenate([z, w], axis=1)], axis=0
    )


def pair_dot(x, w2):
    half = x.shape[0] // 2
    out = dot(jnp.concatenate([x[:half], x[half:]], axis=1), w2)
    n = out.shape[1] // 2
    return jnp.concatenate([out[:, :n], out[:, n:]], axis=0)


def gained(w, gain):
    w = w.astype(F32)
    return twice(((w - jnp.mean(w, axis=1, keepdims=True)) * gain).astype(BF))


def mean_weight(gain):
    lat = gain.shape[1]
    return twice(jnp.broadcast_to(1.0 / (gain * gain * lat), (lat, lat)).T.astype(BF))


def norm(hidden, w, m):
    c = pair_dot(hidden, w)
    return c * lax.rsqrt(pair_dot((c * c).astype(BF), m) + 1e-05)


def half_silu(y):
    return (y * jnp.tanh(y) + y).astype(BF)


def fine_kernel(base_ref, edge_ref, last_ref, before_ref, after_ref, *refs):
    hbm, refs = refs[:12], refs[12:]
    (edge_out_ref, fine_ref, coarse_ref), refs = refs[:3], refs[3:]
    vmem, refs = refs[:12], refs[12:]
    own_ref, send_ref, recv_ref, cmap_ref, w1_ref, u_ref, v_ref = vmem[:7]
    edge_w2_ref, nw1_ref, node_w2_ref, gain_ref, ngain_ref = vmem[7:]
    sent_s, recv_s, we_s, w2_s, m_s, nw1_s, nw2_s, nm_s, code_s, loc_s, hid_s, inc_s, pool_s, sem = refs
    step = pl.program_id(0)
    steps = pl.num_programs(0) - 2
    rows, lat = own_ref.shape
    per = edge_ref.shape[0] // STEP
    groups = per // TILE
    idx_rows = STEP * groups
    crows = coarse_ref.shape[0]
    low_blocks = 3
    high_blocks = (TILE + 2 * HALO) // TILE - low_blocks

    @pl.when(step == 0)
    def _():
        copies = [pltpu.make_async_copy(a, b, sem.at[i]) for i, (a, b) in enumerate(zip(hbm, vmem))]
        for c in copies:
            c.start()
        for c in copies:
            c.wait()
        w_eff = w1_ref[...].astype(F32) + lax.dot_general(
            u_ref[...], v_ref[...], (((0,), (0,)), ((), ())), preferred_element_type=F32
        )
        w_eff = (0.5 * w_eff).astype(BF)
        we_s[...] = twice(w_eff[:lat])
        ws = w_eff[lat : 2 * lat]
        both = dot(own_ref[...], jnp.concatenate([ws, w_eff[2 * lat :]], axis=1)).astype(BF)
        sent_s[0:HALO] = dot(before_ref[...], ws).astype(BF)
        sent_s[HALO : HALO + rows] = both[:, :lat]
        sent_s[HALO + rows :] = dot(after_ref[...], ws).astype(BF)
        recv_s[...] = both[:, lat:]
        w2_s[...] = gained(edge_w2_ref[...], gain_ref[...])
        m_s[...] = mean_weight(gain_ref[...])
        nw2_s[...] = gained(node_w2_ref[...], ngain_ref[...])
        nm_s[...] = mean_weight(ngain_ref[...])
        nw1_s[...] = nw1_ref[...] * 0.5
        pool_s[...] = jnp.zeros_like(pool_s)
        recv = recv_ref[...]
        loc = recv & (TILE - 1)
        off = send_ref[...] - (recv - loc) + HALO
        hi = off >= low_blocks * TILE
        lo = jnp.where(hi, off - low_blocks * TILE, off)
        code = lo | (loc << 16) | jnp.where(hi, jnp.int32(-(2**31)), 0)
        for s in range(rows // TILE // STEP):
            sl = slice(s * idx_rows, (s + 1) * idx_rows)
            code_s[s, :, 0:idx_rows] = code[sl].T
            loc_s[s, 0:idx_rows] = loc[sl]

    this, prev, past = step, step - 1, step - 2
    part = per // PARTS
    lane = lax.broadcasted_iota(I16, (TILE, TILE), 1)
    sub = lax.broadcasted_iota(I16, (TILE, TILE), 0)
    csub = lax.broadcasted_iota(I16, (crows, TILE), 0)
    incoming = [[] for _ in range(STEP)]

    def weights(k):
        start = pl.multiple_of((this * STEP + k) * TILE, TILE)
        mine = recv_s[pl.ds(start, TILE)]
        low = jnp.concatenate([sent_s[pl.ds(start, low_blocks * TILE)], mine], axis=0)
        high = jnp.concatenate(
            [
                sent_s[pl.ds(start + low_blocks * TILE, high_blocks * TILE)],
                sent_s[pl.ds(start, (low_blocks - high_blocks) * TILE)],
                mine,
            ],
            axis=0,
        )
        return jnp.concatenate([low, high], axis=1)

    def first(k, q):
        at = slice(k * per + q * part, k * per + (q + 1) * part)
        code_t = code_s[this]
        lhs, upper = [], []
        for j in range(part // TILE):
            word = column(code_t, at.start // TILE + j)
            o = word.astype(I16) & I16(511)
            r = (word >> 16).astype(I16) & I16(TILE - 1)
            lhs.append(jnp.concatenate(pick(o, lane, low_blocks) + pick(r, lane, 1), axis=1))
            upper.append(word < 0)
        out = dot(jnp.concatenate(lhs, axis=0), weights(k))
        y = pair_dot(edge_ref[at], we_s[...])
        yield
        y = y + jnp.where(jnp.concatenate(upper, axis=0), out[:, lat:], out[:, :lat])
        hid_s[at] = half_silu(y)

    def second(k, q):
        at = slice(k * per + q * part, k * per + (q + 1) * part)
        c = pair_dot(hid_s[at], w2_s[...])
        yield
        var = pair_dot((c * c).astype(BF), m_s[...])
        yield
        new = (last_ref[at].astype(F32) + c * lax.rsqrt(var + 1e-05)).astype(BF)
        edge_out_ref[at] = new
        loc = loc_s[prev]
        back = [
            one_hot(along_lanes(loc[j : j + 1], TILE) == sub)
            for j in range(at.start // TILE, at.stop // TILE)
        ]
        incoming[k].append(dot(jnp.concatenate(back, axis=1), new))
        yield
        if q == PARTS - 1:
            inc_s[k * TILE : (k + 1) * TILE] = sum(incoming[k][1:], incoming[k][0]).astype(BF)

    def third():
        here = pl.ds(pl.multiple_of(past * STEP * TILE, STEP * TILE), STEP * TILE)
        own = own_ref[here]
        y = dot(jnp.concatenate([own, inc_s[...]], axis=1), nw1_s[...])
        yield
        c = pair_dot(half_silu(y), nw2_s[...])
        yield
        var = pair_dot((c * c).astype(BF), nm_s[...])
        yield
        fine = (own.astype(F32) + c * lax.rsqrt(var + 1e-05)).astype(BF)
        fine_ref[here] = fine
        member = []
        for k in range(STEP):
            local = cmap_ref[pl.ds(past * STEP + k, 1), :] - base_ref[0] * crows
            member.append(one_hot(along_lanes(local, crows) == csub))
        fine = jnp.concatenate([fine, jnp.ones_like(fine)], axis=1)
        pool_s[...] += dot(jnp.concatenate(member, axis=1), fine)

    def stages(one, two, three):
        for k in range(STEP):
            incoming[k].clear()
        active = [third()] if three else []
        todo = [(k, q) for k in range(STEP) for q in range(PARTS)] if one or two else []
        while active or todo:
            if todo:
                k, q = todo.pop(0)
                active = [second(k, q)] * two + [first(k, q)] * one + active
            alive = []
            for g in active:
                try:
                    next(g)
                    alive.append(g)
                except StopIteration:
                    pass
            active = alive

    full = (step >= 2) & (step < steps)
    for when, which in (
        (full, (True, True, True)),
        (step == 0, (True, False, False)),
        (step == 1, (True, True, False)),
        (step == steps, (False, True, True)),
        (step == steps + 1, (False, False, True)),
    ):
        pl.when(when)(functools.partial(stages, *which))

    @pl.when(step == steps + 1)
    def _():
        total = pool_s[...]
        coarse_ref[...] = (total[:, :lat] / jnp.maximum(total[:, lat:], 1.0)).astype(BF)


def coarse_kernel(
    base_ref, send_ref, recv_ref, cmap_ref, fine_ref, w1_ref, w2_ref, gain_ref, *refs
):
    tables, (out_ref, out_s, sem) = refs[:-3], refs[-3:]
    dev = base_ref[0]
    crows, lat = tables[0].shape
    rows = send_ref.shape[0]
    nodes = fine_ref.shape[0]
    chunks = crows // TILE
    blocks = chunks * len(tables)
    lows = (blocks + 1) // 2
    send = send_ref[...]
    owner = lax.div(send, jnp.full_like(send, crows))
    other = owner ^ dev
    slot = jnp.zeros_like(send)
    for j in range(len(tables) - 1):
        slot = jnp.where(other == (1 << j), j + 1, slot)
    off = send - owner * crows + slot * crows
    hi = off >= lows * TILE
    lo = jnp.where(hi, off - lows * TILE, off)
    loc = recv_ref[...] - dev * crows
    w1 = w1_ref[...] * 0.5
    proj = jnp.concatenate([dot(t[...], w1[:lat]).astype(BF) for t in tables], axis=0)
    own = tables[0][...]
    mine = dot(own, w1[lat:]).astype(BF)
    low = proj[: lows * TILE]
    high = proj[lows * TILE :]
    if high.shape[0] < low.shape[0]:
        high = jnp.concatenate([high, low[high.shape[0] :]], axis=0)
    rhs = jnp.concatenate(
        [jnp.concatenate([low, mine], axis=0), jnp.concatenate([high, mine], axis=0)], axis=1
    )
    lane = lax.broadcasted_iota(I16, (TILE, TILE), 1)
    lo_t, hi_t, loc_t = lo.T, hi.astype(jnp.int32).T, loc.T
    csub = lax.broadcasted_iota(I16, (crows, TILE), 0)
    w2 = twice(w2_ref[...])
    group = 6 if rows % 6 == 0 else 1
    total = own.astype(F32)
    for g in range(rows // group):
        lhs, upper, back = [], [], []
        for j in range(group):
            col = g * group + j
            o = column(lo_t, col).astype(I16)
            r = column(loc_t, col).astype(I16)
            lhs.append(jnp.concatenate(pick(o, lane, lows) + pick(r, lane, chunks), axis=1))
            upper.append(column(hi_t, col) > 0)
            back.append(one_hot(along_lanes(loc[col : col + 1], crows) == csub))
        out = dot(jnp.concatenate(lhs, axis=0), rhs)
        y = jnp.where(jnp.concatenate(upper, axis=0), out[:, lat:], out[:, :lat])
        msg = pair_dot(half_silu(y), w2).astype(BF)
        total = total + dot(jnp.concatenate(back, axis=1), msg)
    centred = total - jnp.mean(total, axis=1, keepdims=True)
    var = jnp.mean(centred * centred, axis=1, keepdims=True)
    delta = (centred * lax.rsqrt(var + 1e-05) * gain_ref[...]).astype(BF)
    half = (chunks + 1) // 2
    high = delta[half * TILE :]
    if high.shape[0] < half * TILE:
        high = jnp.concatenate([high, delta[high.shape[0] : half * TILE]], axis=0)
    rhs = jnp.concatenate([delta[: half * TILE], high], axis=1)
    cm = cmap_ref[...] - dev * crows
    hi = cm >= half * TILE
    lo_t = jnp.where(hi, cm - half * TILE, cm).T
    hi_t = hi.astype(jnp.int32).T
    tiles = nodes // TILE
    part = 6 if tiles % 6 == 0 else 1
    copies = []
    for p in range(tiles // part):
        hot, upper = [], []
        for t in range(p * part, (p + 1) * part):
            hot.append(jnp.concatenate(pick(column(lo_t, t).astype(I16), lane, half), axis=1))
            upper.append(column(hi_t, t) > 0)
        out = dot(jnp.concatenate(hot, axis=0), rhs)
        back = jnp.where(jnp.concatenate(upper, axis=0), out[:, lat:], out[:, :lat])
        sl = pl.ds(p * part * TILE, part * TILE)
        out_s[sl] = (fine_ref[sl].astype(F32) + back).astype(BF)
        copies.append(pltpu.make_async_copy(out_s.at[sl], out_ref.at[sl], sem.at[p]))
        copies[-1].start()
    for c in copies:
        c.wait()


def on_device(
    node_latent, edge_latent, receivers, senders, coarse_map, coarse_recv, coarse_send,
    edge_w1, mod_u, mod_v, edge_w2, edge_gain, node_w1, node_w2, node_gain,
    coarse_w1, coarse_w2, coarse_gain,
):
    axes = ("dom", "sub")
    size = lax.axis_size(axes)
    dev = lax.axis_index(axes).astype(jnp.int32).reshape(1)
    nodes, lat = node_latent.shape
    edges = edge_latent.shape[0]
    tiles = nodes // TILE
    per = edges // tiles
    crows = nodes // COARSEN
    steps = tiles // STEP
    up = [(i, i + 1) for i in range(size - 1)]
    down = [(j, i) for i, j in up]
    before = lax.ppermute(node_latent[nodes - HALO :], axes, up)
    after = lax.ppermute(node_latent[:HALO], axes, down)
    cmap2 = coarse_map.reshape(tiles, TILE)
    vm = pl.BlockSpec(memory_space=pltpu.VMEM)
    sm = pl.BlockSpec(memory_space=pltpu.SMEM)
    hb = pl.BlockSpec(memory_space=pltpu.HBM)
    hbm = (
        node_latent, senders.reshape(edges // TILE, TILE), receivers.reshape(edges // TILE, TILE),
        cmap2, edge_w1, mod_u.T, mod_v, edge_w2, node_w1, node_w2,
        edge_gain.reshape(1, lat), node_gain.reshape(1, lat),
    )
    big = (STEP * per, lat)
    index = pltpu.VMEM((steps, PAD, TILE), jnp.int32)
    square = pltpu.VMEM((2 * lat, 2 * lat), BF)
    far = pltpu.with_memory_space_constraint(edge_latent, pltpu.HBM)
    edge_out, fine, coarse = pl.pallas_call(
        fine_kernel,
        grid=(steps + 2,),
        in_specs=[
            sm,
            pl.BlockSpec(big, lambda i: (jnp.minimum(i, steps - 1), 0)),
            pl.BlockSpec(big, lambda i: (jnp.clip(i - 1, 0, steps - 1), 0)),
            vm, vm,
        ] + [hb] * len(hbm),
        out_specs=[pl.BlockSpec(big, lambda i: (jnp.clip(i - 1, 0, steps - 1), 0)), vm, vm],
        out_shape=[
            jax.ShapeDtypeStruct((edges, lat), BF),
            jax.ShapeDtypeStruct((nodes, lat), BF),
            jax.ShapeDtypeStruct((crows, lat), BF),
        ],
        scratch_shapes=[pltpu.VMEM(a.shape, a.dtype) for a in hbm] + [
            pltpu.VMEM((nodes + 2 * HALO, lat), BF),
            pltpu.VMEM((nodes, lat), BF),
            square, square, square,
            pltpu.VMEM((2 * lat, lat), BF),
            square, square,
            pltpu.VMEM((steps, TILE, PAD), jnp.int32),
            index,
            pltpu.VMEM(big, BF),
            pltpu.VMEM((STEP * TILE, lat), BF),
            pltpu.VMEM((crows, 2 * lat), F32),
            pltpu.SemaphoreType.DMA((len(hbm),)),
        ],
        compiler_params=pltpu.CompilerParams(
            dimension_semantics=("arbitrary",), vmem_limit_bytes=48 * 2**20
        ),
        name="fine",
    )(dev, far, far, before, after, *[pltpu.with_memory_space_constraint(a, pltpu.HBM) for a in hbm])
    tables = [coarse]
    bit = 1
    while bit < size:
        tables.append(lax.ppermute(coarse, axes, [(i, i ^ bit) for i in range(size)]))
        bit *= 2
    cedges = coarse_send.shape[0]
    node_out = pl.pallas_call(
        coarse_kernel,
        in_specs=[sm] + [vm] * (7 + len(tables)),
        out_specs=hb,
        out_shape=jax.ShapeDtypeStruct((nodes, lat), BF),
        scratch_shapes=[pltpu.VMEM((nodes, lat), BF), pltpu.SemaphoreType.DMA((tiles,))],
        compiler_params=pltpu.CompilerParams(vmem_limit_bytes=48 * 2**20),
        name="coarse",
    )(
        dev, coarse_send.reshape(cedges // TILE, TILE), coarse_recv.reshape(cedges // TILE, TILE),
        cmap2, fine, coarse_w1, coarse_w2, coarse_gain.reshape(1, lat), *tables,
    )
    return (node_out, edge_out)


def solution(mesh):
    split = P(("groups", "dom", "sub"))
    wide = P(("groups", "dom", "sub"), None)
    return jax.shard_map(
        on_device,
        mesh=mesh,
        in_specs=(wide, wide) + (split,) * 5 + (P(),) * 11,
        out_specs=(wide, wide),
        check_vma=False,
    )
```

time: 66 us -> 49.9 us (0.76)
  local copies, waits for them, and re-layouts: 10.7 us -> 0.91 us
  Pallas kernels: 35.2 us -> 28.5 us
  waiting for transfers between devices: 4.62 us -> 5.48 us
    unnamed x33 -> x12, local copies, waits for them, and re-layouts: 9.73 us -> 0.02 us
    pallas_call x1, Pallas kernels: 26.2 us -> 21.5 us  [on_device(): pl.pallas_call(fine_kernel, grid=(steps + 2,), in_specs=[sm, pl.BlockSpec...]
    pallas_call x1, Pallas kernels: 9.05 us -> 6.99 us  [on_device(): pl.pallas_call(coarse_kernel, in_specs=[sm] + [vm] * (7 + len(tables)), o...]
    ppermute x1, waiting for transfers between devices: 0.01 us -> 0.86 us  [on_device(): before = lax.ppermute(node_latent[nodes - HALO:], axes, up)]
  transfers between devices with their start and end apart: 6 -> 6, of which waited for: 3 -> 4; matrix products, arithmetic and copies ran while one was open for 1% -> 0% of each run, Pallas kernels for 0% -> 0%
where the time goes in v2:
time: 49.9 us; the launch traced here: 49.6 us
  Pallas kernels  28.5 us (57%)
  starting transfers between devices  14.1 us (28%)
  waiting for transfers between devices  5.48 us (11%)
  local copies, waits for them, and re-layouts  0.91 us (2%)
  between operations  0.73 us (1%)
    pallas_call x1, Pallas kernels, on_device(): pl.pallas_call(fine_kernel, grid=(steps + 2,), in_specs=[sm, pl.BlockSpec...  21.5 us
    ppermute x4, starting transfers between devices, on_device(): lax.ppermute(coarse, axes, [(i, i ^ bit) for i in range(size)])  9.74 us
    pallas_call x1, Pallas kernels, on_device(): pl.pallas_call(coarse_kernel, in_specs=[sm] + [vm] * (7 + len(tables)), o...  6.99 us
    ppermute x4, waiting for transfers between devices, on_device(): lax.ppermute(coarse, axes, [(i, i ^ bit) for i in range(size)])  4.61 us
    ppermute x1, starting transfers between devices, on_device(): before = lax.ppermute(node_latent[nodes - HALO:], axes, up)  3.03 us
    ppermute x1, starting transfers between devices, on_device(): after = lax.ppermute(node_latent[:HALO], axes, down)  1.29 us
  transfers between devices with their start and end apart: 6, of which 4 were waited for; matrix products, arithmetic and copies ran while one was open for 0% of the time, Pallas kernels for 0%

profile of v2, /device:TPU:0, one launch (start us, length us, event | category | flops | bytes accessed | tf_op | source)
XLA Modules:
  0.0 49.6 jit_solution(14257503190712250407)
XLA Ops:
  0.6 0.9 %fusion = (bf16[256,128]{1,0:T(8,128)(2,1)S(1)}, bf16[256,128]{1,0:T(8,128)(2,1)S(1)}) fusion(bf16[3072,128]{1,0:T(8,128)(2,1)} %refs_0_.1), kind=kLoop, calls=%fused_computation | loop fusion | bytes 262144 | tf_op jit(solution)/shard_map/slice | solution.py:331
  1.5 1.3 %collective-permute-start.1 = (bf16[256,128]{1,0:T(8,128)(2,1)S(1)}, bf16[256,128]{1,0:T(8,128)(2,1)S(1)}, u32[]{:S(2)}, u32[]{:S(2)}) collective-permute-start(bf16[256,128]{1,0:T(8,128)(2,1)S(1)} %get-tuple-element.8), channel_id=1, source_target_pairs={{1,0},{2,1},{3,2},{4,3},{5,4},{6,5},{7,6},{8,7},{9,8},{10,9},{11,1... | collective-permute-start | bytes 196616 | tf_op jit(solution)/shard_map/ppermute | solution.py:331
  2.8 3.0 %collective-permute-start = (bf16[256,128]{1,0:T(8,128)(2,1)S(1)}, bf16[256,128]{1,0:T(8,128)(2,1)S(1)}, u32[]{:S(2)}, u32[]{:S(2)}) collective-permute-start(bf16[256,128]{1,0:T(8,128)(2,1)S(1)} %get-tuple-element.9), channel_id=1, source_target_pairs={{0,1},{1,2},{2,3},{3,4},{4,5},{5,6},{6,7},{7,8},{8,9},{9,10},{10,1... | collective-permute-start | bytes 196616 | tf_op jit(solution)/shard_map/ppermute | solution.py:330
  5.9 0.0 collective-permute-done.1.after_ref
  5.9 0.9 %collective-permute-done.before_ref = bf16[256,128]{1,0:T(8,128)(2,1)S(1)} collective-permute-done((bf16[256,128]{1,0:T(8,128)(2,1)S(1)}, bf16[256,128]{1,0:T(8,128)(2,1)S(1)}, u32[]{:S(2)}, u32[]{:S(2)}) %collective-permute-start) | collective-permute-done | bytes 65568 | tf_op jit(solution)/shard_map/ppermute | solution.py:330
  6.7 0.0 copy-start
  6.7 0.0 copy-start.1
  6.7 0.0 copy-start.2
  6.7 0.0 copy-start.3
  6.7 0.0 copy-start.4
  6.8 0.0 copy-start.5
  6.8 21.5 %fine.1 = (bf16[18432,128]{1,0:T(8,128)(2,1)}, bf16[3072,128]{1,0:T(8,128)(2,1)S(1)}, bf16[384,128]{1,0:T(8,128)(2,1)S(1)}) custom-call(s32[1]{0:T(128)} %bitcast.base_ref, bf16[18432,128]{1,0:T(8,128)(2,1)} %last_ref.1, bf16[18432,128]{1,0:T(8,128)(2,1)} %last_ref.1, bf16[256,128]{1,0:T(8,128)(2,1)S(1)} %collective-permute-done.before_ref, ...), custom_call_target="tpu_custom_call" | custom-call | tf_op jit(solution)/shard_map/fine/pallas_call | solution.py:345
  28.2 8.1 %collective-permute-start.5 = (bf16[384,128]{1,0:T(8,128)(2,1)S(1)}, bf16[384,128]{1,0:T(8,128)(2,1)S(1)}, u32[]{:S(2)}, u32[]{:S(2)}) collective-permute-start(bf16[384,128]{1,0:T(8,128)(2,1)S(1)} %get-tuple-element.6.refs_0_), channel_id=1, source_target_pairs={{0,8},{1,9},{2,10},{3,11},{4,12},{5,13},{6,14},{7,15},{8,0},{9,1},... | collective-permute-start | bytes 294920 | tf_op jit(solution)/shard_map/ppermute | solution.py:381
  36.4 1.6 %collective-permute-start.4 = (bf16[384,128]{1,0:T(8,128)(2,1)S(1)}, bf16[384,128]{1,0:T(8,128)(2,1)S(1)}, u32[]{:S(2)}, u32[]{:S(2)}) collective-permute-start(bf16[384,128]{1,0:T(8,128)(2,1)S(1)} %get-tuple-element.6.refs_0_), channel_id=1, source_target_pairs={{0,4},{1,5},{2,6},{3,7},{4,0},{5,1},{6,2},{7,3},{8,12},{9,13},{10,... | collective-permute-start | bytes 294920 | tf_op jit(solution)/shard_map/ppermute | solution.py:381
  38.0 0.0 collective-permute-start.3
  38.0 0.0 collective-permute-start.2
  38.0 1.0 %collective-permute-done.5.refs_4_ = bf16[384,128]{1,0:T(8,128)(2,1)S(1)} collective-permute-done((bf16[384,128]{1,0:T(8,128)(2,1)S(1)}, bf16[384,128]{1,0:T(8,128)(2,1)S(1)}, u32[]{:S(2)}, u32[]{:S(2)}) %collective-permute-start.5) | collective-permute-done | bytes 98336 | tf_op jit(solution)/shard_map/ppermute | solution.py:381
  39.0 2.0 %collective-permute-done.4.refs_3_ = bf16[384,128]{1,0:T(8,128)(2,1)S(1)} collective-permute-done((bf16[384,128]{1,0:T(8,128)(2,1)S(1)}, bf16[384,128]{1,0:T(8,128)(2,1)S(1)}, u32[]{:S(2)}, u32[]{:S(2)}) %collective-permute-start.4) | collective-permute-done | bytes 98336 | tf_op jit(solution)/shard_map/ppermute | solution.py:381
  41.0 1.6 %collective-permute-done.3.refs_2_ = bf16[384,128]{1,0:T(8,128)(2,1)S(1)} collective-permute-done((bf16[384,128]{1,0:T(8,128)(2,1)S(1)}, bf16[384,128]{1,0:T(8,128)(2,1)S(1)}, u32[]{:S(2)}, u32[]{:S(2)}) %collective-permute-start.3) | collective-permute-done | bytes 98336 | tf_op jit(solution)/shard_map/ppermute | solution.py:381
  42.6 0.0 collective-permute-done.2.refs_1_
  42.6 0.0 copy-done
  42.6 0.0 copy-done.1
  42.6 0.0 copy-done.2
  42.6 0.0 copy-done.3
  42.6 0.0 copy-done.4
  42.6 0.0 copy-done.5
  42.6 7.0 %coarse.1 = bf16[3072,128]{1,0:T(8,128)(2,1)} custom-call(s32[1]{0:T(128)} %bitcast.base_ref, s32[18,128]{1,0:T(8,128)S(1)} %bitcast.12, s32[18,128]{1,0:T(8,128)S(1)} %bitcast.13, s32[24,128]{1,0:T(8,128)S(1)} %bitcast.11, bf16[3072,128]{1,0:T(8,128)(2,1)S(1)} %get-tuple-element.5.fine_ref, bf16[256,128]{1,0:T(8,128)(2,1)S(1)} %copy-done, ...), custom_call_target="tpu_custom_call" | custom-call | tf_op jit(solution)/shard_map/coarse/pallas_call | solution.py:384
Async XLA Ops:
  1.5 4.4 %collective-permute-start.1 = (bf16[256,128]{1,0:T(8,128)(2,1)S(1)}, bf16[256,128]{1,0:T(8,128)(2,1)S(1)}, u32[]{:S(2)}, u32[]{:S(2)}) collective-permute-start(bf16[256,128]{1,0:T(8,128)(2,1)S(1)} %get-tuple-element.8), channel_id=1, source_target_pairs={{1,0},{2,1},{3,2},{4,3},{5,4},{6,5},{7,6},{8,7},{9,8},{10,9},{11,1... | collective-permute-start | bytes 196616 | tf_op jit(solution)/shard_map/ppermute | solution.py:331
  2.8 3.9 %collective-permute-start = (bf16[256,128]{1,0:T(8,128)(2,1)S(1)}, bf16[256,128]{1,0:T(8,128)(2,1)S(1)}, u32[]{:S(2)}, u32[]{:S(2)}) collective-permute-start(bf16[256,128]{1,0:T(8,128)(2,1)S(1)} %get-tuple-element.9), channel_id=1, source_target_pairs={{0,1},{1,2},{2,3},{3,4},{4,5},{5,6},{6,7},{7,8},{8,9},{9,10},{10,1... | collective-permute-start | bytes 196616 | tf_op jit(solution)/shard_map/ppermute | solution.py:330
  6.7 35.9 %copy-start = (bf16[256,128]{1,0:T(8,128)(2,1)S(1)}, bf16[256,128]{1,0:T(8,128)(2,1)}, u32[]{:S(2)}) copy-start(bf16[256,128]{1,0:T(8,128)(2,1)} %w1_ref.1) | copy-start | bytes 196612
  6.7 35.9 %copy-start.1 = (s32[3072]{0:T(1024)S(1)}, s32[3072]{0:T(1024)}, u32[]{:S(2)}) copy-start(s32[3072]{0:T(1024)} %param.22) | copy-start | bytes 36868
  6.7 35.9 %copy-start.2 = (bf16[128,128]{1,0:T(8,128)(2,1)S(1)}, bf16[128,128]{1,0:T(8,128)(2,1)}, u32[]{:S(2)}) copy-start(bf16[128,128]{1,0:T(8,128)(2,1)} %w2_ref.1) | copy-start | bytes 98308
  6.7 35.9 %copy-start.3 = (s32[2304]{0:T(1024)S(1)}, s32[2304]{0:T(1024)}, u32[]{:S(2)}) copy-start(s32[2304]{0:T(1024)} %param.24) | copy-start | bytes 27652
  6.7 35.9 %copy-start.4 = (s32[2304]{0:T(1024)S(1)}, s32[2304]{0:T(1024)}, u32[]{:S(2)}) copy-start(s32[2304]{0:T(1024)} %param.23) | copy-start | bytes 27652
  6.8 35.9 %copy-start.5 = (f32[128]{0:T(128)S(1)}, f32[128]{0:T(128)}, u32[]{:S(2)}) copy-start(f32[128]{0:T(128)} %param.35) | copy-start | bytes 1540
  28.2 10.7 %collective-permute-start.5 = (bf16[384,128]{1,0:T(8,128)(2,1)S(1)}, bf16[384,128]{1,0:T(8,128)(2,1)S(1)}, u32[]{:S(2)}, u32[]{:S(2)}) collective-permute-start(bf16[384,128]{1,0:T(8,128)(2,1)S(1)} %get-tuple-element.6.refs_0_), channel_id=1, source_target_pairs={{0,8},{1,9},{2,10},{3,11},{4,12},{5,13},{6,14},{7,15},{8,0},{9,1},... | collective-permute-start | bytes 294920 | tf_op jit(solution)/shard_map/ppermute | solution.py:381
  36.4 4.6 %collective-permute-start.4 = (bf16[384,128]{1,0:T(8,128)(2,1)S(1)}, bf16[384,128]{1,0:T(8,128)(2,1)S(1)}, u32[]{:S(2)}, u32[]{:S(2)}) collective-permute-start(bf16[384,128]{1,0:T(8,128)(2,1)S(1)} %get-tuple-element.6.refs_0_), channel_id=1, source_target_pairs={{0,4},{1,5},{2,6},{3,7},{4,0},{5,1},{6,2},{7,3},{8,12},{9,13},{10,... | collective-permute-start | bytes 294920 | tf_op jit(solution)/shard_map/ppermute | solution.py:381
  38.0 4.6 %collective-permute-start.3 = (bf16[384,128]{1,0:T(8,128)(2,1)S(1)}, bf16[384,128]{1,0:T(8,128)(2,1)S(1)}, u32[]{:S(2)}, u32[]{:S(2)}) collective-permute-start(bf16[384,128]{1,0:T(8,128)(2,1)S(1)} %get-tuple-element.6.refs_0_), channel_id=1, source_target_pairs={{0,2},{1,3},{2,0},{3,1},{4,6},{5,7},{6,4},{7,5},{8,10},{9,11},{10,... | collective-permute-start | bytes 294920 | tf_op jit(solution)/shard_map/ppermute | solution.py:381
  38.0 4.6 %collective-permute-start.2 = (bf16[384,128]{1,0:T(8,128)(2,1)S(1)}, bf16[384,128]{1,0:T(8,128)(2,1)S(1)}, u32[]{:S(2)}, u32[]{:S(2)}) collective-permute-start(bf16[384,128]{1,0:T(8,128)(2,1)S(1)} %get-tuple-element.6.refs_0_), channel_id=1, source_target_pairs={{0,1},{1,0},{2,3},{3,2},{4,5},{5,4},{6,7},{7,6},{8,9},{9,8},{10,11... | collective-permute-start | bytes 294920 | tf_op jit(solution)/shard_map/ppermute | solution.py:381

commit v3 on v2

--- a/solution.py
+++ b/solution.py
@@ -69,6 +69,21 @@
 
 def half_silu(y):
     return (y * jnp.tanh(y) + y).astype(BF)
+
+
+def interleave(queue, active):
+    queue = list(queue)
+    while active or queue:
+        if queue:
+            active = list(queue.pop(0)) + active
+        alive = []
+        for part in active:
+            try:
+                next(part)
+                alive.append(part)
+            except StopIteration:
+                pass
+        active = alive
 
 
 def fine_kernel(base_ref, edge_ref, last_ref, before_ref, after_ref, *refs):
@@ -199,20 +214,11 @@
     def stages(one, two, three):
         for k in range(STEP):
             incoming[k].clear()
-        active = [third()] if three else []
         todo = [(k, q) for k in range(STEP) for q in range(PARTS)] if one or two else []
-        while active or todo:
-            if todo:
-                k, q = todo.pop(0)
-                active = [second(k, q)] * two + [first(k, q)] * one + active
-            alive = []
-            for g in active:
-                try:
-                    next(g)
-                    alive.append(g)
-                except StopIteration:
-                    pass
-            active = alive
+        interleave(
+            [[second(k, q)] * two + [first(k, q)] * one for k, q in todo],
+            [third()] if three else [],
+        )
 
     full = (step >= 2) & (step < steps)
     for when, which in (
@@ -230,12 +236,39 @@
         coarse_ref[...] = (total[:, :lat] / jnp.maximum(total[:, lat:], 1.0)).astype(BF)
 
 
+def near_kernel(base_ref, send_ref, recv_ref, own_ref, w1_ref, pre_ref):
+    crows, lat = own_ref.shape
+    rows = send_ref.shape[0]
+    first = base_ref[0] * crows
+    blocks = crows // TILE
+    send = send_ref[...] - first
+    mine = (send >= 0) & (send < crows)
+    code_t = (jnp.where(mine, send, crows) | ((recv_ref[...] - first) << 16)).T
+    w1 = w1_ref[...] * 0.5
+    rhs = dot(own_ref[...], jnp.concatenate([w1[:lat], w1[lat:]], axis=1)).astype(BF)
+    rhs = jnp.concatenate([rhs[:, :lat], rhs[:, lat:]], axis=0)
+    lane = lax.broadcasted_iota(I16, (TILE, TILE), 1)
+    group = 3 if rows % 3 == 0 else 1
+
+    def part(g):
+        lhs = []
+        for col in range(g, g + group):
+            word = column(code_t, col)
+            o, r = word.astype(I16), (word >> 16).astype(I16)
+            lhs.append(jnp.concatenate(pick(o, lane, blocks) + pick(r, lane, blocks), axis=1))
+        out = dot(jnp.concatenate(lhs, axis=0), rhs)
+        yield
+        pre_ref[g * TILE : (g + group) * TILE] = out
+
+    interleave([[part(g)] for g in range(0, rows, group)], [])
+
+
 def coarse_kernel(
-    base_ref, send_ref, recv_ref, cmap_ref, fine_ref, w1_ref, w2_ref, gain_ref, *refs
+    base_ref, send_ref, recv_ref, cmap_ref, fine_ref, pre_ref, w1_ref, w2_ref, gain_ref, *refs
 ):
-    tables, (out_ref, out_s, sem) = refs[:-3], refs[-3:]
+    (own_ref, *tables), (out_ref, out_s, sem) = refs[:-3], refs[-3:]
     dev = base_ref[0]
-    crows, lat = tables[0].shape
+    crows, lat = own_ref.shape
     rows = send_ref.shape[0]
     nodes = fine_ref.shape[0]
     chunks = crows // TILE
@@ -244,43 +277,45 @@
     send = send_ref[...]
     owner = lax.div(send, jnp.full_like(send, crows))
     other = owner ^ dev
-    slot = jnp.zeros_like(send)
-    for j in range(len(tables) - 1):
-        slot = jnp.where(other == (1 << j), j + 1, slot)
+    slot = jnp.full_like(send, -1)
+    for j in range(len(tables)):
+        slot = jnp.where(other == (1 << j), j, slot)
     off = send - owner * crows + slot * crows
     hi = off >= lows * TILE
     lo = jnp.where(hi, off - lows * TILE, off)
+    code_t = jnp.where(
+        slot < 0, lows * TILE, lo | jnp.where(hi, jnp.int32(-(2**31)), 0)
+    ).T
     loc = recv_ref[...] - dev * crows
-    w1 = w1_ref[...] * 0.5
-    proj = jnp.concatenate([dot(t[...], w1[:lat]).astype(BF) for t in tables], axis=0)
-    own = tables[0][...]
-    mine = dot(own, w1[lat:]).astype(BF)
-    low = proj[: lows * TILE]
-    high = proj[lows * TILE :]
+    w1 = twice(w1_ref[:lat] * 0.5)
+    proj = jnp.concatenate([pair_dot(t[...], w1).astype(BF) for t in tables], axis=0)
+    low, high = proj[: lows * TILE], proj[lows * TILE :]
     if high.shape[0] < low.shape[0]:
         high = jnp.concatenate([high, low[high.shape[0] :]], axis=0)
-    rhs = jnp.concatenate(
-        [jnp.concatenate([low, mine], axis=0), jnp.concatenate([high, mine], axis=0)], axis=1
-    )
+    rhs = jnp.concatenate([low, high], axis=1)
     lane = lax.broadcasted_iota(I16, (TILE, TILE), 1)
-    lo_t, hi_t, loc_t = lo.T, hi.astype(jnp.int32).T, loc.T
     csub = lax.broadcasted_iota(I16, (crows, TILE), 0)
     w2 = twice(w2_ref[...])
-    group = 6 if rows % 6 == 0 else 1
-    total = own.astype(F32)
-    for g in range(rows // group):
-        lhs, upper, back = [], [], []
-        for j in range(group):
-            col = g * group + j
-            o = column(lo_t, col).astype(I16)
-            r = column(loc_t, col).astype(I16)
-            lhs.append(jnp.concatenate(pick(o, lane, lows) + pick(r, lane, chunks), axis=1))
-            upper.append(column(hi_t, col) > 0)
-            back.append(one_hot(along_lanes(loc[col : col + 1], crows) == csub))
+    group = 2 if rows % 2 == 0 else 1
+    total = [own_ref[...].astype(F32)]
+
+    def part(g):
+        lhs, upper = [], []
+        for col in range(g, g + group):
+            word = column(code_t, col)
+            lhs.append(jnp.concatenate(pick(word.astype(I16), lane, lows), axis=1))
+            upper.append(word < 0)
         out = dot(jnp.concatenate(lhs, axis=0), rhs)
+        yield
         y = jnp.where(jnp.concatenate(upper, axis=0), out[:, lat:], out[:, :lat])
-        msg = pair_dot(half_silu(y), w2).astype(BF)
-        total = total + dot(jnp.concatenate(back, axis=1), msg)
+        y = half_silu(y + pre_ref[g * TILE : (g + group) * TILE])
+        msg = pair_dot(y, w2)
+        yield
+        back = [one_hot(along_lanes(loc[col : col + 1], crows) == csub) for col in range(g, g + group)]
+        total[0] = total[0] + dot(jnp.concatenate(back, axis=1), msg.astype(BF))
+
+    interleave([[part(g)] for g in range(0, rows, group)], [])
+    total = total[0]
     centred = total - jnp.mean(total, axis=1, keepdims=True)
     var = jnp.mean(centred * centred, axis=1, keepdims=True)
     delta = (centred * lax.rsqrt(var + 1e-05) * gain_ref[...]).astype(BF)
@@ -291,22 +326,26 @@
     rhs = jnp.concatenate([delta[: half * TILE], high], axis=1)
     cm = cmap_ref[...] - dev * crows
     hi = cm >= half * TILE
-    lo_t = jnp.where(hi, cm - half * TILE, cm).T
-    hi_t = hi.astype(jnp.int32).T
+    cm_t = (jnp.where(hi, cm - half * TILE, cm) | jnp.where(hi, jnp.int32(-(2**31)), 0)).T
     tiles = nodes // TILE
-    part = 6 if tiles % 6 == 0 else 1
+    size = 4 if tiles % 4 == 0 else 1
     copies = []
-    for p in range(tiles // part):
+
+    def spread(p):
         hot, upper = [], []
-        for t in range(p * part, (p + 1) * part):
-            hot.append(jnp.concatenate(pick(column(lo_t, t).astype(I16), lane, half), axis=1))
-            upper.append(column(hi_t, t) > 0)
+        for t in range(p, p + size):
+            word = column(cm_t, t)
+            hot.append(jnp.concatenate(pick(word.astype(I16), lane, half), axis=1))
+            upper.append(word < 0)
         out = dot(jnp.concatenate(hot, axis=0), rhs)
+        yield
         back = jnp.where(jnp.concatenate(upper, axis=0), out[:, lat:], out[:, :lat])
-        sl = pl.ds(p * part * TILE, part * TILE)
+        sl = pl.ds(p * TILE, size * TILE)
         out_s[sl] = (fine_ref[sl].astype(F32) + back).astype(BF)
         copies.append(pltpu.make_async_copy(out_s.at[sl], out_ref.at[sl], sem.at[p]))
         copies[-1].start()
+
+    interleave([[spread(p)] for p in range(0, tiles, size)], [])
     for c in copies:
         c.wait()
 
@@ -381,17 +420,27 @@
         tables.append(lax.ppermute(coarse, axes, [(i, i ^ bit) for i in range(size)]))
         bit *= 2
     cedges = coarse_send.shape[0]
+    csend2 = coarse_send.reshape(cedges // TILE, TILE)
+    crecv2 = coarse_recv.reshape(cedges // TILE, TILE)
+    pre = pl.pallas_call(
+        near_kernel,
+        in_specs=[sm] + [vm] * 4,
+        out_specs=vm,
+        out_shape=jax.ShapeDtypeStruct((cedges, lat), F32),
+        compiler_params=pltpu.CompilerParams(vmem_limit_bytes=32 * 2**20),
+        name="near",
+    )(dev, csend2, crecv2, coarse, coarse_w1)
     node_out = pl.pallas_call(
         coarse_kernel,
-        in_specs=[sm] + [vm] * (7 + len(tables)),
+        in_specs=[sm] + [vm] * (8 + len(tables)),
         out_specs=hb,
         out_shape=jax.ShapeDtypeStruct((nodes, lat), BF),
         scratch_shapes=[pltpu.VMEM((nodes, lat), BF), pltpu.SemaphoreType.DMA((tiles,))],
-        compiler_params=pltpu.CompilerParams(vmem_limit_bytes=48 * 2**20),
+        compiler_params=pltpu.CompilerParams(vmem_limit_bytes=32 * 2**20),
         name="coarse",
     )(
-        dev, coarse_send.reshape(cedges // TILE, TILE), coarse_recv.reshape(cedges // TILE, TILE),
-        cmap2, fine, coarse_w1, coarse_w2, coarse_gain.reshape(1, lat), *tables,
+        dev, csend2, crecv2, cmap2, fine, pre, coarse_w1, coarse_w2, coarse_gain.reshape(1, lat),
+        *tables,
     )
     return (node_out, edge_out)
 

time: 49.9 us -> 47.2 us (0.946)
  Pallas kernels: 28.5 us -> 27.1 us
  waiting for transfers between devices: 5.48 us -> 4.14 us
    pallas_call x1 -> x2, Pallas kernels: 6.99 us -> 5.62 us  [the longest x1 4.32 us: on_device(): pl.pallas_call(coarse_kernel, in_specs=[sm] + [vm] * (8 + len(tables)), o...]
    ppermute x4, waiting for transfers between devices: 4.61 us -> 3.27 us  [on_device(): lax.ppermute(coarse, axes, [(i, i ^ bit) for i in range(size)])]
  transfers between devices with their start and end apart: 6 -> 6, of which waited for: 4 -> 3; matrix products, arithmetic and copies ran while one was open for 0% -> 0% of each run, Pallas kernels for 0% -> 3%
where the time goes in v3:
time: 47.2 us; the launch traced here: 46.9 us
  Pallas kernels  27.1 us (57%)
  starting transfers between devices  14.1 us (30%)
  waiting for transfers between devices  4.14 us (9%)
  local copies, waits for them, and re-layouts  0.91 us (2%)
  between operations  0.74 us (2%)
    pallas_call x1, Pallas kernels, on_device(): pl.pallas_call(fine_kernel, grid=(steps + 2,), in_specs=[sm, pl.BlockSpec...  21.5 us
    ppermute x4, starting transfers between devices, on_device(): lax.ppermute(coarse, axes, [(i, i ^ bit) for i in range(size)])  9.74 us
    pallas_call x1, Pallas kernels, on_device(): pl.pallas_call(coarse_kernel, in_specs=[sm] + [vm] * (8 + len(tables)), o...  4.32 us
    ppermute x4, waiting for transfers between devices, on_device(): lax.ppermute(coarse, axes, [(i, i ^ bit) for i in range(size)])  3.27 us
    ppermute x1, starting transfers between devices, on_device(): before = lax.ppermute(node_latent[nodes - HALO:], axes, up)  3.03 us
    pallas_call x1, Pallas kernels, on_device(): pl.pallas_call(near_kernel, in_specs=[sm] + [vm] * 4, out_specs=vm, out_s...  1.3 us
    ppermute x1, starting transfers between devices, on_device(): after = lax.ppermute(node_latent[:HALO], axes, down)  1.29 us
  transfers between devices with their start and end apart: 6, of which 3 were waited for; matrix products, arithmetic and copies ran while one was open for 0% of the time, Pallas kernels for 3%

profile of v3, /device:TPU:0, one launch (start us, length us, event | category | flops | bytes accessed | tf_op | source)
XLA Modules:
  0.0 46.9 jit_solution(9144144102831748752)
XLA Ops:
  0.6 0.9 %fusion = (bf16[256,128]{1,0:T(8,128)(2,1)S(1)}, bf16[256,128]{1,0:T(8,128)(2,1)S(1)}) fusion(bf16[3072,128]{1,0:T(8,128)(2,1)} %refs_0_.1), kind=kLoop, calls=%fused_computation | loop fusion | bytes 262144 | tf_op jit(solution)/shard_map/slice | solution.py:370
  1.5 1.3 %collective-permute-start.1 = (bf16[256,128]{1,0:T(8,128)(2,1)S(1)}, bf16[256,128]{1,0:T(8,128)(2,1)S(1)}, u32[]{:S(2)}, u32[]{:S(2)}) collective-permute-start(bf16[256,128]{1,0:T(8,128)(2,1)S(1)} %get-tuple-element.8), channel_id=1, source_target_pairs={{1,0},{2,1},{3,2},{4,3},{5,4},{6,5},{7,6},{8,7},{9,8},{10,9},{11,1... | collective-permute-start | bytes 196616 | tf_op jit(solution)/shard_map/ppermute | solution.py:370
  2.8 3.0 %collective-permute-start = (bf16[256,128]{1,0:T(8,128)(2,1)S(1)}, bf16[256,128]{1,0:T(8,128)(2,1)S(1)}, u32[]{:S(2)}, u32[]{:S(2)}) collective-permute-start(bf16[256,128]{1,0:T(8,128)(2,1)S(1)} %get-tuple-element.9), channel_id=1, source_target_pairs={{0,1},{1,2},{2,3},{3,4},{4,5},{5,6},{6,7},{7,8},{8,9},{9,10},{10,1... | collective-permute-start | bytes 196616 | tf_op jit(solution)/shard_map/ppermute | solution.py:369
  5.9 0.0 collective-permute-done.1.after_ref
  5.9 0.9 %collective-permute-done.before_ref = bf16[256,128]{1,0:T(8,128)(2,1)S(1)} collective-permute-done((bf16[256,128]{1,0:T(8,128)(2,1)S(1)}, bf16[256,128]{1,0:T(8,128)(2,1)S(1)}, u32[]{:S(2)}, u32[]{:S(2)}) %collective-permute-start) | collective-permute-done | bytes 65568 | tf_op jit(solution)/shard_map/ppermute | solution.py:369
  6.7 0.0 copy-start
  6.7 0.0 copy-start.1
  6.7 0.0 copy-start.2
  6.7 0.0 copy-start.3
  6.7 0.0 copy-start.4
  6.8 0.0 copy-start.5
  6.8 21.5 %fine.1 = (bf16[18432,128]{1,0:T(8,128)(2,1)}, bf16[3072,128]{1,0:T(8,128)(2,1)S(1)}, bf16[384,128]{1,0:T(8,128)(2,1)S(1)}) custom-call(s32[1]{0:T(128)} %bitcast.base_ref, bf16[18432,128]{1,0:T(8,128)(2,1)} %last_ref.1, bf16[18432,128]{1,0:T(8,128)(2,1)} %last_ref.1, bf16[256,128]{1,0:T(8,128)(2,1)S(1)} %collective-permute-done.before_ref, ...), custom_call_target="tpu_custom_call" | custom-call | tf_op jit(solution)/shard_map/fine/pallas_call | solution.py:384
  28.3 8.1 %collective-permute-start.5 = (bf16[384,128]{1,0:T(8,128)(2,1)S(1)}, bf16[384,128]{1,0:T(8,128)(2,1)S(1)}, u32[]{:S(2)}, u32[]{:S(2)}) collective-permute-start(bf16[384,128]{1,0:T(8,128)(2,1)S(1)} %get-tuple-element.6.own_ref.refs_0_), channel_id=1, source_target_pairs={{0,8},{1,9},{2,10},{3,11},{4,12},{5,13},{6,14},{7,15},{8,0},{9,1},... | collective-permute-start | bytes 294920 | tf_op jit(solution)/shard_map/ppermute | solution.py:420
  36.4 1.6 %collective-permute-start.4 = (bf16[384,128]{1,0:T(8,128)(2,1)S(1)}, bf16[384,128]{1,0:T(8,128)(2,1)S(1)}, u32[]{:S(2)}, u32[]{:S(2)}) collective-permute-start(bf16[384,128]{1,0:T(8,128)(2,1)S(1)} %get-tuple-element.6.own_ref.refs_0_), channel_id=1, source_target_pairs={{0,4},{1,5},{2,6},{3,7},{4,0},{5,1},{6,2},{7,3},{8,12},{9,13},{10,... | collective-permute-start | bytes 294920 | tf_op jit(solution)/shard_map/ppermute | solution.py:420
  38.0 0.0 collective-permute-start.3
  38.0 0.0 collective-permute-start.2
  38.0 0.0 copy-done
  38.0 0.0 copy-done.1
  38.0 0.0 copy-done.2
  38.0 1.3 %near.1.pre_ref = f32[2304,128]{1,0:T(8,128)S(1)} custom-call(s32[1]{0:T(128)} %bitcast.base_ref, s32[18,128]{1,0:T(8,128)S(1)} %bitcast.10, s32[18,128]{1,0:T(8,128)S(1)} %bitcast.12, bf16[384,128]{1,0:T(8,128)(2,1)S(1)} %get-tuple-element.6.own_ref.refs_0_, bf16[256,128]{1,0:T(8,128)(2,1)S(1)} %copy-done), custom_call_target="tpu_custom_call" | custom-call | tf_op jit(solution)/shard_map/near/pallas_call | solution.py:425
  39.3 0.0 collective-permute-done.5.refs_4_
  39.3 1.7 %collective-permute-done.4.refs_3_ = bf16[384,128]{1,0:T(8,128)(2,1)S(1)} collective-permute-done((bf16[384,128]{1,0:T(8,128)(2,1)S(1)}, bf16[384,128]{1,0:T(8,128)(2,1)S(1)}, u32[]{:S(2)}, u32[]{:S(2)}) %collective-permute-start.4) | collective-permute-done | bytes 98336 | tf_op jit(solution)/shard_map/ppermute | solution.py:420
  41.0 1.6 %collective-permute-done.3.refs_2_ = bf16[384,128]{1,0:T(8,128)(2,1)S(1)} collective-permute-done((bf16[384,128]{1,0:T(8,128)(2,1)S(1)}, bf16[384,128]{1,0:T(8,128)(2,1)S(1)}, u32[]{:S(2)}, u32[]{:S(2)}) %collective-permute-start.3) | collective-permute-done | bytes 98336 | tf_op jit(solution)/shard_map/ppermute | solution.py:420
  42.6 0.0 collective-permute-done.2.refs_1_
  42.6 0.0 copy-done.3
  42.6 0.0 copy-done.4
  42.6 0.0 copy-done.5
  42.6 4.3 %coarse.1 = bf16[3072,128]{1,0:T(8,128)(2,1)} custom-call(s32[1]{0:T(128)} %bitcast.base_ref, s32[18,128]{1,0:T(8,128)S(1)} %bitcast.11, s32[18,128]{1,0:T(8,128)S(1)} %bitcast.13, s32[24,128]{1,0:T(8,128)S(1)} %bitcast.15, bf16[3072,128]{1,0:T(8,128)(2,1)S(1)} %get-tuple-element.5.fine_ref, f32[2304,128]{1,0:T(8,128)S(1)} %near.1.pre_ref, ...), custom_call_target="tpu_custom_call" | custom-call | tf_op jit(solution)/shard_map/coarse/pallas_call | solution.py:433
Async XLA Ops:
  1.5 4.4 %collective-permute-start.1 = (bf16[256,128]{1,0:T(8,128)(2,1)S(1)}, bf16[256,128]{1,0:T(8,128)(2,1)S(1)}, u32[]{:S(2)}, u32[]{:S(2)}) collective-permute-start(bf16[256,128]{1,0:T(8,128)(2,1)S(1)} %get-tuple-element.8), channel_id=1, source_target_pairs={{1,0},{2,1},{3,2},{4,3},{5,4},{6,5},{7,6},{8,7},{9,8},{10,9},{11,1... | collective-permute-start | bytes 196616 | tf_op jit(solution)/shard_map/ppermute | solution.py:370
  2.8 3.9 %collective-permute-start = (bf16[256,128]{1,0:T(8,128)(2,1)S(1)}, bf16[256,128]{1,0:T(8,128)(2,1)S(1)}, u32[]{:S(2)}, u32[]{:S(2)}) collective-permute-start(bf16[256,128]{1,0:T(8,128)(2,1)S(1)} %get-tuple-element.9), channel_id=1, source_target_pairs={{0,1},{1,2},{2,3},{3,4},{4,5},{5,6},{6,7},{7,8},{8,9},{9,10},{10,1... | collective-permute-start | bytes 196616 | tf_op jit(solution)/shard_map/ppermute | solution.py:369
  6.7 31.3 %copy-start = (bf16[256,128]{1,0:T(8,128)(2,1)S(1)}, bf16[256,128]{1,0:T(8,128)(2,1)}, u32[]{:S(2)}) copy-start(bf16[256,128]{1,0:T(8,128)(2,1)} %w1_ref.3) | copy-start | bytes 196612
  6.7 31.3 %copy-start.1 = (s32[2304]{0:T(1024)S(1)}, s32[2304]{0:T(1024)}, u32[]{:S(2)}) copy-start(s32[2304]{0:T(1024)} %param.24) | copy-start | bytes 27652
  6.7 31.3 %copy-start.2 = (s32[2304]{0:T(1024)S(1)}, s32[2304]{0:T(1024)}, u32[]{:S(2)}) copy-start(s32[2304]{0:T(1024)} %param.23) | copy-start | bytes 27652
  6.7 35.9 %copy-start.3 = (s32[3072]{0:T(1024)S(1)}, s32[3072]{0:T(1024)}, u32[]{:S(2)}) copy-start(s32[3072]{0:T(1024)} %param.22) | copy-start | bytes 36868
  6.7 35.9 %copy-start.4 = (bf16[128,128]{1,0:T(8,128)(2,1)S(1)}, bf16[128,128]{1,0:T(8,128)(2,1)}, u32[]{:S(2)}) copy-start(bf16[128,128]{1,0:T(8,128)(2,1)} %w2_ref.1) | copy-start | bytes 98308
  6.8 35.9 %copy-start.5 = (f32[128]{0:T(128)S(1)}, f32[128]{0:T(128)}, u32[]{:S(2)}) copy-start(f32[128]{0:T(128)} %param.35) | copy-start | bytes 1540
  28.3 11.1 %collective-permute-start.5 = (bf16[384,128]{1,0:T(8,128)(2,1)S(1)}, bf16[384,128]{1,0:T(8,128)(2,1)S(1)}, u32[]{:S(2)}, u32[]{:S(2)}) collective-permute-start(bf16[384,128]{1,0:T(8,128)(2,1)S(1)} %get-tuple-element.6.own_ref.refs_0_), channel_id=1, source_target_pairs={{0,8},{1,9},{2,10},{3,11},{4,12},{5,13},{6,14},{7,15},{8,0},{9,1},... | collective-permute-start | bytes 294920 | tf_op jit(solution)/shard_map/ppermute | solution.py:420
  36.4 4.6 %collective-permute-start.4 = (bf16[384,128]{1,0:T(8,128)(2,1)S(1)}, bf16[384,128]{1,0:T(8,128)(2,1)S(1)}, u32[]{:S(2)}, u32[]{:S(2)}) collective-permute-start(bf16[384,128]{1,0:T(8,128)(2,1)S(1)} %get-tuple-element.6.own_ref.refs_0_), channel_id=1, source_target_pairs={{0,4},{1,5},{2,6},{3,7},{4,0},{5,1},{6,2},{7,3},{8,12},{9,13},{10,... | collective-permute-start | bytes 294920 | tf_op jit(solution)/shard_map/ppermute | solution.py:420
  38.0 4.6 %collective-permute-start.3 = (bf16[384,128]{1,0:T(8,128)(2,1)S(1)}, bf16[384,128]{1,0:T(8,128)(2,1)S(1)}, u32[]{:S(2)}, u32[]{:S(2)}) collective-permute-start(bf16[384,128]{1,0:T(8,128)(2,1)S(1)} %get-tuple-element.6.own_ref.refs_0_), channel_id=1, source_target_pairs={{0,2},{1,3},{2,0},{3,1},{4,6},{5,7},{6,4},{7,5},{8,10},{9,11},{10,... | collective-permute-start | bytes 294920 | tf_op jit(solution)/shard_map/ppermute | solution.py:420
  38.0 4.6 %collective-permute-start.2 = (bf16[384,128]{1,0:T(8,128)(2,1)S(1)}, bf16[384,128]{1,0:T(8,128)(2,1)S(1)}, u32[]{:S(2)}, u32[]{:S(2)}) collective-permute-start(bf16[384,128]{1,0:T(8,128)(2,1)S(1)} %get-tuple-element.6.own_ref.refs_0_), channel_id=1, source_target_pairs={{0,1},{1,0},{2,3},{3,2},{4,5},{5,4},{6,7},{7,6},{8,9},{9,8},{10,11... | collective-permute-start | bytes 294920 | tf_op jit(solution)/shard_map/ppermute | solution.py:420

commit v4 on v3

--- a/solution.py
+++ b/solution.py
@@ -12,6 +12,8 @@
 COARSEN = 8
 STEP = 2
 PARTS = 2
+LOW = 3
+HIGH = (TILE + 2 * HALO) // TILE - LOW
 PAD = 16
 BF = jnp.bfloat16
 F32 = jnp.float32
@@ -28,6 +30,10 @@
 
 def pick(off, lane, blocks):
     return [one_hot(off == lane + I16(c * TILE)) for c in range(blocks)]
+
+
+def aligned(row):
+    return row if isinstance(row, int) else pl.multiple_of(row, TILE)
 
 
 def column(rows_t, col):
@@ -58,13 +64,16 @@
 
 
 def mean_weight(gain):
+    return 1.0 / (gain * gain * gain.shape[1])
+
+
+def mean_square(gain):
     lat = gain.shape[1]
-    return twice(jnp.broadcast_to(1.0 / (gain * gain * lat), (lat, lat)).T.astype(BF))
-
-
-def norm(hidden, w, m):
-    c = pair_dot(hidden, w)
-    return c * lax.rsqrt(pair_dot((c * c).astype(BF), m) + 1e-05)
+    return twice(jnp.broadcast_to(mean_weight(gain), (lat, lat)).T.astype(BF))
+
+
+def scaled(c, weight):
+    return c * lax.rsqrt(jnp.sum(c * c * weight, axis=1, keepdims=True) + 1e-05)
 
 
 def half_silu(y):
@@ -86,27 +95,144 @@
         active = alive
 
 
-def fine_kernel(base_ref, edge_ref, last_ref, before_ref, after_ref, *refs):
+def make_stages(block, window, base, refs, base_ref):
+    edge_ref, last_ref, edge_out_ref, own_ref, cmap_ref, fine_ref = refs[:6]
+    sent_s, recv_s, we_s, w2_s, m_s, nw1_s, nw2_s, nm_s, code_s, loc_s = refs[6:16]
+    hid_s, inc_s, pool_s, per = refs[16:]
+    lat = sent_s.shape[1]
+    crows = pool_s.shape[0]
+    groups = per // TILE
+    part = per // PARTS
+    lane = lax.broadcasted_iota(I16, (TILE, TILE), 1)
+    sub = lax.broadcasted_iota(I16, (TILE, TILE), 0)
+    csub = lax.broadcasted_iota(I16, (crows, TILE), 0)
+    incoming = {}
+
+    def rows_of(s, k, q):
+        start = (base(s) + k) * per + q * part
+        return slice(start, start + part), (k * per + q * part) // TILE
+
+    def weights(s, k):
+        start = aligned(window(s) + k * TILE)
+        at = aligned((block(s) * STEP + k) * TILE)
+        mine = recv_s[pl.ds(at, TILE)]
+        low = jnp.concatenate([sent_s[pl.ds(start, LOW * TILE)], mine], axis=0)
+        high = jnp.concatenate(
+            [
+                sent_s[pl.ds(start + LOW * TILE, HIGH * TILE)],
+                sent_s[pl.ds(start, (LOW - HIGH) * TILE)],
+                mine,
+            ],
+            axis=0,
+        )
+        return jnp.concatenate([low, high], axis=1)
+
+    def first(s, k, q):
+        at, col0 = rows_of(s, k, q)
+        code_t = code_s[block(s)]
+        lhs, upper = [], []
+        for j in range(part // TILE):
+            word = column(code_t, col0 + j)
+            o = word.astype(I16) & I16(511)
+            r = (word >> 16).astype(I16) & I16(TILE - 1)
+            lhs.append(jnp.concatenate(pick(o, lane, LOW) + pick(r, lane, 1), axis=1))
+            upper.append(word < 0)
+        y = pair_dot(edge_ref[at], we_s[...])
+        out = dot(jnp.concatenate(lhs, axis=0), weights(s, k))
+        yield
+        y = y + jnp.where(jnp.concatenate(upper, axis=0), out[:, lat:], out[:, :lat])
+        hid_s[at] = half_silu(y)
+
+    def second(s, k, q):
+        at, col0 = rows_of(s, k, q)
+        c = pair_dot(hid_s[at], w2_s[...])
+        yield
+        new = (last_ref[at].astype(F32) + scaled(c, m_s[...])).astype(BF)
+        edge_out_ref[at] = new
+        loc = loc_s[block(s)]
+        back = [
+            one_hot(along_lanes(loc[j : j + 1], TILE) == sub)
+            for j in range(col0, col0 + part // TILE)
+        ]
+        incoming.setdefault(k + base(s), []).append((back, new))
+        yield
+        if q == PARTS - 1:
+            backs, news = zip(*incoming.pop(k + base(s)))
+            row = (base(s) + k) * TILE
+            inc_s[row : row + TILE] = dot(
+                jnp.concatenate(sum(backs, []), axis=1), jnp.concatenate(news, axis=0)
+            ).astype(BF)
+
+    def third(s):
+        here = pl.ds(aligned(block(s) * STEP * TILE), STEP * TILE)
+        own = own_ref[here]
+        got = inc_s[base(s) * TILE : (base(s) + STEP) * TILE]
+        y = dot(jnp.concatenate([own, got], axis=1), nw1_s[...])
+        yield
+        c = pair_dot(half_silu(y), nw2_s[...])
+        yield
+        var = pair_dot((c * c).astype(BF), nm_s[...])
+        yield
+        fine = (own.astype(F32) + c * lax.rsqrt(var + 1e-05)).astype(BF)
+        fine_ref[here] = fine
+        member = []
+        for k in range(STEP):
+            local = cmap_ref[pl.ds(block(s) * STEP + k, 1), :] - base_ref[0] * crows
+            member.append(one_hot(along_lanes(local, crows) == csub))
+        fine = jnp.concatenate([fine, jnp.ones_like(fine)], axis=1)
+        pool_s[...] += dot(jnp.concatenate(member, axis=1), fine)
+
+    return first, second, third
+
+
+def run_stages(step, count, stages):
+    first, second, third = stages
+    parts = [(k, q) for k in range(STEP) for q in range(PARTS)]
+
+    def run(one, two, three):
+        interleave(
+            [
+                [second(step - 1, k, q)] * two + [first(step, k, q)] * one
+                for k, q in (parts if one or two else [])
+            ],
+            [third(step - 2)] if three else [],
+        )
+
+    for when, which in (
+        ((step >= 2) & (step < count), (True, True, True)),
+        (step == 0, (True, False, False)),
+        (step == 1, (True, True, False)),
+        (step == count, (False, True, True)),
+        (step == count + 1, (False, False, True)),
+    ):
+        pl.when(when)(functools.partial(run, *which))
+
+
+def inner_kernel(count, base_ref, edge_ref, last_ref, all_ref, *refs):
     hbm, refs = refs[:12], refs[12:]
-    (edge_out_ref, fine_ref, coarse_ref), refs = refs[:3], refs[3:]
-    vmem, refs = refs[:12], refs[12:]
-    own_ref, send_ref, recv_ref, cmap_ref, w1_ref, u_ref, v_ref = vmem[:7]
-    edge_w2_ref, nw1_ref, node_w2_ref, gain_ref, ngain_ref = vmem[7:]
-    sent_s, recv_s, we_s, w2_s, m_s, nw1_s, nw2_s, nm_s, code_s, loc_s, hid_s, inc_s, pool_s, sem = refs
+    edge_out_ref, fine_ref, pool_ref, ws_ref, ends_ref, own_ref, cmap_ref = refs[:7]
+    ready, refs = refs[7:17], refs[17:]
+    vmem, (hid_s, inc_s, sem) = refs[:10], refs[10:]
+    send_ref, recv_ref, w1_ref, u_ref, v_ref = vmem[:5]
+    edge_w2_ref, node_w1_ref, node_w2_ref, gain_ref, ngain_ref = vmem[5:]
+    vmem = (own_ref, cmap_ref) + vmem
+    sent_s, recv_s, we_s, w2_s, m_s, nw1_s, nw2_s, nm_s, code_s, loc_s = ready
     step = pl.program_id(0)
-    steps = pl.num_programs(0) - 2
     rows, lat = own_ref.shape
-    per = edge_ref.shape[0] // STEP
-    groups = per // TILE
-    idx_rows = STEP * groups
-    crows = coarse_ref.shape[0]
-    low_blocks = 3
-    high_blocks = (TILE + 2 * HALO) // TILE - low_blocks
+    size = edge_ref.shape[0]
+    idx_rows = size // TILE
+    ends = [
+        pltpu.make_async_copy(
+            all_ref.at[pl.ds(at * size, size)], ends_ref.at[pl.ds(n * size, size)],
+            sem.at[len(hbm) + n],
+        )
+        for n, at in enumerate((0, count + 1))
+    ]
 
     @pl.when(step == 0)
     def _():
         copies = [pltpu.make_async_copy(a, b, sem.at[i]) for i, (a, b) in enumerate(zip(hbm, vmem))]
-        for c in copies:
+        for c in copies + ends:
             c.start()
         for c in copies:
             c.wait()
@@ -116,124 +242,95 @@
         w_eff = (0.5 * w_eff).astype(BF)
         we_s[...] = twice(w_eff[:lat])
         ws = w_eff[lat : 2 * lat]
+        ws_ref[...] = ws
         both = dot(own_ref[...], jnp.concatenate([ws, w_eff[2 * lat :]], axis=1)).astype(BF)
-        sent_s[0:HALO] = dot(before_ref[...], ws).astype(BF)
-        sent_s[HALO : HALO + rows] = both[:, :lat]
-        sent_s[HALO + rows :] = dot(after_ref[...], ws).astype(BF)
+        sent_s[...] = both[:, :lat]
         recv_s[...] = both[:, lat:]
         w2_s[...] = gained(edge_w2_ref[...], gain_ref[...])
         m_s[...] = mean_weight(gain_ref[...])
+        nw1_s[...] = node_w1_ref[...] * 0.5
         nw2_s[...] = gained(node_w2_ref[...], ngain_ref[...])
-        nm_s[...] = mean_weight(ngain_ref[...])
-        nw1_s[...] = nw1_ref[...] * 0.5
-        pool_s[...] = jnp.zeros_like(pool_s)
+        nm_s[...] = mean_square(ngain_ref[...])
+        pool_ref[...] = jnp.zeros_like(pool_ref)
         recv = recv_ref[...]
         loc = recv & (TILE - 1)
         off = send_ref[...] - (recv - loc) + HALO
-        hi = off >= low_blocks * TILE
-        lo = jnp.where(hi, off - low_blocks * TILE, off)
+        hi = off >= LOW * TILE
+        lo = jnp.where(hi, off - LOW * TILE, off)
         code = lo | (loc << 16) | jnp.where(hi, jnp.int32(-(2**31)), 0)
         for s in range(rows // TILE // STEP):
             sl = slice(s * idx_rows, (s + 1) * idx_rows)
             code_s[s, :, 0:idx_rows] = code[sl].T
             loc_s[s, 0:idx_rows] = loc[sl]
 
-    this, prev, past = step, step - 1, step - 2
-    part = per // PARTS
-    lane = lax.broadcasted_iota(I16, (TILE, TILE), 1)
-    sub = lax.broadcasted_iota(I16, (TILE, TILE), 0)
-    csub = lax.broadcasted_iota(I16, (crows, TILE), 0)
-    incoming = [[] for _ in range(STEP)]
-
-    def weights(k):
-        start = pl.multiple_of((this * STEP + k) * TILE, TILE)
-        mine = recv_s[pl.ds(start, TILE)]
-        low = jnp.concatenate([sent_s[pl.ds(start, low_blocks * TILE)], mine], axis=0)
-        high = jnp.concatenate(
-            [
-                sent_s[pl.ds(start + low_blocks * TILE, high_blocks * TILE)],
-                sent_s[pl.ds(start, (low_blocks - high_blocks) * TILE)],
-                mine,
-            ],
-            axis=0,
+    run_stages(
+        step, count,
+        make_stages(
+            lambda s: s + 1, lambda s: (s + 1) * STEP * TILE - HALO, lambda s: 0,
+            (edge_ref, last_ref, edge_out_ref, own_ref, cmap_ref, fine_ref) + ready
+            + (hid_s, inc_s, pool_ref, size // STEP),
+            base_ref,
+        ),
+    )
+
+    @pl.when(step == count + 1)
+    def _():
+        for c in ends:
+            c.wait()
+
+
+def border_kernel(
+    last_block, base_ref, ends_ref, own_ref, across_ref, within_ref, cmap_ref, pool_ref,
+    ws_ref, *refs
+):
+    ready, refs = refs[:10], refs[12:]
+    edge_out_ref, fine_ref, coarse_ref, win_s, out_s, hid_s, inc_s, pool_s, sem = refs
+    sent_ref = ready[0]
+    rows, lat = sent_ref.shape
+    size = ends_ref.shape[0] // 2
+    span = STEP * TILE + 2 * HALO
+    inside = span - HALO
+    even = base_ref[0] % 2 == 0
+    across, within = across_ref[...], within_ref[...]
+    ws = ws_ref[...]
+    win_s[:HALO] = dot(jnp.where(even, across, within), ws).astype(BF)
+    win_s[HALO:span] = sent_ref[:inside]
+    win_s[span : span + inside] = sent_ref[rows - inside :]
+    win_s[span + inside :] = dot(jnp.where(even, within, across), ws).astype(BF)
+    pool_s[...] = pool_ref[...]
+    first, second, third = make_stages(
+        lambda s: s * last_block, lambda s: s * span, lambda s: s * STEP,
+        (ends_ref, ends_ref, out_s, own_ref, cmap_ref, fine_ref, win_s) + ready[1:]
+        + (hid_s, inc_s, pool_s, size // STEP),
+        base_ref,
+    )
+    copies = []
+
+    def send(s):
+        copies.append(
+            pltpu.make_async_copy(
+                out_s.at[pl.ds(s * size, size)],
+                edge_out_ref.at[pl.ds(s * last_block * size, size)],
+                sem.at[s],
+            )
         )
-        return jnp.concatenate([low, high], axis=1)
-
-    def first(k, q):
-        at = slice(k * per + q * part, k * per + (q + 1) * part)
-        code_t = code_s[this]
-        lhs, upper = [], []
-        for j in range(part // TILE):
-            word = column(code_t, at.start // TILE + j)
-            o = word.astype(I16) & I16(511)
-            r = (word >> 16).astype(I16) & I16(TILE - 1)
-            lhs.append(jnp.concatenate(pick(o, lane, low_blocks) + pick(r, lane, 1), axis=1))
-            upper.append(word < 0)
-        out = dot(jnp.concatenate(lhs, axis=0), weights(k))
-        y = pair_dot(edge_ref[at], we_s[...])
-        yield
-        y = y + jnp.where(jnp.concatenate(upper, axis=0), out[:, lat:], out[:, :lat])
-        hid_s[at] = half_silu(y)
-
-    def second(k, q):
-        at = slice(k * per + q * part, k * per + (q + 1) * part)
-        c = pair_dot(hid_s[at], w2_s[...])
-        yield
-        var = pair_dot((c * c).astype(BF), m_s[...])
-        yield
-        new = (last_ref[at].astype(F32) + c * lax.rsqrt(var + 1e-05)).astype(BF)
-        edge_out_ref[at] = new
-        loc = loc_s[prev]
-        back = [
-            one_hot(along_lanes(loc[j : j + 1], TILE) == sub)
-            for j in range(at.start // TILE, at.stop // TILE)
-        ]
-        incoming[k].append(dot(jnp.concatenate(back, axis=1), new))
-        yield
-        if q == PARTS - 1:
-            inc_s[k * TILE : (k + 1) * TILE] = sum(incoming[k][1:], incoming[k][0]).astype(BF)
-
-    def third():
-        here = pl.ds(pl.multiple_of(past * STEP * TILE, STEP * TILE), STEP * TILE)
-        own = own_ref[here]
-        y = dot(jnp.concatenate([own, inc_s[...]], axis=1), nw1_s[...])
-        yield
-        c = pair_dot(half_silu(y), nw2_s[...])
-        yield
-        var = pair_dot((c * c).astype(BF), nm_s[...])
-        yield
-        fine = (own.astype(F32) + c * lax.rsqrt(var + 1e-05)).astype(BF)
-        fine_ref[here] = fine
-        member = []
-        for k in range(STEP):
-            local = cmap_ref[pl.ds(past * STEP + k, 1), :] - base_ref[0] * crows
-            member.append(one_hot(along_lanes(local, crows) == csub))
-        fine = jnp.concatenate([fine, jnp.ones_like(fine)], axis=1)
-        pool_s[...] += dot(jnp.concatenate(member, axis=1), fine)
-
-    def stages(one, two, three):
-        for k in range(STEP):
-            incoming[k].clear()
-        todo = [(k, q) for k in range(STEP) for q in range(PARTS)] if one or two else []
-        interleave(
-            [[second(k, q)] * two + [first(k, q)] * one for k, q in todo],
-            [third()] if three else [],
-        )
-
-    full = (step >= 2) & (step < steps)
-    for when, which in (
-        (full, (True, True, True)),
-        (step == 0, (True, False, False)),
-        (step == 1, (True, True, False)),
-        (step == steps, (False, True, True)),
-        (step == steps + 1, (False, False, True)),
-    ):
-        pl.when(when)(functools.partial(stages, *which))
-
-    @pl.when(step == steps + 1)
-    def _():
-        total = pool_s[...]
-        coarse_ref[...] = (total[:, :lat] / jnp.maximum(total[:, lat:], 1.0)).astype(BF)
+        copies[-1].start()
+        yield
+
+    parts = [(s, k, q) for s in range(2) for k in range(STEP) for q in range(PARTS)]
+    half = STEP * PARTS
+    ticks = [[] for _ in range(2 * half + 8)]
+    for n, p in enumerate(parts):
+        ticks[n].append(first(*p))
+        ticks[n + 2].insert(0, second(*p))
+    for s in range(2):
+        done = (s + 1) * half + 1 + 3
+        ticks[done] += [send(s), third(s)]
+    interleave(ticks, [])
+    total = pool_s[...]
+    coarse_ref[...] = (total[:, :lat] / jnp.maximum(total[:, lat:], 1.0)).astype(BF)
+    for c in copies:
+        c.wait()
 
 
 def near_kernel(base_ref, send_ref, recv_ref, own_ref, w1_ref, pre_ref):
@@ -364,56 +461,85 @@
     per = edges // tiles
     crows = nodes // COARSEN
     steps = tiles // STEP
-    up = [(i, i + 1) for i in range(size - 1)]
-    down = [(j, i) for i, j in up]
-    before = lax.ppermute(node_latent[nodes - HALO :], axes, up)
-    after = lax.ppermute(node_latent[:HALO], axes, down)
+    even = dev[0] % 2 == 0
+    ends = (node_latent[:HALO], node_latent[nodes - HALO :])
+    across = [(i, i + 1) for i in range(1, size - 1, 2)]
+    within = [(i, i + 1) for i in range(0, size, 2)]
+    across = lax.ppermute(
+        jnp.where(even, ends[0], ends[1]), axes, across + [(j, i) for i, j in across]
+    )
+    within = lax.ppermute(
+        jnp.where(even, ends[1], ends[0]), axes, within + [(j, i) for i, j in within]
+    )
     cmap2 = coarse_map.reshape(tiles, TILE)
     vm = pl.BlockSpec(memory_space=pltpu.VMEM)
     sm = pl.BlockSpec(memory_space=pltpu.SMEM)
     hb = pl.BlockSpec(memory_space=pltpu.HBM)
     hbm = (
-        node_latent, senders.reshape(edges // TILE, TILE), receivers.reshape(edges // TILE, TILE),
-        cmap2, edge_w1, mod_u.T, mod_v, edge_w2, node_w1, node_w2,
-        edge_gain.reshape(1, lat), node_gain.reshape(1, lat),
+        node_latent, cmap2, senders.reshape(edges // TILE, TILE),
+        receivers.reshape(edges // TILE, TILE), edge_w1, mod_u.T, mod_v, edge_w2, node_w1,
+        node_w2, edge_gain.reshape(1, lat), node_gain.reshape(1, lat),
     )
     big = (STEP * per, lat)
-    index = pltpu.VMEM((steps, PAD, TILE), jnp.int32)
-    square = pltpu.VMEM((2 * lat, 2 * lat), BF)
-    far = pltpu.with_memory_space_constraint(edge_latent, pltpu.HBM)
-    edge_out, fine, coarse = pl.pallas_call(
-        fine_kernel,
-        grid=(steps + 2,),
+    apart = lambda a: pltpu.with_memory_space_constraint(a, pltpu.HBM)
+    far = apart(edge_latent)
+    count = steps - 2
+    full = jax.ShapeDtypeStruct((edges, lat), BF)
+    inner_block = lambda i: (jnp.clip(i, 0, count - 1) + 1, 0)
+    ready = [
+        jax.ShapeDtypeStruct(shape, dtype)
+        for shape, dtype in [((nodes, lat), BF)] * 2
+        + [((2 * lat, 2 * lat), BF)] * 2
+        + [((1, lat), F32), ((2 * lat, lat), BF), ((2 * lat, 2 * lat), BF), ((2 * lat, 2 * lat), BF)]
+        + [((steps, TILE, PAD), jnp.int32), ((steps, PAD, TILE), jnp.int32)]
+    ]
+    edge_out, fine, pool, ws, ends, own, cmap2, *ready = pl.pallas_call(
+        functools.partial(inner_kernel, count),
+        grid=(count + 2,),
         in_specs=[
             sm,
-            pl.BlockSpec(big, lambda i: (jnp.minimum(i, steps - 1), 0)),
-            pl.BlockSpec(big, lambda i: (jnp.clip(i - 1, 0, steps - 1), 0)),
-            vm, vm,
-        ] + [hb] * len(hbm),
-        out_specs=[pl.BlockSpec(big, lambda i: (jnp.clip(i - 1, 0, steps - 1), 0)), vm, vm],
+            pl.BlockSpec(big, inner_block),
+            pl.BlockSpec(big, lambda i: inner_block(i - 1)),
+        ] + [hb] * (1 + len(hbm)),
+        out_specs=[pl.BlockSpec(big, lambda i: inner_block(i - 1))] + [vm] * (6 + len(ready)),
         out_shape=[
-            jax.ShapeDtypeStruct((edges, lat), BF),
+            full,
+            jax.ShapeDtypeStruct((nodes, lat), BF),
+            jax.ShapeDtypeStruct((crows, 2 * lat), F32),
+            jax.ShapeDtypeStruct((lat, lat), BF),
+            jax.ShapeDtypeStruct((2 * STEP * per, lat), BF),
+            jax.ShapeDtypeStruct((nodes, lat), BF),
+            jax.ShapeDtypeStruct(cmap2.shape, cmap2.dtype),
+        ] + ready,
+        scratch_shapes=[pltpu.VMEM(a.shape, a.dtype) for a in hbm[2:]]
+        + [pltpu.VMEM(big, BF), pltpu.VMEM((STEP * TILE, lat), BF)]
+        + [pltpu.SemaphoreType.DMA((len(hbm) + 2,))],
+        compiler_params=pltpu.CompilerParams(
+            dimension_semantics=("arbitrary",), vmem_limit_bytes=24 * 2**20
+        ),
+        name="inner",
+    )(dev, far, far, far, *[apart(a) for a in hbm])
+    edge_out, fine, coarse = pl.pallas_call(
+        functools.partial(border_kernel, steps - 1),
+        in_specs=[sm] + [vm] * (7 + len(ready)) + [hb, vm],
+        out_specs=[hb, vm, vm],
+        out_shape=[
+            full,
             jax.ShapeDtypeStruct((nodes, lat), BF),
             jax.ShapeDtypeStruct((crows, lat), BF),
         ],
-        scratch_shapes=[pltpu.VMEM(a.shape, a.dtype) for a in hbm] + [
-            pltpu.VMEM((nodes + 2 * HALO, lat), BF),
-            pltpu.VMEM((nodes, lat), BF),
-            square, square, square,
-            pltpu.VMEM((2 * lat, lat), BF),
-            square, square,
-            pltpu.VMEM((steps, TILE, PAD), jnp.int32),
-            index,
-            pltpu.VMEM(big, BF),
-            pltpu.VMEM((STEP * TILE, lat), BF),
+        input_output_aliases={8 + len(ready): 0, 9 + len(ready): 1},
+        scratch_shapes=[
+            pltpu.VMEM((2 * (STEP * TILE + 2 * HALO), lat), BF),
+            pltpu.VMEM((2 * STEP * per, lat), BF),
+            pltpu.VMEM((2 * STEP * per, lat), BF),
+            pltpu.VMEM((2 * STEP * TILE, lat), BF),
             pltpu.VMEM((crows, 2 * lat), F32),
-            pltpu.SemaphoreType.DMA((len(hbm),)),
+            pltpu.SemaphoreType.DMA((2,)),
         ],
-        compiler_params=pltpu.CompilerParams(
-            dimension_semantics=("arbitrary",), vmem_limit_bytes=48 * 2**20
-        ),
-        name="fine",
-    )(dev, far, far, before, after, *[pltpu.with_memory_space_constraint(a, pltpu.HBM) for a in hbm])
+        compiler_params=pltpu.CompilerParams(vmem_limit_bytes=24 * 2**20),
+        name="border",
+    )(dev, ends, own, across, within, cmap2, pool, ws, *ready, edge_out, fine)
     tables = [coarse]
     bit = 1
     while bit < size:

time: 47.2 us -> 40.7 us (0.86)
  starting transfers between devices: 14.1 us -> 9.78 us
  waiting for transfers between devices: 4.14 us -> 2.68 us
  Pallas kernels: 27.1 us -> 26.1 us
  other arithmetic: 0 us -> 0.89 us
  local copies, waits for them, and re-layouts: 0.91 us -> 0.03 us
    ppermute x2, starting transfers between devices: 4.33 us -> 1.17 us  [the longest x1 0.65 us: on_device(): lax.ppermute(jnp.where(even, ends[0], ends[1]), axes, across + [(j, i) fo...]
    ppermute x4, starting transfers between devices: 9.74 us -> 8.61 us  [on_device(): lax.ppermute(coarse, axes, [(i, i ^ bit) for i in range(size)])]
    pallas_call x1 -> x2, Pallas kernels: 21.5 us -> 20.5 us  [the longest x1 17.3 us: on_device(): pl.pallas_call(functools.partial(inner_kernel, count), grid=(count + 2,),...]
    select_n x0 -> x1, other arithmetic: none -> 0.89 us  [on_device(): jnp.where(even, ends[1], ends[0])]
    slice x1 -> x0, local copies, waits for them, and re-layouts: 0.88 us -> none  [on_device(): after = lax.ppermute(node_latent[:HALO], axes, down)]
    ppermute x2, waiting for transfers between devices: 0.87 us -> 0.01 us  [the longest x1 0.01 us: on_device(): lax.ppermute(jnp.where(even, ends[1], ends[0]), axes, within + [(j, i) fo...]
    ppermute x4, waiting for transfers between devices: 3.27 us -> 2.67 us  [on_device(): lax.ppermute(coarse, axes, [(i, i ^ bit) for i in range(size)])]
  transfers between devices with their start and end apart: 6 -> 6, of which waited for: 3 -> 3; matrix products, arithmetic and copies ran while one was open for 0% -> 0% of each run, Pallas kernels for 3% -> 46%
where the time goes in v4:
time: 40.7 us; the launch traced here: 40.2 us
  Pallas kernels  26.1 us (64%)
  starting transfers between devices  9.78 us (24%)
  waiting for transfers between devices  2.68 us (7%)
  other arithmetic  0.89 us (2%)
  between operations  0.75 us (2%)
    pallas_call x1, Pallas kernels, on_device(): pl.pallas_call(functools.partial(inner_kernel, count), grid=(count + 2,),...  17.3 us
    ppermute x4, starting transfers between devices, on_device(): lax.ppermute(coarse, axes, [(i, i ^ bit) for i in range(size)])  8.61 us
    pallas_call x1, Pallas kernels, on_device(): pl.pallas_call(coarse_kernel, in_specs=[sm] + [vm] * (8 + len(tables)), o...  4.32 us
    pallas_call x1, Pallas kernels, on_device(): pl.pallas_call(functools.partial(border_kernel, steps - 1), in_specs=[sm]...  3.18 us
    ppermute x4, waiting for transfers between devices, on_device(): lax.ppermute(coarse, axes, [(i, i ^ bit) for i in range(size)])  2.67 us
    pallas_call x1, Pallas kernels, on_device(): pl.pallas_call(near_kernel, in_specs=[sm] + [vm] * 4, out_specs=vm, out_s...  1.3 us
    select_n x1, other arithmetic, on_device(): jnp.where(even, ends[1], ends[0])  0.89 us
  transfers between devices with their start and end apart: 6, of which 3 were waited for; matrix products, arithmetic and copies ran while one was open for 0% of the time, Pallas kernels for 46%

profile of v4, /device:TPU:0, one launch (start us, length us, event | category | flops | bytes accessed | tf_op | source)
XLA Modules:
  0.0 40.2 jit_solution(16597636830139461649)
XLA Ops:
  0.6 0.9 %broadcast_select_fusion = (bf16[256,128]{1,0:T(8,128)(2,1)S(1)}, bf16[256,128]{1,0:T(8,128)(2,1)S(1)}) fusion(pred[]{:T(512)S(6)} %eq.5, bf16[3072,128]{1,0:T(8,128)(2,1)} %refs_0_.1), kind=kLoop, calls=%fused_computation | loop fusion | flops 65536 | bytes 262145 | tf_op jit(solution)/shard_map/jit(_where)/select_n | solution.py:472
  1.5 0.5 %collective-permute-start.1 = (bf16[256,128]{1,0:T(8,128)(2,1)S(1)}, bf16[256,128]{1,0:T(8,128)(2,1)S(1)}, u32[]{:S(2)}, u32[]{:S(2)}) collective-permute-start(bf16[256,128]{1,0:T(8,128)(2,1)S(1)} %get-tuple-element.42), channel_id=1, source_target_pairs={{0,1},{2,3},{4,5},{6,7},{8,9},{10,11},{12,13},{14,15},{1,0},{3,2},... | collective-permute-start | bytes 196616 | tf_op jit(solution)/shard_map/ppermute | solution.py:471
  2.1 0.7 %collective-permute-start = (bf16[256,128]{1,0:T(8,128)(2,1)S(1)}, bf16[256,128]{1,0:T(8,128)(2,1)S(1)}, u32[]{:S(2)}, u32[]{:S(2)}) collective-permute-start(bf16[256,128]{1,0:T(8,128)(2,1)S(1)} %get-tuple-element.43), channel_id=1, source_target_pairs={{1,2},{3,4},{5,6},{7,8},{9,10},{11,12},{13,14},{2,1},{4,3},{6,5},{... | collective-permute-start | bytes 196616 | tf_op jit(solution)/shard_map/ppermute | solution.py:468
  2.7 17.3 %inner.1 = (bf16[18432,128]{1,0:T(8,128)(2,1)}, bf16[3072,128]{1,0:T(8,128)(2,1)S(1)}, f32[384,256]{1,0:T(8,128)S(1)}, bf16[128,128]{1,0:T(8,128)(2,1)S(1)}, bf1...) custom-call(s32[1]{0:T(128)} %bitcast.base_ref, ...), custom_call_target="tpu_custom_call" | custom-call | tf_op jit(solution)/shard_map/inner/pallas_call | solution.py:496
  20.0 0.0 collective-permute-done.1.within_ref
  20.0 0.0 collective-permute-done.across_ref
  20.1 0.0 copy-start
  20.1 0.0 copy-start.1
  20.1 0.0 copy-start.2
  20.1 0.0 copy-start.3
  20.1 0.0 copy-start.4
  20.1 3.2 %border.1 = (bf16[18432,128]{1,0:T(8,128)(2,1)}, bf16[3072,128]{1,0:T(8,128)(2,1)S(1)}, bf16[384,128]{1,0:T(8,128)(2,1)S(1)}) custom-call(s32[1]{0:T(128)} %bitcast.base_ref, bf16[3072,128]{1,0:T(8,128)(2,1)S(1)} %get-tuple-element.23.ends_ref, bf16[3072,128]{1,0:T(8,128)(2,1)S(1)} %get-tuple-element.24.own_ref, ...), custom_call_target="tpu_custom_call", output_to_operand_aliasing={{0}: (18, {}), {1}: (19, {})} | custom-call | tf_op jit(solution)/shard_map/border/pallas_call | solution.py:522
  23.3 6.4 %collective-permute-start.5 = (bf16[384,128]{1,0:T(8,128)(2,1)S(1)}, bf16[384,128]{1,0:T(8,128)(2,1)S(1)}, u32[]{:S(2)}, u32[]{:S(2)}) collective-permute-start(bf16[384,128]{1,0:T(8,128)(2,1)S(1)} %get-tuple-element.40.own_ref.refs_0_), channel_id=1, source_target_pairs={{0,8},{1,9},{2,10},{3,11},{4,12},{5,13},{6,14},{7,15},{8,0},{9,1},... | collective-permute-start | bytes 294920 | tf_op jit(solution)/shard_map/ppermute | solution.py:546
  29.7 1.6 %collective-permute-start.4 = (bf16[384,128]{1,0:T(8,128)(2,1)S(1)}, bf16[384,128]{1,0:T(8,128)(2,1)S(1)}, u32[]{:S(2)}, u32[]{:S(2)}) collective-permute-start(bf16[384,128]{1,0:T(8,128)(2,1)S(1)} %get-tuple-element.40.own_ref.refs_0_), channel_id=1, source_target_pairs={{0,4},{1,5},{2,6},{3,7},{4,0},{5,1},{6,2},{7,3},{8,12},{9,13},{10,... | collective-permute-start | bytes 294920 | tf_op jit(solution)/shard_map/ppermute | solution.py:546
  31.3 0.6 %collective-permute-start.3 = (bf16[384,128]{1,0:T(8,128)(2,1)S(1)}, bf16[384,128]{1,0:T(8,128)(2,1)S(1)}, u32[]{:S(2)}, u32[]{:S(2)}) collective-permute-start(bf16[384,128]{1,0:T(8,128)(2,1)S(1)} %get-tuple-element.40.own_ref.refs_0_), channel_id=1, source_target_pairs={{0,2},{1,3},{2,0},{3,1},{4,6},{5,7},{6,4},{7,5},{8,10},{9,11},{10,... | collective-permute-start | bytes 294920 | tf_op jit(solution)/shard_map/ppermute | solution.py:546
  31.9 0.0 collective-permute-start.2
  31.9 0.0 copy-done
  31.9 0.0 copy-done.1
  31.9 0.0 copy-done.2
  31.9 1.3 %near.1.pre_ref = f32[2304,128]{1,0:T(8,128)S(1)} custom-call(s32[1]{0:T(128)} %bitcast.base_ref, s32[18,128]{1,0:T(8,128)S(1)} %bitcast.10, s32[18,128]{1,0:T(8,128)S(1)} %bitcast.12, bf16[384,128]{1,0:T(8,128)(2,1)S(1)} %get-tuple-element.40.own_ref.refs_0_, bf16[256,128]{1,0:T(8,128)(2,1)S(1)} %copy-done), custom_call_target="tpu_custom_call" | custom-call | tf_op jit(solution)/shard_map/near/pallas_call | solution.py:551
  33.2 1.8 %collective-permute-done.5.refs_4_ = bf16[384,128]{1,0:T(8,128)(2,1)S(1)} collective-permute-done((bf16[384,128]{1,0:T(8,128)(2,1)S(1)}, bf16[384,128]{1,0:T(8,128)(2,1)S(1)}, u32[]{:S(2)}, u32[]{:S(2)}) %collective-permute-start.5) | collective-permute-done | bytes 98336 | tf_op jit(solution)/shard_map/ppermute | solution.py:546
  35.1 0.2 collective-permute-done.4.refs_3_
  35.3 0.6 %collective-permute-done.3.refs_2_ = bf16[384,128]{1,0:T(8,128)(2,1)S(1)} collective-permute-done((bf16[384,128]{1,0:T(8,128)(2,1)S(1)}, bf16[384,128]{1,0:T(8,128)(2,1)S(1)}, u32[]{:S(2)}, u32[]{:S(2)}) %collective-permute-start.3) | collective-permute-done | bytes 98336 | tf_op jit(solution)/shard_map/ppermute | solution.py:546
  35.9 0.0 collective-permute-done.2.refs_1_
  35.9 0.0 copy-done.3
  35.9 0.0 copy-done.4
  35.9 4.3 %coarse.1 = bf16[3072,128]{1,0:T(8,128)(2,1)} custom-call(s32[1]{0:T(128)} %bitcast.base_ref, s32[18,128]{1,0:T(8,128)S(1)} %bitcast.11, s32[18,128]{1,0:T(8,128)S(1)} %bitcast.13, s32[24,128]{1,0:T(8,128)S(1)} %get-tuple-element.22.cmap_ref, bf16[3072,128]{1,0:T(8,128)(2,1)S(1)} %get-tuple-element.39.fine_ref, f32[2304,128]{1,0:T(8,128)S(1)} %near.1.pre_ref, ...), custom_call_target="tpu_custom_call" | custom-call | tf_op jit(solution)/shard_map/coarse/pallas_call | solution.py:559
Async XLA Ops:
  1.5 18.5 %collective-permute-start.1 = (bf16[256,128]{1,0:T(8,128)(2,1)S(1)}, bf16[256,128]{1,0:T(8,128)(2,1)S(1)}, u32[]{:S(2)}, u32[]{:S(2)}) collective-permute-start(bf16[256,128]{1,0:T(8,128)(2,1)S(1)} %get-tuple-element.42), channel_id=1, source_target_pairs={{0,1},{2,3},{4,5},{6,7},{8,9},{10,11},{12,13},{14,15},{1,0},{3,2},... | collective-permute-start | bytes 196616 | tf_op jit(solution)/shard_map/ppermute | solution.py:471
  2.1 18.0 %collective-permute-start = (bf16[256,128]{1,0:T(8,128)(2,1)S(1)}, bf16[256,128]{1,0:T(8,128)(2,1)S(1)}, u32[]{:S(2)}, u32[]{:S(2)}) collective-permute-start(bf16[256,128]{1,0:T(8,128)(2,1)S(1)} %get-tuple-element.43), channel_id=1, source_target_pairs={{1,2},{3,4},{5,6},{7,8},{9,10},{11,12},{13,14},{2,1},{4,3},{6,5},{... | collective-permute-start | bytes 196616 | tf_op jit(solution)/shard_map/ppermute | solution.py:468
  20.1 11.9 %copy-start = (bf16[256,128]{1,0:T(8,128)(2,1)S(1)}, bf16[256,128]{1,0:T(8,128)(2,1)}, u32[]{:S(2)}) copy-start(bf16[256,128]{1,0:T(8,128)(2,1)} %w1_ref.3) | copy-start | bytes 196612
  20.1 11.9 %copy-start.1 = (s32[2304]{0:T(1024)S(1)}, s32[2304]{0:T(1024)}, u32[]{:S(2)}) copy-start(s32[2304]{0:T(1024)} %param.24) | copy-start | bytes 27652
  20.1 11.8 %copy-start.2 = (s32[2304]{0:T(1024)S(1)}, s32[2304]{0:T(1024)}, u32[]{:S(2)}) copy-start(s32[2304]{0:T(1024)} %param.23) | copy-start | bytes 27652
  20.1 15.8 %copy-start.3 = (bf16[128,128]{1,0:T(8,128)(2,1)S(1)}, bf16[128,128]{1,0:T(8,128)(2,1)}, u32[]{:S(2)}) copy-start(bf16[128,128]{1,0:T(8,128)(2,1)} %w2_ref.1) | copy-start | bytes 98308
  20.1 15.8 %copy-start.4 = (f32[128]{0:T(128)S(1)}, f32[128]{0:T(128)}, u32[]{:S(2)}) copy-start(f32[128]{0:T(128)} %param.35) | copy-start | bytes 1540
  23.3 11.8 %collective-permute-start.5 = (bf16[384,128]{1,0:T(8,128)(2,1)S(1)}, bf16[384,128]{1,0:T(8,128)(2,1)S(1)}, u32[]{:S(2)}, u32[]{:S(2)}) collective-permute-start(bf16[384,128]{1,0:T(8,128)(2,1)S(1)} %get-tuple-element.40.own_ref.refs_0_), channel_id=1, source_target_pairs={{0,8},{1,9},{2,10},{3,11},{4,12},{5,13},{6,14},{7,15},{8,0},{9,1},... | collective-permute-start | bytes 294920 | tf_op jit(solution)/shard_map/ppermute | solution.py:546
  29.7 5.6 %collective-permute-start.4 = (bf16[384,128]{1,0:T(8,128)(2,1)S(1)}, bf16[384,128]{1,0:T(8,128)(2,1)S(1)}, u32[]{:S(2)}, u32[]{:S(2)}) collective-permute-start(bf16[384,128]{1,0:T(8,128)(2,1)S(1)} %get-tuple-element.40.own_ref.refs_0_), channel_id=1, source_target_pairs={{0,4},{1,5},{2,6},{3,7},{4,0},{5,1},{6,2},{7,3},{8,12},{9,13},{10,... | collective-permute-start | bytes 294920 | tf_op jit(solution)/shard_map/ppermute | solution.py:546
  31.3 4.6 %collective-permute-start.3 = (bf16[384,128]{1,0:T(8,128)(2,1)S(1)}, bf16[384,128]{1,0:T(8,128)(2,1)S(1)}, u32[]{:S(2)}, u32[]{:S(2)}) collective-permute-start(bf16[384,128]{1,0:T(8,128)(2,1)S(1)} %get-tuple-element.40.own_ref.refs_0_), channel_id=1, source_target_pairs={{0,2},{1,3},{2,0},{3,1},{4,6},{5,7},{6,4},{7,5},{8,10},{9,11},{10,... | collective-permute-start | bytes 294920 | tf_op jit(solution)/shard_map/ppermute | solution.py:546
  31.9 4.0 %collective-permute-start.2 = (bf16[384,128]{1,0:T(8,128)(2,1)S(1)}, bf16[384,128]{1,0:T(8,128)(2,1)S(1)}, u32[]{:S(2)}, u32[]{:S(2)}) collective-permute-start(bf16[384,128]{1,0:T(8,128)(2,1)S(1)} %get-tuple-element.40.own_ref.refs_0_), channel_id=1, source_target_pairs={{0,1},{1,0},{2,3},{3,2},{4,5},{5,4},{6,7},{7,6},{8,9},{9,8},{10,11... | collective-permute-start | bytes 294920 | tf_op jit(solution)/shard_map/ppermute | solution.py:546

commit v5 on v4

--- a/solution.py
+++ b/solution.py
@@ -95,10 +95,10 @@
         active = alive
 
 
-def make_stages(block, window, base, refs, base_ref):
-    edge_ref, last_ref, edge_out_ref, own_ref, cmap_ref, fine_ref = refs[:6]
-    sent_s, recv_s, we_s, w2_s, m_s, nw1_s, nw2_s, nm_s, code_s, loc_s = refs[6:16]
-    hid_s, inc_s, pool_s, per = refs[16:]
+def make_stages(block, window, base, held, refs, base_ref):
+    edge_ref, own_ref, cmap_ref, fine_ref = refs[:4]
+    sent_s, recv_s, we_s, w2_s, m_s, nw1_s, nw2_s, nm_s, code_s, loc_s = refs[4:14]
+    hid_s, inc_s, pool_s, per = refs[14:]
     lat = sent_s.shape[1]
     crows = pool_s.shape[0]
     groups = per // TILE
@@ -109,8 +109,10 @@
     incoming = {}
 
     def rows_of(s, k, q):
-        start = (base(s) + k) * per + q * part
-        return slice(start, start + part), (k * per + q * part) // TILE
+        start = k * per + q * part
+        row = held(s) * per + start
+        at = pl.ds(aligned(base(s) * per + start), part)
+        return at, slice(row, row + part), start // TILE
 
     def weights(s, k):
         start = aligned(window(s) + k * TILE)
@@ -128,7 +130,7 @@
         return jnp.concatenate([low, high], axis=1)
 
     def first(s, k, q):
-        at, col0 = rows_of(s, k, q)
+        at, held_at, col0 = rows_of(s, k, q)
         code_t = code_s[block(s)]
         lhs, upper = [], []
         for j in range(part // TILE):
@@ -141,24 +143,24 @@
         out = dot(jnp.concatenate(lhs, axis=0), weights(s, k))
         yield
         y = y + jnp.where(jnp.concatenate(upper, axis=0), out[:, lat:], out[:, :lat])
-        hid_s[at] = half_silu(y)
+        hid_s[held_at] = half_silu(y)
 
     def second(s, k, q):
-        at, col0 = rows_of(s, k, q)
-        c = pair_dot(hid_s[at], w2_s[...])
-        yield
-        new = (last_ref[at].astype(F32) + scaled(c, m_s[...])).astype(BF)
-        edge_out_ref[at] = new
+        at, held_at, col0 = rows_of(s, k, q)
+        c = pair_dot(hid_s[held_at], w2_s[...])
+        yield
+        new = (edge_ref[at].astype(F32) + scaled(c, m_s[...])).astype(BF)
+        edge_ref[at] = new
         loc = loc_s[block(s)]
         back = [
             one_hot(along_lanes(loc[j : j + 1], TILE) == sub)
             for j in range(col0, col0 + part // TILE)
         ]
-        incoming.setdefault(k + base(s), []).append((back, new))
+        incoming.setdefault(k + held(s), []).append((back, new))
         yield
         if q == PARTS - 1:
-            backs, news = zip(*incoming.pop(k + base(s)))
-            row = (base(s) + k) * TILE
+            backs, news = zip(*incoming.pop(k + held(s)))
+            row = (held(s) + k) * TILE
             inc_s[row : row + TILE] = dot(
                 jnp.concatenate(sum(backs, []), axis=1), jnp.concatenate(news, axis=0)
             ).astype(BF)
@@ -166,7 +168,7 @@
     def third(s):
         here = pl.ds(aligned(block(s) * STEP * TILE), STEP * TILE)
         own = own_ref[here]
-        got = inc_s[base(s) * TILE : (base(s) + STEP) * TILE]
+        got = inc_s[held(s) * TILE : (held(s) + STEP) * TILE]
         y = dot(jnp.concatenate([own, got], axis=1), nw1_s[...])
         yield
         c = pair_dot(half_silu(y), nw2_s[...])
@@ -208,83 +210,127 @@
         pl.when(when)(functools.partial(run, *which))
 
 
-def inner_kernel(count, base_ref, edge_ref, last_ref, all_ref, *refs):
+def ready_kernel(base_ref, edge_ref, *refs):
     hbm, refs = refs[:12], refs[12:]
-    edge_out_ref, fine_ref, pool_ref, ws_ref, ends_ref, own_ref, cmap_ref = refs[:7]
-    ready, refs = refs[7:17], refs[17:]
-    vmem, (hid_s, inc_s, sem) = refs[:10], refs[10:]
+    (across_ref, within_ref, ws_ref, edges_ref, own_ref, cmap_ref), refs = refs[:6], refs[6:]
+    ready, vmem, sem = refs[:10], refs[10:20], refs[20]
     send_ref, recv_ref, w1_ref, u_ref, v_ref = vmem[:5]
     edge_w2_ref, node_w1_ref, node_w2_ref, gain_ref, ngain_ref = vmem[5:]
     vmem = (own_ref, cmap_ref) + vmem
     sent_s, recv_s, we_s, w2_s, m_s, nw1_s, nw2_s, nm_s, code_s, loc_s = ready
+    rows, lat = own_ref.shape
+    idx_rows = send_ref.shape[0] // (rows // TILE) * STEP
+    size = idx_rows * TILE
+    copies = [pltpu.make_async_copy(a, b, sem.at[i]) for i, (a, b) in enumerate(zip(hbm, vmem))]
+    order = [4, 5, 6, 0, 10, 11, 7, 9, 3, 2, 8, 1]
+    for i in order:
+        copies[i].start()
+    early = pltpu.make_async_copy(
+        edge_ref.at[pl.ds(size, size)], edges_ref.at[pl.ds(0, size)], sem.at[len(hbm)]
+    )
+    early.start()
+    for i in order[:3]:
+        copies[i].wait()
+    w_eff = w1_ref[...].astype(F32) + lax.dot_general(
+        u_ref[...], v_ref[...], (((0,), (0,)), ((), ())), preferred_element_type=F32
+    )
+    w_eff = (0.5 * w_eff).astype(BF)
+    we_s[...] = twice(w_eff[:lat])
+    ws = w_eff[lat : 2 * lat]
+    ws_ref[...] = ws
+    for i in order[3:]:
+        copies[i].wait()
+    even = base_ref[0] % 2 == 0
+    head, tail = own_ref[:HALO], own_ref[rows - HALO :]
+    across_ref[...] = jnp.where(even, head, tail)
+    within_ref[...] = jnp.where(even, tail, head)
+    both = dot(own_ref[...], jnp.concatenate([ws, w_eff[2 * lat :]], axis=1)).astype(BF)
+    sent_s[...] = both[:, :lat]
+    recv_s[...] = both[:, lat:]
+    w2_s[...] = gained(edge_w2_ref[...], gain_ref[...])
+    m_s[...] = mean_weight(gain_ref[...])
+    nw1_s[...] = node_w1_ref[...] * 0.5
+    nw2_s[...] = gained(node_w2_ref[...], ngain_ref[...])
+    nm_s[...] = mean_square(ngain_ref[...])
+    recv = recv_ref[...]
+    loc = recv & (TILE - 1)
+    off = send_ref[...] - (recv - loc) + HALO
+    hi = off >= LOW * TILE
+    lo = jnp.where(hi, off - LOW * TILE, off)
+    code = lo | (loc << 16) | jnp.where(hi, jnp.int32(-(2**31)), 0)
+    for s in range(rows // TILE // STEP):
+        sl = slice(s * idx_rows, (s + 1) * idx_rows)
+        code_s[s, :, 0:idx_rows] = code[sl].T
+        loc_s[s, 0:idx_rows] = loc[sl]
+    early.wait()
+
+
+def inner_kernel(count, base_ref, all_ref, own_ref, cmap_ref, *refs):
+    ready, refs = refs[:10], refs[11:]
+    edges_ref, edge_out_ref, fine_ref, pool_ref, ends_ref, hid_s, inc_s, sem_in, sem_out = refs
     step = pl.program_id(0)
-    rows, lat = own_ref.shape
-    size = edge_ref.shape[0]
-    idx_rows = size // TILE
+    size = hid_s.shape[0]
+
+    def fetch(n):
+        return pltpu.make_async_copy(
+            all_ref.at[pl.ds((n + 1) * size, size)], edges_ref.at[pl.ds(n * size, size)],
+            sem_in.at[n],
+        )
+
+    def store(n):
+        return pltpu.make_async_copy(
+            edges_ref.at[pl.ds(n * size, size)], edge_out_ref.at[pl.ds((n + 1) * size, size)],
+            sem_out.at[n],
+        )
+
     ends = [
         pltpu.make_async_copy(
             all_ref.at[pl.ds(at * size, size)], ends_ref.at[pl.ds(n * size, size)],
-            sem.at[len(hbm) + n],
+            sem_in.at[count + n],
         )
         for n, at in enumerate((0, count + 1))
     ]
 
     @pl.when(step == 0)
     def _():
-        copies = [pltpu.make_async_copy(a, b, sem.at[i]) for i, (a, b) in enumerate(zip(hbm, vmem))]
-        for c in copies + ends:
+        for n in range(1, count):
+            fetch(n).start()
+        for c in ends:
             c.start()
-        for c in copies:
-            c.wait()
-        w_eff = w1_ref[...].astype(F32) + lax.dot_general(
-            u_ref[...], v_ref[...], (((0,), (0,)), ((), ())), preferred_element_type=F32
-        )
-        w_eff = (0.5 * w_eff).astype(BF)
-        we_s[...] = twice(w_eff[:lat])
-        ws = w_eff[lat : 2 * lat]
-        ws_ref[...] = ws
-        both = dot(own_ref[...], jnp.concatenate([ws, w_eff[2 * lat :]], axis=1)).astype(BF)
-        sent_s[...] = both[:, :lat]
-        recv_s[...] = both[:, lat:]
-        w2_s[...] = gained(edge_w2_ref[...], gain_ref[...])
-        m_s[...] = mean_weight(gain_ref[...])
-        nw1_s[...] = node_w1_ref[...] * 0.5
-        nw2_s[...] = gained(node_w2_ref[...], ngain_ref[...])
-        nm_s[...] = mean_square(ngain_ref[...])
         pool_ref[...] = jnp.zeros_like(pool_ref)
-        recv = recv_ref[...]
-        loc = recv & (TILE - 1)
-        off = send_ref[...] - (recv - loc) + HALO
-        hi = off >= LOW * TILE
-        lo = jnp.where(hi, off - LOW * TILE, off)
-        code = lo | (loc << 16) | jnp.where(hi, jnp.int32(-(2**31)), 0)
-        for s in range(rows // TILE // STEP):
-            sl = slice(s * idx_rows, (s + 1) * idx_rows)
-            code_s[s, :, 0:idx_rows] = code[sl].T
-            loc_s[s, 0:idx_rows] = loc[sl]
+
+    @pl.when((step > 0) & (step < count))
+    def _():
+        fetch(step).wait()
 
     run_stages(
         step, count,
         make_stages(
-            lambda s: s + 1, lambda s: (s + 1) * STEP * TILE - HALO, lambda s: 0,
-            (edge_ref, last_ref, edge_out_ref, own_ref, cmap_ref, fine_ref) + ready
+            lambda s: s + 1, lambda s: (s + 1) * STEP * TILE - HALO, lambda s: s * STEP,
+            lambda s: 0,
+            (edges_ref, own_ref, cmap_ref, fine_ref) + ready
             + (hid_s, inc_s, pool_ref, size // STEP),
             base_ref,
         ),
     )
 
+    @pl.when((step > 0) & (step < count))
+    def _():
+        store(step - 1).start()
+
     @pl.when(step == count + 1)
     def _():
+        for n in range(count - 1):
+            store(n).wait()
         for c in ends:
             c.wait()
 
 
 def border_kernel(
-    last_block, base_ref, ends_ref, own_ref, across_ref, within_ref, cmap_ref, pool_ref,
-    ws_ref, *refs
+    last_block, base_ref, own_ref, across_ref, within_ref, cmap_ref, pool_ref, ws_ref, *refs
 ):
     ready, refs = refs[:10], refs[12:]
-    edge_out_ref, fine_ref, coarse_ref, win_s, out_s, hid_s, inc_s, pool_s, sem = refs
+    ends_ref, fine_ref, coarse_ref, win_s, hid_s, inc_s, pool_s = refs
     sent_ref = ready[0]
     rows, lat = sent_ref.shape
     size = ends_ref.shape[0] // 2
@@ -299,24 +345,11 @@
     win_s[span + inside :] = dot(jnp.where(even, within, across), ws).astype(BF)
     pool_s[...] = pool_ref[...]
     first, second, third = make_stages(
-        lambda s: s * last_block, lambda s: s * span, lambda s: s * STEP,
-        (ends_ref, ends_ref, out_s, own_ref, cmap_ref, fine_ref, win_s) + ready[1:]
+        lambda s: s * last_block, lambda s: s * span, lambda s: s * STEP, lambda s: s * STEP,
+        (ends_ref, own_ref, cmap_ref, fine_ref, win_s) + ready[1:]
         + (hid_s, inc_s, pool_s, size // STEP),
         base_ref,
     )
-    copies = []
-
-    def send(s):
-        copies.append(
-            pltpu.make_async_copy(
-                out_s.at[pl.ds(s * size, size)],
-                edge_out_ref.at[pl.ds(s * last_block * size, size)],
-                sem.at[s],
-            )
-        )
-        copies[-1].start()
-        yield
-
     parts = [(s, k, q) for s in range(2) for k in range(STEP) for q in range(PARTS)]
     half = STEP * PARTS
     ticks = [[] for _ in range(2 * half + 8)]
@@ -325,15 +358,31 @@
         ticks[n + 2].insert(0, second(*p))
     for s in range(2):
         done = (s + 1) * half + 1 + 3
-        ticks[done] += [send(s), third(s)]
+        ticks[done].append(third(s))
     interleave(ticks, [])
     total = pool_s[...]
     coarse_ref[...] = (total[:, :lat] / jnp.maximum(total[:, lat:], 1.0)).astype(BF)
+
+
+def near_kernel(
+    last_block, base_ref, send_ref, recv_ref, own_ref, w1_ref, edges_ref, ends_ref, _, pre_ref,
+    edge_out_ref, sem
+):
+    size = ends_ref.shape[0] // 2
+    copies = [
+        pltpu.make_async_copy(
+            source.at[pl.ds(row, size)], edge_out_ref.at[pl.ds(at * size, size)], sem.at[n]
+        )
+        for n, (source, row, at) in enumerate(
+            (
+                (ends_ref, 0, 0),
+                (ends_ref, size, last_block),
+                (edges_ref, edges_ref.shape[0] - size, last_block - 1),
+            )
+        )
+    ]
     for c in copies:
-        c.wait()
-
-
-def near_kernel(base_ref, send_ref, recv_ref, own_ref, w1_ref, pre_ref):
+        c.start()
     crows, lat = own_ref.shape
     rows = send_ref.shape[0]
     first = base_ref[0] * crows
@@ -358,6 +407,8 @@
         pre_ref[g * TILE : (g + group) * TILE] = out
 
     interleave([[part(g)] for g in range(0, rows, group)], [])
+    for c in copies:
+        c.wait()
 
 
 def coarse_kernel(
@@ -461,16 +512,6 @@
     per = edges // tiles
     crows = nodes // COARSEN
     steps = tiles // STEP
-    even = dev[0] % 2 == 0
-    ends = (node_latent[:HALO], node_latent[nodes - HALO :])
-    across = [(i, i + 1) for i in range(1, size - 1, 2)]
-    within = [(i, i + 1) for i in range(0, size, 2)]
-    across = lax.ppermute(
-        jnp.where(even, ends[0], ends[1]), axes, across + [(j, i) for i, j in across]
-    )
-    within = lax.ppermute(
-        jnp.where(even, ends[1], ends[0]), axes, within + [(j, i) for i, j in within]
-    )
     cmap2 = coarse_map.reshape(tiles, TILE)
     vm = pl.BlockSpec(memory_space=pltpu.VMEM)
     sm = pl.BlockSpec(memory_space=pltpu.SMEM)
@@ -485,7 +526,6 @@
     far = apart(edge_latent)
     count = steps - 2
     full = jax.ShapeDtypeStruct((edges, lat), BF)
-    inner_block = lambda i: (jnp.clip(i, 0, count - 1) + 1, 0)
     ready = [
         jax.ShapeDtypeStruct(shape, dtype)
         for shape, dtype in [((nodes, lat), BF)] * 2
@@ -493,53 +533,69 @@
         + [((1, lat), F32), ((2 * lat, lat), BF), ((2 * lat, 2 * lat), BF), ((2 * lat, 2 * lat), BF)]
         + [((steps, TILE, PAD), jnp.int32), ((steps, PAD, TILE), jnp.int32)]
     ]
-    edge_out, fine, pool, ws, ends, own, cmap2, *ready = pl.pallas_call(
+    shape = jax.ShapeDtypeStruct
+    params = pltpu.CompilerParams(vmem_limit_bytes=24 * 2**20)
+    rows = STEP * per
+    across, within, ws, inner_edges, own, cmap2, *ready = pl.pallas_call(
+        ready_kernel,
+        in_specs=[sm] + [hb] * (1 + len(hbm)),
+        out_specs=[vm] * (6 + len(ready)),
+        out_shape=[
+            shape((HALO, lat), BF),
+            shape((HALO, lat), BF),
+            shape((lat, lat), BF),
+            shape((count * rows, lat), BF),
+            shape((nodes, lat), BF),
+            shape(cmap2.shape, cmap2.dtype),
+        ] + ready,
+        scratch_shapes=[pltpu.VMEM(a.shape, a.dtype) for a in hbm[2:]]
+        + [pltpu.SemaphoreType.DMA((len(hbm) + 1,))],
+        compiler_params=params,
+        name="ready",
+    )(dev, far, *[apart(a) for a in hbm])
+    pairs = [(i, i + 1) for i in range(1, size - 1, 2)]
+    across = lax.ppermute(across, axes, pairs + [(j, i) for i, j in pairs])
+    pairs = [(i, i + 1) for i in range(0, size, 2)]
+    within = lax.ppermute(within, axes, pairs + [(j, i) for i, j in pairs])
+    inner_edges, edge_out, fine, pool, ends = pl.pallas_call(
         functools.partial(inner_kernel, count),
         grid=(count + 2,),
-        in_specs=[
-            sm,
-            pl.BlockSpec(big, inner_block),
-            pl.BlockSpec(big, lambda i: inner_block(i - 1)),
-        ] + [hb] * (1 + len(hbm)),
-        out_specs=[pl.BlockSpec(big, lambda i: inner_block(i - 1))] + [vm] * (6 + len(ready)),
+        in_specs=[sm, hb] + [vm] * (3 + len(ready)),
+        out_specs=[vm, hb, vm, vm, vm],
         out_shape=[
+            shape((count * rows, lat), BF),
             full,
-            jax.ShapeDtypeStruct((nodes, lat), BF),
-            jax.ShapeDtypeStruct((crows, 2 * lat), F32),
-            jax.ShapeDtypeStruct((lat, lat), BF),
-            jax.ShapeDtypeStruct((2 * STEP * per, lat), BF),
-            jax.ShapeDtypeStruct((nodes, lat), BF),
-            jax.ShapeDtypeStruct(cmap2.shape, cmap2.dtype),
-        ] + ready,
-        scratch_shapes=[pltpu.VMEM(a.shape, a.dtype) for a in hbm[2:]]
-        + [pltpu.VMEM(big, BF), pltpu.VMEM((STEP * TILE, lat), BF)]
-        + [pltpu.SemaphoreType.DMA((len(hbm) + 2,))],
+            shape((nodes, lat), BF),
+            shape((crows, 2 * lat), F32),
+            shape((2 * rows, lat), BF),
+        ],
+        input_output_aliases={4 + len(ready): 0},
+        scratch_shapes=[
+            pltpu.VMEM((rows, lat), BF),
+            pltpu.VMEM((STEP * TILE, lat), BF),
+            pltpu.SemaphoreType.DMA((count + 2,)),
+            pltpu.SemaphoreType.DMA((count,)),
+        ],
         compiler_params=pltpu.CompilerParams(
             dimension_semantics=("arbitrary",), vmem_limit_bytes=24 * 2**20
         ),
         name="inner",
-    )(dev, far, far, far, *[apart(a) for a in hbm])
-    edge_out, fine, coarse = pl.pallas_call(
+    )(dev, far, own, cmap2, *ready, inner_edges)
+    ends, fine, coarse = pl.pallas_call(
         functools.partial(border_kernel, steps - 1),
-        in_specs=[sm] + [vm] * (7 + len(ready)) + [hb, vm],
-        out_specs=[hb, vm, vm],
-        out_shape=[
-            full,
-            jax.ShapeDtypeStruct((nodes, lat), BF),
-            jax.ShapeDtypeStruct((crows, lat), BF),
-        ],
-        input_output_aliases={8 + len(ready): 0, 9 + len(ready): 1},
+        in_specs=[sm] + [vm] * (8 + len(ready)),
+        out_specs=[vm] * 3,
+        out_shape=[shape((2 * rows, lat), BF), shape((nodes, lat), BF), shape((crows, lat), BF)],
+        input_output_aliases={7 + len(ready): 0, 8 + len(ready): 1},
         scratch_shapes=[
             pltpu.VMEM((2 * (STEP * TILE + 2 * HALO), lat), BF),
-            pltpu.VMEM((2 * STEP * per, lat), BF),
-            pltpu.VMEM((2 * STEP * per, lat), BF),
+            pltpu.VMEM((2 * rows, lat), BF),
             pltpu.VMEM((2 * STEP * TILE, lat), BF),
             pltpu.VMEM((crows, 2 * lat), F32),
-            pltpu.SemaphoreType.DMA((2,)),
         ],
-        compiler_params=pltpu.CompilerParams(vmem_limit_bytes=24 * 2**20),
+        compiler_params=params,
         name="border",
-    )(dev, ends, own, across, within, cmap2, pool, ws, *ready, edge_out, fine)
+    )(dev, own, across, within, cmap2, pool, ws, *ready, ends, fine)
     tables = [coarse]
     bit = 1
     while bit < size:
@@ -548,14 +604,16 @@
     cedges = coarse_send.shape[0]
     csend2 = coarse_send.reshape(cedges // TILE, TILE)
     crecv2 = coarse_recv.reshape(cedges // TILE, TILE)
-    pre = pl.pallas_call(
-        near_kernel,
-        in_specs=[sm] + [vm] * 4,
-        out_specs=vm,
-        out_shape=jax.ShapeDtypeStruct((cedges, lat), F32),
-        compiler_params=pltpu.CompilerParams(vmem_limit_bytes=32 * 2**20),
+    pre, edge_out = pl.pallas_call(
+        functools.partial(near_kernel, steps - 1),
+        in_specs=[sm] + [vm] * 6 + [hb],
+        out_specs=[vm, hb],
+        out_shape=[shape((cedges, lat), F32), full],
+        input_output_aliases={7: 1},
+        scratch_shapes=[pltpu.SemaphoreType.DMA((3,))],
+        compiler_params=params,
         name="near",
-    )(dev, csend2, crecv2, coarse, coarse_w1)
+    )(dev, csend2, crecv2, coarse, coarse_w1, inner_edges, ends, edge_out)
     node_out = pl.pallas_call(
         coarse_kernel,
         in_specs=[sm] + [vm] * (8 + len(tables)),

time: 40.7 us -> 37.9 us (0.931)
  Pallas kernels: 26.1 us -> 24.4 us
  other arithmetic: 0.89 us -> 0 us
  waiting for transfers between devices: 2.68 us -> 3.22 us
  starting transfers between devices: 9.78 us -> 9.32 us
    ppermute x4, starting transfers between devices: 8.61 us -> 4.26 us  [on_device(): lax.ppermute(coarse, axes, [(i, i ^ bit) for i in range(size)])]
    ppermute x2, starting transfers between devices: 1.17 us -> 5.06 us  [the longest x1 4.39 us: on_device(): within = lax.ppermute(within, axes, pairs + [(j, i) for i, j in pairs])]
    pallas_call x1, Pallas kernels: 17.3 us -> 13.7 us  [on_device(): pl.pallas_call(functools.partial(inner_kernel, count), grid=(count + 2,),...]
    pallas_call x1 -> x2, Pallas kernels: 1.3 us -> 3.38 us  [the longest x1 2.04 us: on_device(): pl.pallas_call(ready_kernel, in_specs=[sm] + [hb] * (1 + len(hbm)), out_s...]
    select_n x1 -> x0, other arithmetic: 0.89 us -> none  [on_device(): jnp.where(even, ends[1], ends[0])]
    ppermute x4, waiting for transfers between devices: 2.67 us -> 3.21 us  [on_device(): lax.ppermute(coarse, axes, [(i, i ^ bit) for i in range(size)])]
  transfers between devices with their start and end apart: 6 -> 6, of which waited for: 3 -> 3; matrix products, arithmetic and copies ran while one was open for 0% -> 0% of each run, Pallas kernels for 46% -> 40%
where the time goes in v5:
time: 37.9 us; the launch traced here: 37.8 us
  Pallas kernels  24.4 us (64%)
  starting transfers between devices  9.32 us (25%)
  waiting for transfers between devices  3.22 us (8%)
  between operations  0.76 us (2%)
    pallas_call x1, Pallas kernels, on_device(): pl.pallas_call(functools.partial(inner_kernel, count), grid=(count + 2,),...  13.7 us
    ppermute x1, starting transfers between devices, on_device(): within = lax.ppermute(within, axes, pairs + [(j, i) for i, j in pairs])  4.39 us
    pallas_call x1, Pallas kernels, on_device(): pl.pallas_call(coarse_kernel, in_specs=[sm] + [vm] * (8 + len(tables)), o...  4.32 us
    ppermute x4, starting transfers between devices, on_device(): lax.ppermute(coarse, axes, [(i, i ^ bit) for i in range(size)])  4.26 us
    ppermute x4, waiting for transfers between devices, on_device(): lax.ppermute(coarse, axes, [(i, i ^ bit) for i in range(size)])  3.21 us
    pallas_call x1, Pallas kernels, on_device(): pl.pallas_call(functools.partial(border_kernel, steps - 1), in_specs=[sm]...  3.02 us
    pallas_call x1, Pallas kernels, on_device(): pl.pallas_call(ready_kernel, in_specs=[sm] + [hb] * (1 + len(hbm)), out_s...  2.04 us
    pallas_call x1, Pallas kernels, on_device(): pl.pallas_call(functools.partial(near_kernel, steps - 1), in_specs=[sm] +...  1.34 us
  transfers between devices with their start and end apart: 6, of which 3 were waited for; matrix products, arithmetic and copies ran while one was open for 0% of the time, Pallas kernels for 40%

profile of v5, /device:TPU:0, one launch (start us, length us, event | category | flops | bytes accessed | tf_op | source)
XLA Modules:
  0.0 37.8 jit_solution(922484362723002507)
XLA Ops:
  0.6 2.0 %ready.1 = (bf16[256,128]{1,0:T(8,128)(2,1)S(1)}, bf16[256,128]{1,0:T(8,128)(2,1)S(1)}, bf16[128,128]{1,0:T(8,128)(2,1)S(1)}, bf16[15360,128]{1,0:T(8,128)(2,1)S...) custom-call(s32[1]{0:T(128)} %bitcast.base_ref, ...), custom_call_target="tpu_custom_call" | custom-call | tf_op jit(solution)/shard_map/ready/pallas_call | solution.py:539
  2.7 0.7 %collective-permute-start = (bf16[256,128]{1,0:T(8,128)(2,1)S(1)}, bf16[256,128]{1,0:T(8,128)(2,1)S(1)}, u32[]{:S(2)}, u32[]{:S(2)}) collective-permute-start(bf16[256,128]{1,0:T(8,128)(2,1)S(1)} %get-tuple-element.30), channel_id=1, source_target_pairs={{1,2},{3,4},{5,6},{7,8},{9,10},{11,12},{13,14},{2,1},{4,3},{6,5},{... | collective-permute-start | bytes 196616 | tf_op jit(solution)/shard_map/ppermute | solution.py:557
  3.4 4.4 %collective-permute-start.1 = (bf16[256,128]{1,0:T(8,128)(2,1)S(1)}, bf16[256,128]{1,0:T(8,128)(2,1)S(1)}, u32[]{:S(2)}, u32[]{:S(2)}) collective-permute-start(bf16[256,128]{1,0:T(8,128)(2,1)S(1)} %get-tuple-element.31), channel_id=1, source_target_pairs={{0,1},{2,3},{4,5},{6,7},{8,9},{10,11},{12,13},{14,15},{1,0},{3,2},... | collective-permute-start | bytes 196616 | tf_op jit(solution)/shard_map/ppermute | solution.py:559
  7.8 13.7 %inner.1 = (bf16[15360,128]{1,0:T(8,128)(2,1)S(1)}, bf16[18432,128]{1,0:T(8,128)(2,1)}, bf16[3072,128]{1,0:T(8,128)(2,1)S(1)}, f32[384,256]{1,0:T(8,128)S(1)}, bf16[3072,128]{1,0:T(8,128)(2,1)S(1)}) custom-call(s32[1]{0:T(128)} %bitcast.base_ref, bf16[18432,128]{1,0:T(8,128)(2,1)} %all_ref.1, ...), custom_call_target="tpu_custom_call", output_to_operand_aliasing={{0}: (14, {})} | custom-call | tf_op jit(solution)/shard_map/inner/pallas_call | solution.py:560
  21.5 0.0 copy-start
  21.5 0.0 copy-start.1
  21.5 0.0 copy-start.2
  21.5 0.0 collective-permute-done.across_ref
  21.5 0.0 collective-permute-done.1.within_ref
  21.5 3.0 %border.1 = (bf16[3072,128]{1,0:T(8,128)(2,1)S(1)}, bf16[3072,128]{1,0:T(8,128)(2,1)S(1)}, bf16[384,128]{1,0:T(8,128)(2,1)S(1)}) custom-call(s32[1]{0:T(128)} %bitcast.base_ref, bf16[3072,128]{1,0:T(8,128)(2,1)S(1)} %get-tuple-element.29.own_ref, ...), custom_call_target="tpu_custom_call", output_to_operand_aliasing={{0}: (17, {}), {1}: (18, {})} | custom-call | tf_op jit(solution)/shard_map/border/pallas_call | solution.py:584
  24.6 2.7 %collective-permute-start.5 = (bf16[384,128]{1,0:T(8,128)(2,1)S(1)}, bf16[384,128]{1,0:T(8,128)(2,1)S(1)}, u32[]{:S(2)}, u32[]{:S(2)}) collective-permute-start(bf16[384,128]{1,0:T(8,128)(2,1)S(1)} %get-tuple-element.48.own_ref.refs_0_), channel_id=1, source_target_pairs={{0,8},{1,9},{2,10},{3,11},{4,12},{5,13},{6,14},{7,15},{8,0},{9,1},... | collective-permute-start | bytes 294920 | tf_op jit(solution)/shard_map/ppermute | solution.py:602
  27.2 1.6 %collective-permute-start.4 = (bf16[384,128]{1,0:T(8,128)(2,1)S(1)}, bf16[384,128]{1,0:T(8,128)(2,1)S(1)}, u32[]{:S(2)}, u32[]{:S(2)}) collective-permute-start(bf16[384,128]{1,0:T(8,128)(2,1)S(1)} %get-tuple-element.48.own_ref.refs_0_), channel_id=1, source_target_pairs={{0,4},{1,5},{2,6},{3,7},{4,0},{5,1},{6,2},{7,3},{8,12},{9,13},{10,... | collective-permute-start | bytes 294920 | tf_op jit(solution)/shard_map/ppermute | solution.py:602
  28.8 0.0 collective-permute-start.3
  28.8 0.0 collective-permute-start.2
  28.8 0.0 copy-done
  28.8 0.0 copy-done.1
  28.9 0.0 copy-done.2
  28.9 0.0 copy-start.3
  28.9 0.0 copy-start.4
  28.9 1.3 %near.1 = (f32[2304,128]{1,0:T(8,128)S(1)}, bf16[18432,128]{1,0:T(8,128)(2,1)}) custom-call(s32[1]{0:T(128)} %bitcast.base_ref, s32[18,128]{1,0:T(8,128)S(1)} %bitcast.10, s32[18,128]{1,0:T(8,128)S(1)} %bitcast.12, bf16[384,128]{1,0:T(8,128)(2,1)S(1)} %get-tuple-element.48.own_ref.refs_0_, ...), custom_call_target="tpu_custom_call", output_to_operand_aliasing={{1}: (7, {})} | custom-call | tf_op jit(solution)/shard_map/near/pallas_call | solution.py:607
  30.2 2.3 %collective-permute-done.5.refs_4_ = bf16[384,128]{1,0:T(8,128)(2,1)S(1)} collective-permute-done((bf16[384,128]{1,0:T(8,128)(2,1)S(1)}, bf16[384,128]{1,0:T(8,128)(2,1)S(1)}, u32[]{:S(2)}, u32[]{:S(2)}) %collective-permute-start.5) | collective-permute-done | bytes 98336 | tf_op jit(solution)/shard_map/ppermute | solution.py:602
  32.5 0.2 collective-permute-done.4.refs_3_
  32.7 0.7 %collective-permute-done.3.refs_2_ = bf16[384,128]{1,0:T(8,128)(2,1)S(1)} collective-permute-done((bf16[384,128]{1,0:T(8,128)(2,1)S(1)}, bf16[384,128]{1,0:T(8,128)(2,1)S(1)}, u32[]{:S(2)}, u32[]{:S(2)}) %collective-permute-start.3) | collective-permute-done | bytes 98336 | tf_op jit(solution)/shard_map/ppermute | solution.py:602
  33.5 0.0 collective-permute-done.2.refs_1_
  33.5 0.0 copy-done.3
  33.5 0.0 copy-done.4
  33.5 4.3 %coarse.1 = bf16[3072,128]{1,0:T(8,128)(2,1)} custom-call(s32[1]{0:T(128)} %bitcast.base_ref, s32[18,128]{1,0:T(8,128)S(1)} %bitcast.11, s32[18,128]{1,0:T(8,128)S(1)} %bitcast.13, s32[24,128]{1,0:T(8,128)S(1)} %get-tuple-element.28.cmap_ref, bf16[3072,128]{1,0:T(8,128)(2,1)S(1)} %get-tuple-element.47.fine_ref, f32[2304,128]{1,0:T(8,128)S(1)} %get-tuple-element.52.pre_ref, ...), custom_call_target="tpu_custom_call" | custom-call | tf_op jit(solution)/shard_map/coarse/pallas_call | solution.py:617
Async XLA Ops:
  2.7 18.8 %collective-permute-start = (bf16[256,128]{1,0:T(8,128)(2,1)S(1)}, bf16[256,128]{1,0:T(8,128)(2,1)S(1)}, u32[]{:S(2)}, u32[]{:S(2)}) collective-permute-start(bf16[256,128]{1,0:T(8,128)(2,1)S(1)} %get-tuple-element.30), channel_id=1, source_target_pairs={{1,2},{3,4},{5,6},{7,8},{9,10},{11,12},{13,14},{2,1},{4,3},{6,5},{... | collective-permute-start | bytes 196616 | tf_op jit(solution)/shard_map/ppermute | solution.py:557
  3.4 18.2 %collective-permute-start.1 = (bf16[256,128]{1,0:T(8,128)(2,1)S(1)}, bf16[256,128]{1,0:T(8,128)(2,1)S(1)}, u32[]{:S(2)}, u32[]{:S(2)}) collective-permute-start(bf16[256,128]{1,0:T(8,128)(2,1)S(1)} %get-tuple-element.31), channel_id=1, source_target_pairs={{0,1},{2,3},{4,5},{6,7},{8,9},{10,11},{12,13},{14,15},{1,0},{3,2},... | collective-permute-start | bytes 196616 | tf_op jit(solution)/shard_map/ppermute | solution.py:559
  21.5 7.4 %copy-start = (bf16[256,128]{1,0:T(8,128)(2,1)S(1)}, bf16[256,128]{1,0:T(8,128)(2,1)}, u32[]{:S(2)}) copy-start(bf16[256,128]{1,0:T(8,128)(2,1)} %w1_ref.3) | copy-start | bytes 196612
  21.5 7.3 %copy-start.1 = (s32[2304]{0:T(1024)S(1)}, s32[2304]{0:T(1024)}, u32[]{:S(2)}) copy-start(s32[2304]{0:T(1024)} %param.24) | copy-start | bytes 27652
  21.5 7.3 %copy-start.2 = (s32[2304]{0:T(1024)S(1)}, s32[2304]{0:T(1024)}, u32[]{:S(2)}) copy-start(s32[2304]{0:T(1024)} %param.23) | copy-start | bytes 27652
  24.6 7.9 %collective-permute-start.5 = (bf16[384,128]{1,0:T(8,128)(2,1)S(1)}, bf16[384,128]{1,0:T(8,128)(2,1)S(1)}, u32[]{:S(2)}, u32[]{:S(2)}) collective-permute-start(bf16[384,128]{1,0:T(8,128)(2,1)S(1)} %get-tuple-element.48.own_ref.refs_0_), channel_id=1, source_target_pairs={{0,8},{1,9},{2,10},{3,11},{4,12},{5,13},{6,14},{7,15},{8,0},{9,1},... | collective-permute-start | bytes 294920 | tf_op jit(solution)/shard_map/ppermute | solution.py:602
  27.2 5.5 %collective-permute-start.4 = (bf16[384,128]{1,0:T(8,128)(2,1)S(1)}, bf16[384,128]{1,0:T(8,128)(2,1)S(1)}, u32[]{:S(2)}, u32[]{:S(2)}) collective-permute-start(bf16[384,128]{1,0:T(8,128)(2,1)S(1)} %get-tuple-element.48.own_ref.refs_0_), channel_id=1, source_target_pairs={{0,4},{1,5},{2,6},{3,7},{4,0},{5,1},{6,2},{7,3},{8,12},{9,13},{10,... | collective-permute-start | bytes 294920 | tf_op jit(solution)/shard_map/ppermute | solution.py:602
  28.8 4.6 %collective-permute-start.3 = (bf16[384,128]{1,0:T(8,128)(2,1)S(1)}, bf16[384,128]{1,0:T(8,128)(2,1)S(1)}, u32[]{:S(2)}, u32[]{:S(2)}) collective-permute-start(bf16[384,128]{1,0:T(8,128)(2,1)S(1)} %get-tuple-element.48.own_ref.refs_0_), channel_id=1, source_target_pairs={{0,2},{1,3},{2,0},{3,1},{4,6},{5,7},{6,4},{7,5},{8,10},{9,11},{10,... | collective-permute-start | bytes 294920 | tf_op jit(solution)/shard_map/ppermute | solution.py:602
  28.8 4.6 %collective-permute-start.2 = (bf16[384,128]{1,0:T(8,128)(2,1)S(1)}, bf16[384,128]{1,0:T(8,128)(2,1)S(1)}, u32[]{:S(2)}, u32[]{:S(2)}) collective-permute-start(bf16[384,128]{1,0:T(8,128)(2,1)S(1)} %get-tuple-element.48.own_ref.refs_0_), channel_id=1, source_target_pairs={{0,1},{1,0},{2,3},{3,2},{4,5},{5,4},{6,7},{7,6},{8,9},{9,8},{10,11... | collective-permute-start | bytes 294920 | tf_op jit(solution)/shard_map/ppermute | solution.py:602
  28.9 4.6 %copy-start.3 = (bf16[128,128]{1,0:T(8,128)(2,1)S(1)}, bf16[128,128]{1,0:T(8,128)(2,1)}, u32[]{:S(2)}) copy-start(bf16[128,128]{1,0:T(8,128)(2,1)} %w2_ref.1) | copy-start | bytes 98308
  28.9 4.6 %copy-start.4 = (f32[128]{0:T(128)S(1)}, f32[128]{0:T(128)}, u32[]{:S(2)}) copy-start(f32[128]{0:T(128)} %param.35) | copy-start | bytes 1540

commit v6 on v5

--- a/solution.py
+++ b/solution.py
@@ -355,18 +355,27 @@
     ticks = [[] for _ in range(2 * half + 8)]
     for n, p in enumerate(parts):
         ticks[n].append(first(*p))
-        ticks[n + 2].insert(0, second(*p))
+        ticks[n + 3].insert(0, second(*p))
     for s in range(2):
-        done = (s + 1) * half + 1 + 3
+        done = (s + 1) * half + 5
         ticks[done].append(third(s))
     interleave(ticks, [])
     total = pool_s[...]
     coarse_ref[...] = (total[:, :lat] / jnp.maximum(total[:, lat:], 1.0)).astype(BF)
 
 
+def half_blocks(blocks):
+    return (blocks + 1) // 2
+
+
+def in_halves(row, half):
+    hi = row >= half * TILE
+    return jnp.where(hi, (row - half * TILE) | jnp.int32(-(2**31)), row)
+
+
 def near_kernel(
-    last_block, base_ref, send_ref, recv_ref, own_ref, w1_ref, edges_ref, ends_ref, _, pre_ref,
-    edge_out_ref, sem
+    last_block, partners, base_ref, send_ref, recv_ref, cmap_ref, own_ref, w1_ref, edges_ref,
+    ends_ref, _, pre_ref, edge_out_ref, far_ref, spread_ref, sem
 ):
     size = ends_ref.shape[0] // 2
     copies = [
@@ -385,9 +394,20 @@
         c.start()
     crows, lat = own_ref.shape
     rows = send_ref.shape[0]
+    tiles = cmap_ref.shape[0]
     first = base_ref[0] * crows
     blocks = crows // TILE
-    send = send_ref[...] - first
+    half, lows = half_blocks(blocks), half_blocks(blocks * partners)
+    send = send_ref[...]
+    owner = lax.div(send, jnp.full_like(send, crows))
+    other = owner ^ base_ref[0]
+    slot = jnp.full_like(send, -1)
+    for j in range(partners):
+        slot = jnp.where(other == (1 << j), j, slot)
+    far = in_halves(jnp.where(slot < 0, 2 * lows * TILE, send - owner * crows + slot * crows), lows)
+    far_t = far.T
+    spread_t = in_halves(cmap_ref[...] - first, half).T
+    send = send - first
     mine = (send >= 0) & (send < crows)
     code_t = (jnp.where(mine, send, crows) | ((recv_ref[...] - first) << 16)).T
     w1 = w1_ref[...] * 0.5
@@ -405,6 +425,10 @@
         out = dot(jnp.concatenate(lhs, axis=0), rhs)
         yield
         pre_ref[g * TILE : (g + group) * TILE] = out
+        for col in range(g, g + group):
+            far_ref[col * TILE : (col + 1) * TILE] = column(far_t, col)
+        for col in range(g * tiles // rows, (g + group) * tiles // rows):
+            spread_ref[col * TILE : (col + 1) * TILE] = column(spread_t, col)
 
     interleave([[part(g)] for g in range(0, rows, group)], [])
     for c in copies:
@@ -412,28 +436,15 @@
 
 
 def coarse_kernel(
-    base_ref, send_ref, recv_ref, cmap_ref, fine_ref, pre_ref, w1_ref, w2_ref, gain_ref, *refs
+    base_ref, recv_ref, far_ref, spread_ref, fine_ref, pre_ref, w1_ref, w2_ref, gain_ref, *refs
 ):
     (own_ref, *tables), (out_ref, out_s, sem) = refs[:-3], refs[-3:]
     dev = base_ref[0]
     crows, lat = own_ref.shape
-    rows = send_ref.shape[0]
+    rows = recv_ref.shape[0]
     nodes = fine_ref.shape[0]
     chunks = crows // TILE
-    blocks = chunks * len(tables)
-    lows = (blocks + 1) // 2
-    send = send_ref[...]
-    owner = lax.div(send, jnp.full_like(send, crows))
-    other = owner ^ dev
-    slot = jnp.full_like(send, -1)
-    for j in range(len(tables)):
-        slot = jnp.where(other == (1 << j), j, slot)
-    off = send - owner * crows + slot * crows
-    hi = off >= lows * TILE
-    lo = jnp.where(hi, off - lows * TILE, off)
-    code_t = jnp.where(
-        slot < 0, lows * TILE, lo | jnp.where(hi, jnp.int32(-(2**31)), 0)
-    ).T
+    lows = half_blocks(chunks * len(tables))
     loc = recv_ref[...] - dev * crows
     w1 = twice(w1_ref[:lat] * 0.5)
     proj = jnp.concatenate([pair_dot(t[...], w1).astype(BF) for t in tables], axis=0)
@@ -444,13 +455,13 @@
     lane = lax.broadcasted_iota(I16, (TILE, TILE), 1)
     csub = lax.broadcasted_iota(I16, (crows, TILE), 0)
     w2 = twice(w2_ref[...])
-    group = 2 if rows % 2 == 0 else 1
+    group = 6 if rows % 6 == 0 else 1
     total = [own_ref[...].astype(F32)]
 
     def part(g):
         lhs, upper = [], []
         for col in range(g, g + group):
-            word = column(code_t, col)
+            word = far_ref[col * TILE : (col + 1) * TILE]
             lhs.append(jnp.concatenate(pick(word.astype(I16), lane, lows), axis=1))
             upper.append(word < 0)
         out = dot(jnp.concatenate(lhs, axis=0), rhs)
@@ -467,14 +478,11 @@
     centred = total - jnp.mean(total, axis=1, keepdims=True)
     var = jnp.mean(centred * centred, axis=1, keepdims=True)
     delta = (centred * lax.rsqrt(var + 1e-05) * gain_ref[...]).astype(BF)
-    half = (chunks + 1) // 2
+    half = half_blocks(chunks)
     high = delta[half * TILE :]
     if high.shape[0] < half * TILE:
         high = jnp.concatenate([high, delta[high.shape[0] : half * TILE]], axis=0)
     rhs = jnp.concatenate([delta[: half * TILE], high], axis=1)
-    cm = cmap_ref[...] - dev * crows
-    hi = cm >= half * TILE
-    cm_t = (jnp.where(hi, cm - half * TILE, cm) | jnp.where(hi, jnp.int32(-(2**31)), 0)).T
     tiles = nodes // TILE
     size = 4 if tiles % 4 == 0 else 1
     copies = []
@@ -482,7 +490,7 @@
     def spread(p):
         hot, upper = [], []
         for t in range(p, p + size):
-            word = column(cm_t, t)
+            word = spread_ref[t * TILE : (t + 1) * TILE]
             hot.append(jnp.concatenate(pick(word.astype(I16), lane, half), axis=1))
             upper.append(word < 0)
         out = dot(jnp.concatenate(hot, axis=0), rhs)
@@ -604,16 +612,21 @@
     cedges = coarse_send.shape[0]
     csend2 = coarse_send.reshape(cedges // TILE, TILE)
     crecv2 = coarse_recv.reshape(cedges // TILE, TILE)
-    pre, edge_out = pl.pallas_call(
-        functools.partial(near_kernel, steps - 1),
-        in_specs=[sm] + [vm] * 6 + [hb],
-        out_specs=[vm, hb],
-        out_shape=[shape((cedges, lat), F32), full],
-        input_output_aliases={7: 1},
+    pre, edge_out, far_words, spread_words = pl.pallas_call(
+        functools.partial(near_kernel, steps - 1, len(tables) - 1),
+        in_specs=[sm] + [vm] * 7 + [hb],
+        out_specs=[vm, hb, vm, vm],
+        out_shape=[
+            shape((cedges, lat), F32),
+            full,
+            shape((cedges, TILE), jnp.int32),
+            shape((nodes, TILE), jnp.int32),
+        ],
+        input_output_aliases={8: 1},
         scratch_shapes=[pltpu.SemaphoreType.DMA((3,))],
         compiler_params=params,
         name="near",
-    )(dev, csend2, crecv2, coarse, coarse_w1, inner_edges, ends, edge_out)
+    )(dev, csend2, crecv2, cmap2, coarse, coarse_w1, inner_edges, ends, edge_out)
     node_out = pl.pallas_call(
         coarse_kernel,
         in_specs=[sm] + [vm] * (8 + len(tables)),
@@ -623,7 +636,7 @@
         compiler_params=pltpu.CompilerParams(vmem_limit_bytes=32 * 2**20),
         name="coarse",
     )(
-        dev, csend2, crecv2, cmap2, fine, pre, coarse_w1, coarse_w2, coarse_gain.reshape(1, lat),
+        dev, crecv2, far_words, spread_words, fine, pre, coarse_w1, coarse_w2, coarse_gain.reshape(1, lat),
         *tables,
     )
     return (node_out, edge_out)

time: 37.9 us -> 37.7 us (level)
  transfers between devices with their start and end apart: 6 -> 6, of which waited for: 3 -> 3; matrix products, arithmetic and copies ran while one was open for 0% -> 0% of each run, Pallas kernels for 40% -> 41%
where the time goes in v6:
time: 37.7 us; the launch traced here: 37.6 us
  Pallas kernels  24.5 us (65%)
  starting transfers between devices  9.29 us (25%)
  waiting for transfers between devices  3.02 us (8%)
  between operations  0.76 us (2%)
    pallas_call x1, Pallas kernels, on_device(): pl.pallas_call(functools.partial(inner_kernel, count), grid=(count + 2,),...  13.8 us
    ppermute x1, starting transfers between devices, on_device(): within = lax.ppermute(within, axes, pairs + [(j, i) for i, j in pairs])  4.39 us
    pallas_call x1, Pallas kernels, on_device(): pl.pallas_call(coarse_kernel, in_specs=[sm] + [vm] * (8 + len(tables)), o...  4.33 us
    ppermute x4, starting transfers between devices, on_device(): lax.ppermute(coarse, axes, [(i, i ^ bit) for i in range(size)])  4.23 us
    ppermute x4, waiting for transfers between devices, on_device(): lax.ppermute(coarse, axes, [(i, i ^ bit) for i in range(size)])  3.01 us
    pallas_call x1, Pallas kernels, on_device(): pl.pallas_call(functools.partial(border_kernel, steps - 1), in_specs=[sm]...  2.81 us
    pallas_call x1, Pallas kernels, on_device(): pl.pallas_call(ready_kernel, in_specs=[sm] + [hb] * (1 + len(hbm)), out_s...  2.04 us
    pallas_call x1, Pallas kernels, on_device(): pl.pallas_call(functools.partial(near_kernel, steps - 1, len(tables) - 1)...  1.54 us
  transfers between devices with their start and end apart: 6, of which 3 were waited for; matrix products, arithmetic and copies ran while one was open for 0% of the time, Pallas kernels for 41%

profile of v6, /device:TPU:0, one launch (start us, length us, event | category | flops | bytes accessed | tf_op | source)
XLA Modules:
  0.0 37.6 jit_solution(11526860534432663286)
XLA Ops:
  0.6 2.0 %ready.1 = (bf16[256,128]{1,0:T(8,128)(2,1)S(1)}, bf16[256,128]{1,0:T(8,128)(2,1)S(1)}, bf16[128,128]{1,0:T(8,128)(2,1)S(1)}, bf16[15360,128]{1,0:T(8,128)(2,1)S...) custom-call(s32[1]{0:T(128)} %bitcast.base_ref, ...), custom_call_target="tpu_custom_call" | custom-call | tf_op jit(solution)/shard_map/ready/pallas_call | solution.py:547
  2.7 0.7 %collective-permute-start = (bf16[256,128]{1,0:T(8,128)(2,1)S(1)}, bf16[256,128]{1,0:T(8,128)(2,1)S(1)}, u32[]{:S(2)}, u32[]{:S(2)}) collective-permute-start(bf16[256,128]{1,0:T(8,128)(2,1)S(1)} %get-tuple-element.32), channel_id=1, source_target_pairs={{1,2},{3,4},{5,6},{7,8},{9,10},{11,12},{13,14},{2,1},{4,3},{6,5},{... | collective-permute-start | bytes 196616 | tf_op jit(solution)/shard_map/ppermute | solution.py:565
  3.4 4.4 %collective-permute-start.1 = (bf16[256,128]{1,0:T(8,128)(2,1)S(1)}, bf16[256,128]{1,0:T(8,128)(2,1)S(1)}, u32[]{:S(2)}, u32[]{:S(2)}) collective-permute-start(bf16[256,128]{1,0:T(8,128)(2,1)S(1)} %get-tuple-element.33), channel_id=1, source_target_pairs={{0,1},{2,3},{4,5},{6,7},{8,9},{10,11},{12,13},{14,15},{1,0},{3,2},... | collective-permute-start | bytes 196616 | tf_op jit(solution)/shard_map/ppermute | solution.py:567
  7.8 13.8 %inner.1 = (bf16[15360,128]{1,0:T(8,128)(2,1)S(1)}, bf16[18432,128]{1,0:T(8,128)(2,1)}, bf16[3072,128]{1,0:T(8,128)(2,1)S(1)}, f32[384,256]{1,0:T(8,128)S(1)}, bf16[3072,128]{1,0:T(8,128)(2,1)S(1)}) custom-call(s32[1]{0:T(128)} %bitcast.base_ref, bf16[18432,128]{1,0:T(8,128)(2,1)} %all_ref.1, ...), custom_call_target="tpu_custom_call", output_to_operand_aliasing={{0}: (14, {})} | custom-call | tf_op jit(solution)/shard_map/inner/pallas_call | solution.py:568
  21.5 0.0 copy-start
  21.5 0.0 copy-start.1
  21.5 0.0 copy-start.3
  21.6 0.0 collective-permute-done.across_ref
  21.6 0.0 collective-permute-done.1.within_ref
  21.6 2.8 %border.1 = (bf16[3072,128]{1,0:T(8,128)(2,1)S(1)}, bf16[3072,128]{1,0:T(8,128)(2,1)S(1)}, bf16[384,128]{1,0:T(8,128)(2,1)S(1)}) custom-call(s32[1]{0:T(128)} %bitcast.base_ref, bf16[3072,128]{1,0:T(8,128)(2,1)S(1)} %get-tuple-element.31.own_ref, ...), custom_call_target="tpu_custom_call", output_to_operand_aliasing={{0}: (17, {}), {1}: (18, {})} | custom-call | tf_op jit(solution)/shard_map/border/pallas_call | solution.py:592
  24.4 2.7 %collective-permute-start.5 = (bf16[384,128]{1,0:T(8,128)(2,1)S(1)}, bf16[384,128]{1,0:T(8,128)(2,1)S(1)}, u32[]{:S(2)}, u32[]{:S(2)}) collective-permute-start(bf16[384,128]{1,0:T(8,128)(2,1)S(1)} %get-tuple-element.49.own_ref.refs_0_), channel_id=1, source_target_pairs={{0,8},{1,9},{2,10},{3,11},{4,12},{5,13},{6,14},{7,15},{8,0},{9,1},... | collective-permute-start | bytes 294920 | tf_op jit(solution)/shard_map/ppermute | solution.py:610
  27.0 1.6 %collective-permute-start.4 = (bf16[384,128]{1,0:T(8,128)(2,1)S(1)}, bf16[384,128]{1,0:T(8,128)(2,1)S(1)}, u32[]{:S(2)}, u32[]{:S(2)}) collective-permute-start(bf16[384,128]{1,0:T(8,128)(2,1)S(1)} %get-tuple-element.49.own_ref.refs_0_), channel_id=1, source_target_pairs={{0,4},{1,5},{2,6},{3,7},{4,0},{5,1},{6,2},{7,3},{8,12},{9,13},{10,... | collective-permute-start | bytes 294920 | tf_op jit(solution)/shard_map/ppermute | solution.py:610
  28.6 0.0 collective-permute-start.3
  28.6 0.0 collective-permute-start.2
  28.6 0.0 copy-done
  28.6 0.0 copy-done.1
  28.6 0.0 copy-done.3
  28.6 0.0 copy-start.2
  28.7 0.0 copy-start.4
  28.7 1.5 %near.1 = (f32[2304,128]{1,0:T(8,128)S(1)}, bf16[18432,128]{1,0:T(8,128)(2,1)}, s32[2304,128]{1,0:T(8,128)S(1)}, s32[3072,128]{1,0:T(8,128)S(1)}) custom-call(s32[1]{0:T(128)} %bitcast.base_ref, s32[18,128]{1,0:T(8,128)S(1)} %bitcast.12, s32[18,128]{1,0:T(8,128)S(1)} %bitcast.10, ...), custom_call_target="tpu_custom_call", output_to_operand_aliasing={{1}: (8, {})} | custom-call | tf_op jit(solution)/shard_map/near/pallas_call | solution.py:615
  30.2 2.1 %collective-permute-done.5.refs_4_ = bf16[384,128]{1,0:T(8,128)(2,1)S(1)} collective-permute-done((bf16[384,128]{1,0:T(8,128)(2,1)S(1)}, bf16[384,128]{1,0:T(8,128)(2,1)S(1)}, u32[]{:S(2)}, u32[]{:S(2)}) %collective-permute-start.5) | collective-permute-done | bytes 98336 | tf_op jit(solution)/shard_map/ppermute | solution.py:610
  32.3 0.2 collective-permute-done.4.refs_3_
  32.5 0.7 %collective-permute-done.3.refs_2_ = bf16[384,128]{1,0:T(8,128)(2,1)S(1)} collective-permute-done((bf16[384,128]{1,0:T(8,128)(2,1)S(1)}, bf16[384,128]{1,0:T(8,128)(2,1)S(1)}, u32[]{:S(2)}, u32[]{:S(2)}) %collective-permute-start.3) | collective-permute-done | bytes 98336 | tf_op jit(solution)/shard_map/ppermute | solution.py:610
  33.2 0.0 collective-permute-done.2.refs_1_
  33.2 0.0 copy-done.2
  33.2 0.0 copy-done.4
  33.2 4.3 %coarse.1 = bf16[3072,128]{1,0:T(8,128)(2,1)} custom-call(s32[1]{0:T(128)} %bitcast.base_ref, s32[18,128]{1,0:T(8,128)S(1)} %bitcast.11, s32[2304,128]{1,0:T(8,128)S(1)} %get-tuple-element.53.far_ref, s32[3072,128]{1,0:T(8,128)S(1)} %get-tuple-element.54.spread_ref, bf16[3072,128]{1,0:T(8,128)(2,1)S(1)} %get-tuple-element.55.fine_ref, ...), custom_call_target="tpu_custom_call" | custom-call | tf_op jit(solution)/shard_map/coarse/pallas_call | solution.py:630
Async XLA Ops:
  2.7 18.9 %collective-permute-start = (bf16[256,128]{1,0:T(8,128)(2,1)S(1)}, bf16[256,128]{1,0:T(8,128)(2,1)S(1)}, u32[]{:S(2)}, u32[]{:S(2)}) collective-permute-start(bf16[256,128]{1,0:T(8,128)(2,1)S(1)} %get-tuple-element.32), channel_id=1, source_target_pairs={{1,2},{3,4},{5,6},{7,8},{9,10},{11,12},{13,14},{2,1},{4,3},{6,5},{... | collective-permute-start | bytes 196616 | tf_op jit(solution)/shard_map/ppermute | solution.py:565
  3.4 18.2 %collective-permute-start.1 = (bf16[256,128]{1,0:T(8,128)(2,1)S(1)}, bf16[256,128]{1,0:T(8,128)(2,1)S(1)}, u32[]{:S(2)}, u32[]{:S(2)}) collective-permute-start(bf16[256,128]{1,0:T(8,128)(2,1)S(1)} %get-tuple-element.33), channel_id=1, source_target_pairs={{0,1},{2,3},{4,5},{6,7},{8,9},{10,11},{12,13},{14,15},{1,0},{3,2},... | collective-permute-start | bytes 196616 | tf_op jit(solution)/shard_map/ppermute | solution.py:567
  21.5 7.1 %copy-start = (bf16[256,128]{1,0:T(8,128)(2,1)S(1)}, bf16[256,128]{1,0:T(8,128)(2,1)}, u32[]{:S(2)}) copy-start(bf16[256,128]{1,0:T(8,128)(2,1)} %w1_ref.3) | copy-start | bytes 196612
  21.5 7.1 %copy-start.1 = (s32[2304]{0:T(1024)S(1)}, s32[2304]{0:T(1024)}, u32[]{:S(2)}) copy-start(s32[2304]{0:T(1024)} %param.23) | copy-start | bytes 27652
  21.5 7.1 %copy-start.3 = (s32[2304]{0:T(1024)S(1)}, s32[2304]{0:T(1024)}, u32[]{:S(2)}) copy-start(s32[2304]{0:T(1024)} %param.24) | copy-start | bytes 27652
  24.4 7.9 %collective-permute-start.5 = (bf16[384,128]{1,0:T(8,128)(2,1)S(1)}, bf16[384,128]{1,0:T(8,128)(2,1)S(1)}, u32[]{:S(2)}, u32[]{:S(2)}) collective-permute-start(bf16[384,128]{1,0:T(8,128)(2,1)S(1)} %get-tuple-element.49.own_ref.refs_0_), channel_id=1, source_target_pairs={{0,8},{1,9},{2,10},{3,11},{4,12},{5,13},{6,14},{7,15},{8,0},{9,1},... | collective-permute-start | bytes 294920 | tf_op jit(solution)/shard_map/ppermute | solution.py:610
  27.0 5.5 %collective-permute-start.4 = (bf16[384,128]{1,0:T(8,128)(2,1)S(1)}, bf16[384,128]{1,0:T(8,128)(2,1)S(1)}, u32[]{:S(2)}, u32[]{:S(2)}) collective-permute-start(bf16[384,128]{1,0:T(8,128)(2,1)S(1)} %get-tuple-element.49.own_ref.refs_0_), channel_id=1, source_target_pairs={{0,4},{1,5},{2,6},{3,7},{4,0},{5,1},{6,2},{7,3},{8,12},{9,13},{10,... | collective-permute-start | bytes 294920 | tf_op jit(solution)/shard_map/ppermute | solution.py:610
  28.6 4.6 %collective-permute-start.3 = (bf16[384,128]{1,0:T(8,128)(2,1)S(1)}, bf16[384,128]{1,0:T(8,128)(2,1)S(1)}, u32[]{:S(2)}, u32[]{:S(2)}) collective-permute-start(bf16[384,128]{1,0:T(8,128)(2,1)S(1)} %get-tuple-element.49.own_ref.refs_0_), channel_id=1, source_target_pairs={{0,2},{1,3},{2,0},{3,1},{4,6},{5,7},{6,4},{7,5},{8,10},{9,11},{10,... | collective-permute-start | bytes 294920 | tf_op jit(solution)/shard_map/ppermute | solution.py:610
  28.6 4.6 %collective-permute-start.2 = (bf16[384,128]{1,0:T(8,128)(2,1)S(1)}, bf16[384,128]{1,0:T(8,128)(2,1)S(1)}, u32[]{:S(2)}, u32[]{:S(2)}) collective-permute-start(bf16[384,128]{1,0:T(8,128)(2,1)S(1)} %get-tuple-element.49.own_ref.refs_0_), channel_id=1, source_target_pairs={{0,1},{1,0},{2,3},{3,2},{4,5},{5,4},{6,7},{7,6},{8,9},{9,8},{10,11... | collective-permute-start | bytes 294920 | tf_op jit(solution)/shard_map/ppermute | solution.py:610
  28.6 4.6 %copy-start.2 = (bf16[128,128]{1,0:T(8,128)(2,1)S(1)}, bf16[128,128]{1,0:T(8,128)(2,1)}, u32[]{:S(2)}) copy-start(bf16[128,128]{1,0:T(8,128)(2,1)} %w2_ref.1) | copy-start | bytes 98308
  28.7 4.6 %copy-start.4 = (f32[128]{0:T(128)S(1)}, f32[128]{0:T(128)}, u32[]{:S(2)}) copy-start(f32[128]{0:T(128)} %param.35) | copy-start | bytes 1540

commit v7 on v6

--- a/solution.py
+++ b/solution.py
@@ -455,7 +455,7 @@
     lane = lax.broadcasted_iota(I16, (TILE, TILE), 1)
     csub = lax.broadcasted_iota(I16, (crows, TILE), 0)
     w2 = twice(w2_ref[...])
-    group = 6 if rows % 6 == 0 else 1
+    group = next(g for g in (9, 6, 3, 2, 1) if rows % g == 0)
     total = [own_ref[...].astype(F32)]
 
     def part(g):

time: 37.7 us -> 37.2 us (0.987)
  Pallas kernels: 24.5 us -> 23.9 us
    pallas_call x1, Pallas kernels: 4.33 us -> 3.76 us  [on_device(): pl.pallas_call(coarse_kernel, in_specs=[sm] + [vm] * (8 + len(tables)), o...]
where the time goes in v7:
time: 37.2 us; the launch traced here: 37 us
  Pallas kernels  23.9 us (64%)
  starting transfers between devices  9.29 us (25%)
  waiting for transfers between devices  3.02 us (8%)
  between operations  0.76 us (2%)
    pallas_call x1, Pallas kernels, on_device(): pl.pallas_call(functools.partial(inner_kernel, count), grid=(count + 2,),...  13.8 us
    ppermute x1, starting transfers between devices, on_device(): within = lax.ppermute(within, axes, pairs + [(j, i) for i, j in pairs])  4.39 us
    ppermute x4, starting transfers between devices, on_device(): lax.ppermute(coarse, axes, [(i, i ^ bit) for i in range(size)])  4.23 us
    pallas_call x1, Pallas kernels, on_device(): pl.pallas_call(coarse_kernel, in_specs=[sm] + [vm] * (8 + len(tables)), o...  3.76 us
    ppermute x4, waiting for transfers between devices, on_device(): lax.ppermute(coarse, axes, [(i, i ^ bit) for i in range(size)])  3.01 us
    pallas_call x1, Pallas kernels, on_device(): pl.pallas_call(functools.partial(border_kernel, steps - 1), in_specs=[sm]...  2.81 us
    pallas_call x1, Pallas kernels, on_device(): pl.pallas_call(ready_kernel, in_specs=[sm] + [hb] * (1 + len(hbm)), out_s...  2.04 us
    pallas_call x1, Pallas kernels, on_device(): pl.pallas_call(functools.partial(near_kernel, steps - 1, len(tables) - 1)...  1.54 us
  transfers between devices with their start and end apart: 6, of which 3 were waited for; matrix products, arithmetic and copies ran while one was open for 0% of the time, Pallas kernels for 41%

profile of v7, /device:TPU:0, one launch (start us, length us, event | category | flops | bytes accessed | tf_op | source)
XLA Modules:
  0.0 37.0 jit_solution(6107795257319742697)
XLA Ops:
  0.6 2.0 %ready.1 = (bf16[256,128]{1,0:T(8,128)(2,1)S(1)}, bf16[256,128]{1,0:T(8,128)(2,1)S(1)}, bf16[128,128]{1,0:T(8,128)(2,1)S(1)}, bf16[15360,128]{1,0:T(8,128)(2,1)S...) custom-call(s32[1]{0:T(128)} %bitcast.base_ref, ...), custom_call_target="tpu_custom_call" | custom-call | tf_op jit(solution)/shard_map/ready/pallas_call | solution.py:547
  2.7 0.7 %collective-permute-start = (bf16[256,128]{1,0:T(8,128)(2,1)S(1)}, bf16[256,128]{1,0:T(8,128)(2,1)S(1)}, u32[]{:S(2)}, u32[]{:S(2)}) collective-permute-start(bf16[256,128]{1,0:T(8,128)(2,1)S(1)} %get-tuple-element.32), channel_id=1, source_target_pairs={{1,2},{3,4},{5,6},{7,8},{9,10},{11,12},{13,14},{2,1},{4,3},{6,5},{... | collective-permute-start | bytes 196616 | tf_op jit(solution)/shard_map/ppermute | solution.py:565
  3.4 4.4 %collective-permute-start.1 = (bf16[256,128]{1,0:T(8,128)(2,1)S(1)}, bf16[256,128]{1,0:T(8,128)(2,1)S(1)}, u32[]{:S(2)}, u32[]{:S(2)}) collective-permute-start(bf16[256,128]{1,0:T(8,128)(2,1)S(1)} %get-tuple-element.33), channel_id=1, source_target_pairs={{0,1},{2,3},{4,5},{6,7},{8,9},{10,11},{12,13},{14,15},{1,0},{3,2},... | collective-permute-start | bytes 196616 | tf_op jit(solution)/shard_map/ppermute | solution.py:567
  7.8 13.8 %inner.1 = (bf16[15360,128]{1,0:T(8,128)(2,1)S(1)}, bf16[18432,128]{1,0:T(8,128)(2,1)}, bf16[3072,128]{1,0:T(8,128)(2,1)S(1)}, f32[384,256]{1,0:T(8,128)S(1)}, bf16[3072,128]{1,0:T(8,128)(2,1)S(1)}) custom-call(s32[1]{0:T(128)} %bitcast.base_ref, bf16[18432,128]{1,0:T(8,128)(2,1)} %all_ref.1, ...), custom_call_target="tpu_custom_call", output_to_operand_aliasing={{0}: (14, {})} | custom-call | tf_op jit(solution)/shard_map/inner/pallas_call | solution.py:568
  21.5 0.0 copy-start
  21.5 0.0 copy-start.1
  21.5 0.0 copy-start.3
  21.6 0.0 collective-permute-done.across_ref
  21.6 0.0 collective-permute-done.1.within_ref
  21.6 2.8 %border.1 = (bf16[3072,128]{1,0:T(8,128)(2,1)S(1)}, bf16[3072,128]{1,0:T(8,128)(2,1)S(1)}, bf16[384,128]{1,0:T(8,128)(2,1)S(1)}) custom-call(s32[1]{0:T(128)} %bitcast.base_ref, bf16[3072,128]{1,0:T(8,128)(2,1)S(1)} %get-tuple-element.31.own_ref, ...), custom_call_target="tpu_custom_call", output_to_operand_aliasing={{0}: (17, {}), {1}: (18, {})} | custom-call | tf_op jit(solution)/shard_map/border/pallas_call | solution.py:592
  24.4 2.7 %collective-permute-start.5 = (bf16[384,128]{1,0:T(8,128)(2,1)S(1)}, bf16[384,128]{1,0:T(8,128)(2,1)S(1)}, u32[]{:S(2)}, u32[]{:S(2)}) collective-permute-start(bf16[384,128]{1,0:T(8,128)(2,1)S(1)} %get-tuple-element.49.own_ref.refs_0_), channel_id=1, source_target_pairs={{0,8},{1,9},{2,10},{3,11},{4,12},{5,13},{6,14},{7,15},{8,0},{9,1},... | collective-permute-start | bytes 294920 | tf_op jit(solution)/shard_map/ppermute | solution.py:610
  27.0 1.6 %collective-permute-start.4 = (bf16[384,128]{1,0:T(8,128)(2,1)S(1)}, bf16[384,128]{1,0:T(8,128)(2,1)S(1)}, u32[]{:S(2)}, u32[]{:S(2)}) collective-permute-start(bf16[384,128]{1,0:T(8,128)(2,1)S(1)} %get-tuple-element.49.own_ref.refs_0_), channel_id=1, source_target_pairs={{0,4},{1,5},{2,6},{3,7},{4,0},{5,1},{6,2},{7,3},{8,12},{9,13},{10,... | collective-permute-start | bytes 294920 | tf_op jit(solution)/shard_map/ppermute | solution.py:610
  28.6 0.0 collective-permute-start.3
  28.6 0.0 collective-permute-start.2
  28.6 0.0 copy-done
  28.6 0.0 copy-done.1
  28.6 0.0 copy-done.3
  28.6 0.0 copy-start.2
  28.7 0.0 copy-start.4
  28.7 1.5 %near.1 = (f32[2304,128]{1,0:T(8,128)S(1)}, bf16[18432,128]{1,0:T(8,128)(2,1)}, s32[2304,128]{1,0:T(8,128)S(1)}, s32[3072,128]{1,0:T(8,128)S(1)}) custom-call(s32[1]{0:T(128)} %bitcast.base_ref, s32[18,128]{1,0:T(8,128)S(1)} %bitcast.12, s32[18,128]{1,0:T(8,128)S(1)} %bitcast.10, ...), custom_call_target="tpu_custom_call", output_to_operand_aliasing={{1}: (8, {})} | custom-call | tf_op jit(solution)/shard_map/near/pallas_call | solution.py:615
  30.2 2.1 %collective-permute-done.5.refs_4_ = bf16[384,128]{1,0:T(8,128)(2,1)S(1)} collective-permute-done((bf16[384,128]{1,0:T(8,128)(2,1)S(1)}, bf16[384,128]{1,0:T(8,128)(2,1)S(1)}, u32[]{:S(2)}, u32[]{:S(2)}) %collective-permute-start.5) | collective-permute-done | bytes 98336 | tf_op jit(solution)/shard_map/ppermute | solution.py:610
  32.3 0.2 collective-permute-done.4.refs_3_
  32.5 0.7 %collective-permute-done.3.refs_2_ = bf16[384,128]{1,0:T(8,128)(2,1)S(1)} collective-permute-done((bf16[384,128]{1,0:T(8,128)(2,1)S(1)}, bf16[384,128]{1,0:T(8,128)(2,1)S(1)}, u32[]{:S(2)}, u32[]{:S(2)}) %collective-permute-start.3) | collective-permute-done | bytes 98336 | tf_op jit(solution)/shard_map/ppermute | solution.py:610
  33.2 0.0 collective-permute-done.2.refs_1_
  33.2 0.0 copy-done.2
  33.2 0.0 copy-done.4
  33.2 3.8 %coarse.1 = bf16[3072,128]{1,0:T(8,128)(2,1)} custom-call(s32[1]{0:T(128)} %bitcast.base_ref, s32[18,128]{1,0:T(8,128)S(1)} %bitcast.11, s32[2304,128]{1,0:T(8,128)S(1)} %get-tuple-element.53.far_ref, s32[3072,128]{1,0:T(8,128)S(1)} %get-tuple-element.54.spread_ref, bf16[3072,128]{1,0:T(8,128)(2,1)S(1)} %get-tuple-element.55.fine_ref, ...), custom_call_target="tpu_custom_call" | custom-call | tf_op jit(solution)/shard_map/coarse/pallas_call | solution.py:630
Async XLA Ops:
  2.7 18.9 %collective-permute-start = (bf16[256,128]{1,0:T(8,128)(2,1)S(1)}, bf16[256,128]{1,0:T(8,128)(2,1)S(1)}, u32[]{:S(2)}, u32[]{:S(2)}) collective-permute-start(bf16[256,128]{1,0:T(8,128)(2,1)S(1)} %get-tuple-element.32), channel_id=1, source_target_pairs={{1,2},{3,4},{5,6},{7,8},{9,10},{11,12},{13,14},{2,1},{4,3},{6,5},{... | collective-permute-start | bytes 196616 | tf_op jit(solution)/shard_map/ppermute | solution.py:565
  3.4 18.2 %collective-permute-start.1 = (bf16[256,128]{1,0:T(8,128)(2,1)S(1)}, bf16[256,128]{1,0:T(8,128)(2,1)S(1)}, u32[]{:S(2)}, u32[]{:S(2)}) collective-permute-start(bf16[256,128]{1,0:T(8,128)(2,1)S(1)} %get-tuple-element.33), channel_id=1, source_target_pairs={{0,1},{2,3},{4,5},{6,7},{8,9},{10,11},{12,13},{14,15},{1,0},{3,2},... | collective-permute-start | bytes 196616 | tf_op jit(solution)/shard_map/ppermute | solution.py:567
  21.5 7.1 %copy-start = (bf16[256,128]{1,0:T(8,128)(2,1)S(1)}, bf16[256,128]{1,0:T(8,128)(2,1)}, u32[]{:S(2)}) copy-start(bf16[256,128]{1,0:T(8,128)(2,1)} %w1_ref.3) | copy-start | bytes 196612
  21.5 7.1 %copy-start.1 = (s32[2304]{0:T(1024)S(1)}, s32[2304]{0:T(1024)}, u32[]{:S(2)}) copy-start(s32[2304]{0:T(1024)} %param.23) | copy-start | bytes 27652
  21.5 7.1 %copy-start.3 = (s32[2304]{0:T(1024)S(1)}, s32[2304]{0:T(1024)}, u32[]{:S(2)}) copy-start(s32[2304]{0:T(1024)} %param.24) | copy-start | bytes 27652
  24.4 7.9 %collective-permute-start.5 = (bf16[384,128]{1,0:T(8,128)(2,1)S(1)}, bf16[384,128]{1,0:T(8,128)(2,1)S(1)}, u32[]{:S(2)}, u32[]{:S(2)}) collective-permute-start(bf16[384,128]{1,0:T(8,128)(2,1)S(1)} %get-tuple-element.49.own_ref.refs_0_), channel_id=1, source_target_pairs={{0,8},{1,9},{2,10},{3,11},{4,12},{5,13},{6,14},{7,15},{8,0},{9,1},... | collective-permute-start | bytes 294920 | tf_op jit(solution)/shard_map/ppermute | solution.py:610
  27.0 5.5 %collective-permute-start.4 = (bf16[384,128]{1,0:T(8,128)(2,1)S(1)}, bf16[384,128]{1,0:T(8,128)(2,1)S(1)}, u32[]{:S(2)}, u32[]{:S(2)}) collective-permute-start(bf16[384,128]{1,0:T(8,128)(2,1)S(1)} %get-tuple-element.49.own_ref.refs_0_), channel_id=1, source_target_pairs={{0,4},{1,5},{2,6},{3,7},{4,0},{5,1},{6,2},{7,3},{8,12},{9,13},{10,... | collective-permute-start | bytes 294920 | tf_op jit(solution)/shard_map/ppermute | solution.py:610
  28.6 4.6 %collective-permute-start.3 = (bf16[384,128]{1,0:T(8,128)(2,1)S(1)}, bf16[384,128]{1,0:T(8,128)(2,1)S(1)}, u32[]{:S(2)}, u32[]{:S(2)}) collective-permute-start(bf16[384,128]{1,0:T(8,128)(2,1)S(1)} %get-tuple-element.49.own_ref.refs_0_), channel_id=1, source_target_pairs={{0,2},{1,3},{2,0},{3,1},{4,6},{5,7},{6,4},{7,5},{8,10},{9,11},{10,... | collective-permute-start | bytes 294920 | tf_op jit(solution)/shard_map/ppermute | solution.py:610
  28.6 4.6 %collective-permute-start.2 = (bf16[384,128]{1,0:T(8,128)(2,1)S(1)}, bf16[384,128]{1,0:T(8,128)(2,1)S(1)}, u32[]{:S(2)}, u32[]{:S(2)}) collective-permute-start(bf16[384,128]{1,0:T(8,128)(2,1)S(1)} %get-tuple-element.49.own_ref.refs_0_), channel_id=1, source_target_pairs={{0,1},{1,0},{2,3},{3,2},{4,5},{5,4},{6,7},{7,6},{8,9},{9,8},{10,11... | collective-permute-start | bytes 294920 | tf_op jit(solution)/shard_map/ppermute | solution.py:610
  28.6 4.6 %copy-start.2 = (bf16[128,128]{1,0:T(8,128)(2,1)S(1)}, bf16[128,128]{1,0:T(8,128)(2,1)}, u32[]{:S(2)}) copy-start(bf16[128,128]{1,0:T(8,128)(2,1)} %w2_ref.1) | copy-start | bytes 98308
  28.7 4.6 %copy-start.4 = (f32[128]{0:T(128)S(1)}, f32[128]{0:T(128)}, u32[]{:S(2)}) copy-start(f32[128]{0:T(128)} %param.35) | copy-start | bytes 1540

commit v8 on v7

--- a/solution.py
+++ b/solution.py
@@ -447,7 +447,7 @@
     lows = half_blocks(chunks * len(tables))
     loc = recv_ref[...] - dev * crows
     w1 = twice(w1_ref[:lat] * 0.5)
-    proj = jnp.concatenate([pair_dot(t[...], w1).astype(BF) for t in tables], axis=0)
+    proj = jnp.concatenate([t[...] for t in tables], axis=0)
     low, high = proj[: lows * TILE], proj[lows * TILE :]
     if high.shape[0] < low.shape[0]:
         high = jnp.concatenate([high, low[high.shape[0] :]], axis=0)
@@ -467,6 +467,8 @@
         out = dot(jnp.concatenate(lhs, axis=0), rhs)
         yield
         y = jnp.where(jnp.concatenate(upper, axis=0), out[:, lat:], out[:, :lat])
+        y = pair_dot(y.astype(BF), w1)
+        yield
         y = half_silu(y + pre_ref[g * TILE : (g + group) * TILE])
         msg = pair_dot(y, w2)
         yield
@@ -484,7 +486,7 @@
         high = jnp.concatenate([high, delta[high.shape[0] : half * TILE]], axis=0)
     rhs = jnp.concatenate([delta[: half * TILE], high], axis=1)
     tiles = nodes // TILE
-    size = 4 if tiles % 4 == 0 else 1
+    size = 3 if tiles % 3 == 0 else 1
     copies = []
 
     def spread(p):

time: 37.2 us -> 37 us (level)
  no operation moved by 1% of the time
where the time goes in v8:
time: 37 us; the launch traced here: 36.9 us
  Pallas kernels  23.8 us (64%)
  starting transfers between devices  9.29 us (25%)
  waiting for transfers between devices  3.02 us (8%)
  between operations  0.76 us (2%)
    pallas_call x1, Pallas kernels, on_device(): pl.pallas_call(functools.partial(inner_kernel, count), grid=(count + 2,),...  13.8 us
    ppermute x1, starting transfers between devices, on_device(): within = lax.ppermute(within, axes, pairs + [(j, i) for i, j in pairs])  4.39 us
    ppermute x4, starting transfers between devices, on_device(): lax.ppermute(coarse, axes, [(i, i ^ bit) for i in range(size)])  4.23 us
    pallas_call x1, Pallas kernels, on_device(): pl.pallas_call(coarse_kernel, in_specs=[sm] + [vm] * (8 + len(tables)), o...  3.64 us
    ppermute x4, waiting for transfers between devices, on_device(): lax.ppermute(coarse, axes, [(i, i ^ bit) for i in range(size)])  3.01 us
    pallas_call x1, Pallas kernels, on_device(): pl.pallas_call(functools.partial(border_kernel, steps - 1), in_specs=[sm]...  2.81 us
    pallas_call x1, Pallas kernels, on_device(): pl.pallas_call(ready_kernel, in_specs=[sm] + [hb] * (1 + len(hbm)), out_s...  2.04 us
    pallas_call x1, Pallas kernels, on_device(): pl.pallas_call(functools.partial(near_kernel, steps - 1, len(tables) - 1)...  1.54 us
  transfers between devices with their start and end apart: 6, of which 3 were waited for; matrix products, arithmetic and copies ran while one was open for 0% of the time, Pallas kernels for 41%

profile of v8, /device:TPU:0, one launch (start us, length us, event | category | flops | bytes accessed | tf_op | source)
XLA Modules:
  0.0 36.9 jit_solution(14797264093512036207)
XLA Ops:
  0.6 2.0 %ready.1 = (bf16[256,128]{1,0:T(8,128)(2,1)S(1)}, bf16[256,128]{1,0:T(8,128)(2,1)S(1)}, bf16[128,128]{1,0:T(8,128)(2,1)S(1)}, bf16[15360,128]{1,0:T(8,128)(2,1)S...) custom-call(s32[1]{0:T(128)} %bitcast.base_ref, ...), custom_call_target="tpu_custom_call" | custom-call | tf_op jit(solution)/shard_map/ready/pallas_call | solution.py:549
  2.7 0.7 %collective-permute-start = (bf16[256,128]{1,0:T(8,128)(2,1)S(1)}, bf16[256,128]{1,0:T(8,128)(2,1)S(1)}, u32[]{:S(2)}, u32[]{:S(2)}) collective-permute-start(bf16[256,128]{1,0:T(8,128)(2,1)S(1)} %get-tuple-element.32), channel_id=1, source_target_pairs={{1,2},{3,4},{5,6},{7,8},{9,10},{11,12},{13,14},{2,1},{4,3},{6,5},{... | collective-permute-start | bytes 196616 | tf_op jit(solution)/shard_map/ppermute | solution.py:567
  3.4 4.4 %collective-permute-start.1 = (bf16[256,128]{1,0:T(8,128)(2,1)S(1)}, bf16[256,128]{1,0:T(8,128)(2,1)S(1)}, u32[]{:S(2)}, u32[]{:S(2)}) collective-permute-start(bf16[256,128]{1,0:T(8,128)(2,1)S(1)} %get-tuple-element.33), channel_id=1, source_target_pairs={{0,1},{2,3},{4,5},{6,7},{8,9},{10,11},{12,13},{14,15},{1,0},{3,2},... | collective-permute-start | bytes 196616 | tf_op jit(solution)/shard_map/ppermute | solution.py:569
  7.8 13.8 %inner.1 = (bf16[15360,128]{1,0:T(8,128)(2,1)S(1)}, bf16[18432,128]{1,0:T(8,128)(2,1)}, bf16[3072,128]{1,0:T(8,128)(2,1)S(1)}, f32[384,256]{1,0:T(8,128)S(1)}, bf16[3072,128]{1,0:T(8,128)(2,1)S(1)}) custom-call(s32[1]{0:T(128)} %bitcast.base_ref, bf16[18432,128]{1,0:T(8,128)(2,1)} %all_ref.1, ...), custom_call_target="tpu_custom_call", output_to_operand_aliasing={{0}: (14, {})} | custom-call | tf_op jit(solution)/shard_map/inner/pallas_call | solution.py:570
  21.5 0.0 copy-start
  21.5 0.0 copy-start.1
  21.5 0.0 copy-start.3
  21.6 0.0 collective-permute-done.across_ref
  21.6 0.0 collective-permute-done.1.within_ref
  21.6 2.8 %border.1 = (bf16[3072,128]{1,0:T(8,128)(2,1)S(1)}, bf16[3072,128]{1,0:T(8,128)(2,1)S(1)}, bf16[384,128]{1,0:T(8,128)(2,1)S(1)}) custom-call(s32[1]{0:T(128)} %bitcast.base_ref, bf16[3072,128]{1,0:T(8,128)(2,1)S(1)} %get-tuple-element.31.own_ref, ...), custom_call_target="tpu_custom_call", output_to_operand_aliasing={{0}: (17, {}), {1}: (18, {})} | custom-call | tf_op jit(solution)/shard_map/border/pallas_call | solution.py:594
  24.4 2.7 %collective-permute-start.5 = (bf16[384,128]{1,0:T(8,128)(2,1)S(1)}, bf16[384,128]{1,0:T(8,128)(2,1)S(1)}, u32[]{:S(2)}, u32[]{:S(2)}) collective-permute-start(bf16[384,128]{1,0:T(8,128)(2,1)S(1)} %get-tuple-element.49.own_ref.refs_0_), channel_id=1, source_target_pairs={{0,8},{1,9},{2,10},{3,11},{4,12},{5,13},{6,14},{7,15},{8,0},{9,1},... | collective-permute-start | bytes 294920 | tf_op jit(solution)/shard_map/ppermute | solution.py:612
  27.0 1.6 %collective-permute-start.4 = (bf16[384,128]{1,0:T(8,128)(2,1)S(1)}, bf16[384,128]{1,0:T(8,128)(2,1)S(1)}, u32[]{:S(2)}, u32[]{:S(2)}) collective-permute-start(bf16[384,128]{1,0:T(8,128)(2,1)S(1)} %get-tuple-element.49.own_ref.refs_0_), channel_id=1, source_target_pairs={{0,4},{1,5},{2,6},{3,7},{4,0},{5,1},{6,2},{7,3},{8,12},{9,13},{10,... | collective-permute-start | bytes 294920 | tf_op jit(solution)/shard_map/ppermute | solution.py:612
  28.6 0.0 collective-permute-start.3
  28.6 0.0 collective-permute-start.2
  28.6 0.0 copy-done
  28.6 0.0 copy-done.1
  28.6 0.0 copy-done.3
  28.6 0.0 copy-start.2
  28.7 0.0 copy-start.4
  28.7 1.5 %near.1 = (f32[2304,128]{1,0:T(8,128)S(1)}, bf16[18432,128]{1,0:T(8,128)(2,1)}, s32[2304,128]{1,0:T(8,128)S(1)}, s32[3072,128]{1,0:T(8,128)S(1)}) custom-call(s32[1]{0:T(128)} %bitcast.base_ref, s32[18,128]{1,0:T(8,128)S(1)} %bitcast.12, s32[18,128]{1,0:T(8,128)S(1)} %bitcast.10, ...), custom_call_target="tpu_custom_call", output_to_operand_aliasing={{1}: (8, {})} | custom-call | tf_op jit(solution)/shard_map/near/pallas_call | solution.py:617
  30.2 2.1 %collective-permute-done.5.refs_4_ = bf16[384,128]{1,0:T(8,128)(2,1)S(1)} collective-permute-done((bf16[384,128]{1,0:T(8,128)(2,1)S(1)}, bf16[384,128]{1,0:T(8,128)(2,1)S(1)}, u32[]{:S(2)}, u32[]{:S(2)}) %collective-permute-start.5) | collective-permute-done | bytes 98336 | tf_op jit(solution)/shard_map/ppermute | solution.py:612
  32.3 0.2 collective-permute-done.4.refs_3_
  32.5 0.7 %collective-permute-done.3.refs_2_ = bf16[384,128]{1,0:T(8,128)(2,1)S(1)} collective-permute-done((bf16[384,128]{1,0:T(8,128)(2,1)S(1)}, bf16[384,128]{1,0:T(8,128)(2,1)S(1)}, u32[]{:S(2)}, u32[]{:S(2)}) %collective-permute-start.3) | collective-permute-done | bytes 98336 | tf_op jit(solution)/shard_map/ppermute | solution.py:612
  33.2 0.0 collective-permute-done.2.refs_1_
  33.2 0.0 copy-done.2
  33.2 0.0 copy-done.4
  33.2 3.6 %coarse.1 = bf16[3072,128]{1,0:T(8,128)(2,1)} custom-call(s32[1]{0:T(128)} %bitcast.base_ref, s32[18,128]{1,0:T(8,128)S(1)} %bitcast.11, s32[2304,128]{1,0:T(8,128)S(1)} %get-tuple-element.53.far_ref, s32[3072,128]{1,0:T(8,128)S(1)} %get-tuple-element.54.spread_ref, bf16[3072,128]{1,0:T(8,128)(2,1)S(1)} %get-tuple-element.55.fine_ref, ...), custom_call_target="tpu_custom_call" | custom-call | tf_op jit(solution)/shard_map/coarse/pallas_call | solution.py:632
Async XLA Ops:
  2.7 18.9 %collective-permute-start = (bf16[256,128]{1,0:T(8,128)(2,1)S(1)}, bf16[256,128]{1,0:T(8,128)(2,1)S(1)}, u32[]{:S(2)}, u32[]{:S(2)}) collective-permute-start(bf16[256,128]{1,0:T(8,128)(2,1)S(1)} %get-tuple-element.32), channel_id=1, source_target_pairs={{1,2},{3,4},{5,6},{7,8},{9,10},{11,12},{13,14},{2,1},{4,3},{6,5},{... | collective-permute-start | bytes 196616 | tf_op jit(solution)/shard_map/ppermute | solution.py:567
  3.4 18.2 %collective-permute-start.1 = (bf16[256,128]{1,0:T(8,128)(2,1)S(1)}, bf16[256,128]{1,0:T(8,128)(2,1)S(1)}, u32[]{:S(2)}, u32[]{:S(2)}) collective-permute-start(bf16[256,128]{1,0:T(8,128)(2,1)S(1)} %get-tuple-element.33), channel_id=1, source_target_pairs={{0,1},{2,3},{4,5},{6,7},{8,9},{10,11},{12,13},{14,15},{1,0},{3,2},... | collective-permute-start | bytes 196616 | tf_op jit(solution)/shard_map/ppermute | solution.py:569
  21.5 7.1 %copy-start = (bf16[256,128]{1,0:T(8,128)(2,1)S(1)}, bf16[256,128]{1,0:T(8,128)(2,1)}, u32[]{:S(2)}) copy-start(bf16[256,128]{1,0:T(8,128)(2,1)} %w1_ref.3) | copy-start | bytes 196612
  21.5 7.1 %copy-start.1 = (s32[2304]{0:T(1024)S(1)}, s32[2304]{0:T(1024)}, u32[]{:S(2)}) copy-start(s32[2304]{0:T(1024)} %param.23) | copy-start | bytes 27652
  21.5 7.1 %copy-start.3 = (s32[2304]{0:T(1024)S(1)}, s32[2304]{0:T(1024)}, u32[]{:S(2)}) copy-start(s32[2304]{0:T(1024)} %param.24) | copy-start | bytes 27652
  24.4 7.9 %collective-permute-start.5 = (bf16[384,128]{1,0:T(8,128)(2,1)S(1)}, bf16[384,128]{1,0:T(8,128)(2,1)S(1)}, u32[]{:S(2)}, u32[]{:S(2)}) collective-permute-start(bf16[384,128]{1,0:T(8,128)(2,1)S(1)} %get-tuple-element.49.own_ref.refs_0_), channel_id=1, source_target_pairs={{0,8},{1,9},{2,10},{3,11},{4,12},{5,13},{6,14},{7,15},{8,0},{9,1},... | collective-permute-start | bytes 294920 | tf_op jit(solution)/shard_map/ppermute | solution.py:612
  27.0 5.5 %collective-permute-start.4 = (bf16[384,128]{1,0:T(8,128)(2,1)S(1)}, bf16[384,128]{1,0:T(8,128)(2,1)S(1)}, u32[]{:S(2)}, u32[]{:S(2)}) collective-permute-start(bf16[384,128]{1,0:T(8,128)(2,1)S(1)} %get-tuple-element.49.own_ref.refs_0_), channel_id=1, source_target_pairs={{0,4},{1,5},{2,6},{3,7},{4,0},{5,1},{6,2},{7,3},{8,12},{9,13},{10,... | collective-permute-start | bytes 294920 | tf_op jit(solution)/shard_map/ppermute | solution.py:612
  28.6 4.6 %collective-permute-start.3 = (bf16[384,128]{1,0:T(8,128)(2,1)S(1)}, bf16[384,128]{1,0:T(8,128)(2,1)S(1)}, u32[]{:S(2)}, u32[]{:S(2)}) collective-permute-start(bf16[384,128]{1,0:T(8,128)(2,1)S(1)} %get-tuple-element.49.own_ref.refs_0_), channel_id=1, source_target_pairs={{0,2},{1,3},{2,0},{3,1},{4,6},{5,7},{6,4},{7,5},{8,10},{9,11},{10,... | collective-permute-start | bytes 294920 | tf_op jit(solution)/shard_map/ppermute | solution.py:612
  28.6 4.6 %collective-permute-start.2 = (bf16[384,128]{1,0:T(8,128)(2,1)S(1)}, bf16[384,128]{1,0:T(8,128)(2,1)S(1)}, u32[]{:S(2)}, u32[]{:S(2)}) collective-permute-start(bf16[384,128]{1,0:T(8,128)(2,1)S(1)} %get-tuple-element.49.own_ref.refs_0_), channel_id=1, source_target_pairs={{0,1},{1,0},{2,3},{3,2},{4,5},{5,4},{6,7},{7,6},{8,9},{9,8},{10,11... | collective-permute-start | bytes 294920 | tf_op jit(solution)/shard_map/ppermute | solution.py:612
  28.6 4.6 %copy-start.2 = (bf16[128,128]{1,0:T(8,128)(2,1)S(1)}, bf16[128,128]{1,0:T(8,128)(2,1)}, u32[]{:S(2)}) copy-start(bf16[128,128]{1,0:T(8,128)(2,1)} %w2_ref.1) | copy-start | bytes 98308
  28.7 4.6 %copy-start.4 = (f32[128]{0:T(128)S(1)}, f32[128]{0:T(128)}, u32[]{:S(2)}) copy-start(f32[128]{0:T(128)} %param.35) | copy-start | bytes 1540

commit v9 on v8

--- a/solution.py
+++ b/solution.py
@@ -222,7 +222,7 @@
     idx_rows = send_ref.shape[0] // (rows // TILE) * STEP
     size = idx_rows * TILE
     copies = [pltpu.make_async_copy(a, b, sem.at[i]) for i, (a, b) in enumerate(zip(hbm, vmem))]
-    order = [4, 5, 6, 0, 10, 11, 7, 9, 3, 2, 8, 1]
+    order = [4, 5, 6, 0, 2, 3, 10, 11, 7, 9, 8, 1]
     for i in order:
         copies[i].start()
     early = pltpu.make_async_copy(

time: 37 us -> 37 us (level)
  transfers between devices with their start and end apart: 6 -> 6, of which waited for: 3 -> 3; matrix products, arithmetic and copies ran while one was open for 0% -> 0% of each run, Pallas kernels for 41% -> 42%
where the time goes in v9:
time: 37 us; the launch traced here: 36.8 us
  Pallas kernels  23.7 us (64%)
  starting transfers between devices  9.31 us (25%)
  waiting for transfers between devices  3.02 us (8%)
  between operations  0.76 us (2%)
    pallas_call x1, Pallas kernels, on_device(): pl.pallas_call(functools.partial(inner_kernel, count), grid=(count + 2,),...  13.7 us
    ppermute x1, starting transfers between devices, on_device(): within = lax.ppermute(within, axes, pairs + [(j, i) for i, j in pairs])  4.39 us
    ppermute x4, starting transfers between devices, on_device(): lax.ppermute(coarse, axes, [(i, i ^ bit) for i in range(size)])  4.26 us
    pallas_call x1, Pallas kernels, on_device(): pl.pallas_call(coarse_kernel, in_specs=[sm] + [vm] * (8 + len(tables)), o...  3.64 us
    ppermute x4, waiting for transfers between devices, on_device(): lax.ppermute(coarse, axes, [(i, i ^ bit) for i in range(size)])  3.01 us
    pallas_call x1, Pallas kernels, on_device(): pl.pallas_call(functools.partial(border_kernel, steps - 1), in_specs=[sm]...  2.81 us
    pallas_call x1, Pallas kernels, on_device(): pl.pallas_call(ready_kernel, in_specs=[sm] + [hb] * (1 + len(hbm)), out_s...  2 us
    pallas_call x1, Pallas kernels, on_device(): pl.pallas_call(functools.partial(near_kernel, steps - 1, len(tables) - 1)...  1.54 us
  transfers between devices with their start and end apart: 6, of which 3 were waited for; matrix products, arithmetic and copies ran while one was open for 0% of the time, Pallas kernels for 42%

profile of v9, /device:TPU:0, one launch (start us, length us, event | category | flops | bytes accessed | tf_op | source)
XLA Modules:
  0.0 36.8 jit_solution(2545381781971180940)
XLA Ops:
  0.6 2.0 %ready.1 = (bf16[256,128]{1,0:T(8,128)(2,1)S(1)}, bf16[256,128]{1,0:T(8,128)(2,1)S(1)}, bf16[128,128]{1,0:T(8,128)(2,1)S(1)}, bf16[15360,128]{1,0:T(8,128)(2,1)S...) custom-call(s32[1]{0:T(128)} %bitcast.base_ref, ...), custom_call_target="tpu_custom_call" | custom-call | tf_op jit(solution)/shard_map/ready/pallas_call | solution.py:549
  2.6 0.7 %collective-permute-start = (bf16[256,128]{1,0:T(8,128)(2,1)S(1)}, bf16[256,128]{1,0:T(8,128)(2,1)S(1)}, u32[]{:S(2)}, u32[]{:S(2)}) collective-permute-start(bf16[256,128]{1,0:T(8,128)(2,1)S(1)} %get-tuple-element.32), channel_id=1, source_target_pairs={{1,2},{3,4},{5,6},{7,8},{9,10},{11,12},{13,14},{2,1},{4,3},{6,5},{... | collective-permute-start | bytes 196616 | tf_op jit(solution)/shard_map/ppermute | solution.py:567
  3.3 4.4 %collective-permute-start.1 = (bf16[256,128]{1,0:T(8,128)(2,1)S(1)}, bf16[256,128]{1,0:T(8,128)(2,1)S(1)}, u32[]{:S(2)}, u32[]{:S(2)}) collective-permute-start(bf16[256,128]{1,0:T(8,128)(2,1)S(1)} %get-tuple-element.33), channel_id=1, source_target_pairs={{0,1},{2,3},{4,5},{6,7},{8,9},{10,11},{12,13},{14,15},{1,0},{3,2},... | collective-permute-start | bytes 196616 | tf_op jit(solution)/shard_map/ppermute | solution.py:569
  7.7 13.7 %inner.1 = (bf16[15360,128]{1,0:T(8,128)(2,1)S(1)}, bf16[18432,128]{1,0:T(8,128)(2,1)}, bf16[3072,128]{1,0:T(8,128)(2,1)S(1)}, f32[384,256]{1,0:T(8,128)S(1)}, bf16[3072,128]{1,0:T(8,128)(2,1)S(1)}) custom-call(s32[1]{0:T(128)} %bitcast.base_ref, bf16[18432,128]{1,0:T(8,128)(2,1)} %all_ref.1, ...), custom_call_target="tpu_custom_call", output_to_operand_aliasing={{0}: (14, {})} | custom-call | tf_op jit(solution)/shard_map/inner/pallas_call | solution.py:570
  21.4 0.0 copy-start
  21.5 0.0 copy-start.1
  21.5 0.0 copy-start.3
  21.5 0.0 collective-permute-done.across_ref
  21.5 0.0 collective-permute-done.1.within_ref
  21.5 2.8 %border.1 = (bf16[3072,128]{1,0:T(8,128)(2,1)S(1)}, bf16[3072,128]{1,0:T(8,128)(2,1)S(1)}, bf16[384,128]{1,0:T(8,128)(2,1)S(1)}) custom-call(s32[1]{0:T(128)} %bitcast.base_ref, bf16[3072,128]{1,0:T(8,128)(2,1)S(1)} %get-tuple-element.31.own_ref, ...), custom_call_target="tpu_custom_call", output_to_operand_aliasing={{0}: (17, {}), {1}: (18, {})} | custom-call | tf_op jit(solution)/shard_map/border/pallas_call | solution.py:594
  24.3 2.6 %collective-permute-start.5 = (bf16[384,128]{1,0:T(8,128)(2,1)S(1)}, bf16[384,128]{1,0:T(8,128)(2,1)S(1)}, u32[]{:S(2)}, u32[]{:S(2)}) collective-permute-start(bf16[384,128]{1,0:T(8,128)(2,1)S(1)} %get-tuple-element.49.own_ref.refs_0_), channel_id=1, source_target_pairs={{0,8},{1,9},{2,10},{3,11},{4,12},{5,13},{6,14},{7,15},{8,0},{9,1},... | collective-permute-start | bytes 294920 | tf_op jit(solution)/shard_map/ppermute | solution.py:612
  27.0 1.6 %collective-permute-start.4 = (bf16[384,128]{1,0:T(8,128)(2,1)S(1)}, bf16[384,128]{1,0:T(8,128)(2,1)S(1)}, u32[]{:S(2)}, u32[]{:S(2)}) collective-permute-start(bf16[384,128]{1,0:T(8,128)(2,1)S(1)} %get-tuple-element.49.own_ref.refs_0_), channel_id=1, source_target_pairs={{0,4},{1,5},{2,6},{3,7},{4,0},{5,1},{6,2},{7,3},{8,12},{9,13},{10,... | collective-permute-start | bytes 294920 | tf_op jit(solution)/shard_map/ppermute | solution.py:612
  28.6 0.0 collective-permute-start.3
  28.6 0.0 collective-permute-start.2
  28.6 0.0 copy-done
  28.6 0.0 copy-done.1
  28.6 0.0 copy-done.3
  28.6 0.0 copy-start.2
  28.6 0.0 copy-start.4
  28.6 1.5 %near.1 = (f32[2304,128]{1,0:T(8,128)S(1)}, bf16[18432,128]{1,0:T(8,128)(2,1)}, s32[2304,128]{1,0:T(8,128)S(1)}, s32[3072,128]{1,0:T(8,128)S(1)}) custom-call(s32[1]{0:T(128)} %bitcast.base_ref, s32[18,128]{1,0:T(8,128)S(1)} %bitcast.12, s32[18,128]{1,0:T(8,128)S(1)} %bitcast.10, ...), custom_call_target="tpu_custom_call", output_to_operand_aliasing={{1}: (8, {})} | custom-call | tf_op jit(solution)/shard_map/near/pallas_call | solution.py:617
  30.2 2.1 %collective-permute-done.5.refs_4_ = bf16[384,128]{1,0:T(8,128)(2,1)S(1)} collective-permute-done((bf16[384,128]{1,0:T(8,128)(2,1)S(1)}, bf16[384,128]{1,0:T(8,128)(2,1)S(1)}, u32[]{:S(2)}, u32[]{:S(2)}) %collective-permute-start.5) | collective-permute-done | bytes 98336 | tf_op jit(solution)/shard_map/ppermute | solution.py:612
  32.2 0.2 collective-permute-done.4.refs_3_
  32.4 0.7 %collective-permute-done.3.refs_2_ = bf16[384,128]{1,0:T(8,128)(2,1)S(1)} collective-permute-done((bf16[384,128]{1,0:T(8,128)(2,1)S(1)}, bf16[384,128]{1,0:T(8,128)(2,1)S(1)}, u32[]{:S(2)}, u32[]{:S(2)}) %collective-permute-start.3) | collective-permute-done | bytes 98336 | tf_op jit(solution)/shard_map/ppermute | solution.py:612
  33.2 0.0 collective-permute-done.2.refs_1_
  33.2 0.0 copy-done.2
  33.2 0.0 copy-done.4
  33.2 3.6 %coarse.1 = bf16[3072,128]{1,0:T(8,128)(2,1)} custom-call(s32[1]{0:T(128)} %bitcast.base_ref, s32[18,128]{1,0:T(8,128)S(1)} %bitcast.11, s32[2304,128]{1,0:T(8,128)S(1)} %get-tuple-element.53.far_ref, s32[3072,128]{1,0:T(8,128)S(1)} %get-tuple-element.54.spread_ref, bf16[3072,128]{1,0:T(8,128)(2,1)S(1)} %get-tuple-element.55.fine_ref, ...), custom_call_target="tpu_custom_call" | custom-call | tf_op jit(solution)/shard_map/coarse/pallas_call | solution.py:632
Async XLA Ops:
  2.6 18.8 %collective-permute-start = (bf16[256,128]{1,0:T(8,128)(2,1)S(1)}, bf16[256,128]{1,0:T(8,128)(2,1)S(1)}, u32[]{:S(2)}, u32[]{:S(2)}) collective-permute-start(bf16[256,128]{1,0:T(8,128)(2,1)S(1)} %get-tuple-element.32), channel_id=1, source_target_pairs={{1,2},{3,4},{5,6},{7,8},{9,10},{11,12},{13,14},{2,1},{4,3},{6,5},{... | collective-permute-start | bytes 196616 | tf_op jit(solution)/shard_map/ppermute | solution.py:567
  3.3 18.2 %collective-permute-start.1 = (bf16[256,128]{1,0:T(8,128)(2,1)S(1)}, bf16[256,128]{1,0:T(8,128)(2,1)S(1)}, u32[]{:S(2)}, u32[]{:S(2)}) collective-permute-start(bf16[256,128]{1,0:T(8,128)(2,1)S(1)} %get-tuple-element.33), channel_id=1, source_target_pairs={{0,1},{2,3},{4,5},{6,7},{8,9},{10,11},{12,13},{14,15},{1,0},{3,2},... | collective-permute-start | bytes 196616 | tf_op jit(solution)/shard_map/ppermute | solution.py:569
  21.4 7.1 %copy-start = (bf16[256,128]{1,0:T(8,128)(2,1)S(1)}, bf16[256,128]{1,0:T(8,128)(2,1)}, u32[]{:S(2)}) copy-start(bf16[256,128]{1,0:T(8,128)(2,1)} %w1_ref.3) | copy-start | bytes 196612
  21.5 7.1 %copy-start.1 = (s32[2304]{0:T(1024)S(1)}, s32[2304]{0:T(1024)}, u32[]{:S(2)}) copy-start(s32[2304]{0:T(1024)} %param.23) | copy-start | bytes 27652
  21.5 7.1 %copy-start.3 = (s32[2304]{0:T(1024)S(1)}, s32[2304]{0:T(1024)}, u32[]{:S(2)}) copy-start(s32[2304]{0:T(1024)} %param.24) | copy-start | bytes 27652
  24.3 7.9 %collective-permute-start.5 = (bf16[384,128]{1,0:T(8,128)(2,1)S(1)}, bf16[384,128]{1,0:T(8,128)(2,1)S(1)}, u32[]{:S(2)}, u32[]{:S(2)}) collective-permute-start(bf16[384,128]{1,0:T(8,128)(2,1)S(1)} %get-tuple-element.49.own_ref.refs_0_), channel_id=1, source_target_pairs={{0,8},{1,9},{2,10},{3,11},{4,12},{5,13},{6,14},{7,15},{8,0},{9,1},... | collective-permute-start | bytes 294920 | tf_op jit(solution)/shard_map/ppermute | solution.py:612
  27.0 5.5 %collective-permute-start.4 = (bf16[384,128]{1,0:T(8,128)(2,1)S(1)}, bf16[384,128]{1,0:T(8,128)(2,1)S(1)}, u32[]{:S(2)}, u32[]{:S(2)}) collective-permute-start(bf16[384,128]{1,0:T(8,128)(2,1)S(1)} %get-tuple-element.49.own_ref.refs_0_), channel_id=1, source_target_pairs={{0,4},{1,5},{2,6},{3,7},{4,0},{5,1},{6,2},{7,3},{8,12},{9,13},{10,... | collective-permute-start | bytes 294920 | tf_op jit(solution)/shard_map/ppermute | solution.py:612
  28.6 4.6 %collective-permute-start.3 = (bf16[384,128]{1,0:T(8,128)(2,1)S(1)}, bf16[384,128]{1,0:T(8,128)(2,1)S(1)}, u32[]{:S(2)}, u32[]{:S(2)}) collective-permute-start(bf16[384,128]{1,0:T(8,128)(2,1)S(1)} %get-tuple-element.49.own_ref.refs_0_), channel_id=1, source_target_pairs={{0,2},{1,3},{2,0},{3,1},{4,6},{5,7},{6,4},{7,5},{8,10},{9,11},{10,... | collective-permute-start | bytes 294920 | tf_op jit(solution)/shard_map/ppermute | solution.py:612
  28.6 4.6 %collective-permute-start.2 = (bf16[384,128]{1,0:T(8,128)(2,1)S(1)}, bf16[384,128]{1,0:T(8,128)(2,1)S(1)}, u32[]{:S(2)}, u32[]{:S(2)}) collective-permute-start(bf16[384,128]{1,0:T(8,128)(2,1)S(1)} %get-tuple-element.49.own_ref.refs_0_), channel_id=1, source_target_pairs={{0,1},{1,0},{2,3},{3,2},{4,5},{5,4},{6,7},{7,6},{8,9},{9,8},{10,11... | collective-permute-start | bytes 294920 | tf_op jit(solution)/shard_map/ppermute | solution.py:612
  28.6 4.6 %copy-start.2 = (bf16[128,128]{1,0:T(8,128)(2,1)S(1)}, bf16[128,128]{1,0:T(8,128)(2,1)}, u32[]{:S(2)}) copy-start(bf16[128,128]{1,0:T(8,128)(2,1)} %w2_ref.1) | copy-start | bytes 98308
  28.6 4.6 %copy-start.4 = (f32[128]{0:T(128)S(1)}, f32[128]{0:T(128)}, u32[]{:S(2)}) copy-start(f32[128]{0:T(128)} %param.35) | copy-start | bytes 1540
